TPU v7x, 128 devices: a whole 4x4x4 slice. The times are simulated.
128 devices in a mesh: blocks: 32 (over y, z, core), wide: 4 (over x).
Axes of the slice: x: 4, y: 4, z: 4, core: 2. Of those that a mesh axis runs over, the one named last changes fastest.
Arguments:
- thermal_anomaly: float32 [480, 61440], P('wide', 'blocks'), may hold values from -6 to 6
- saltiness_anomaly: float32 [480, 61440], P('wide', 'blocks'), may hold values from -6 to 6
- zonal_current_layers: float32 [480, 61440], P('wide', 'blocks'), may hold values from -6 to 6
- meridional_current_layers: float32 [480, 61440], P('wide', 'blocks'), may hold values from -6 to 6
- sea_elevation: float32 [480, 7680], P('wide', 'blocks'), may hold values from -6 to 6
- zonal_current_average: float32 [480, 7680], P('wide', 'blocks'), may hold values from -3 to 3
- meridional_current_average: float32 [480, 7680], P('wide', 'blocks'), may hold values from -3 to 3
- water_tile_flags: int32 [8, 128], P('wide', 'blocks'), may hold values 0 or 1
- diffusivity_selector: int32 [480, 7680], P('wide', 'blocks'), may hold values from 0 to 7
- second_order_diffusivity: float32 [8], replicated, may hold values from 0.03 to 0.12
- fourth_order_diffusivity: float32 [8], replicated, may hold values from 0.004 to 0.016
Outputs:
- temperature_next: float32 [480, 61440], P('wide', 'blocks')
- salinity_next: float32 [480, 61440], P('wide', 'blocks')
- zonal_next: float32 [480, 61440], P('wide', 'blocks')
- meridional_next: float32 [480, 61440], P('wide', 'blocks')
- height_next: float32 [480, 7680], P('wide', 'blocks')
- zonal_transport_next: float32 [480, 7680], P('wide', 'blocks')
- meridional_transport_next: float32 [480, 7680], P('wide', 'blocks')
All inputs are finite; a program needn't handle non-finite values. No bound on the sum of `water_tile_flags` on one device may be relied on, other than what follows from the above.
Results may differ from a plain program's by a relative error of at most 0.00002.
Values sent between devices are 32-bit elements; how exact they have to be, the bound alone decides.
A program may use at most 128 MiB of HBM per device.

v0:
```python
import functools

import jax
import jax.numpy as jnp
from jax import lax
from jax.experimental import pallas as pl
from jax.experimental.pallas import tpu as pltpu
from jax.sharding import PartitionSpec as P

BLOCK = 60
LEVELS = 8
NSUB = 4
ROWS = 120
COLS = 240
LANES = COLS * LEVELS
TILES = LANES // 128
RING = TILES + 1
PAD = 16
BAND = ROWS + 2 * PAD
MESH = pl.DeviceIdType.MESH
VMEM_BYTES = 56 * 1024 * 1024


def lanes_of(shape=(8, 128)):
    return lax.broadcasted_iota(jnp.int32, shape, 1)


def rows_of(shape=(8, 128)):
    return lax.broadcasted_iota(jnp.int32, shape, 0)


def lane_xor(tile, bit):
    keep = (lanes_of(tile.shape) // bit) % 2 == 0
    return jnp.where(keep, pltpu.roll(tile, 128 - bit, 1), pltpu.roll(tile, bit, 1))


def row_xor(tile, bit):
    keep = (rows_of(tile.shape) // bit) % 2 == 0
    return jnp.where(keep, pltpu.roll(tile, 8 - bit, 0), pltpu.roll(tile, bit, 0))


def turn_lanes(tile, bits):
    for bit in bits:
        tile = lane_xor(tile, bit)
    return tile


def turn_rows(tile):
    for bit in (1, 2, 4):
        tile = row_xor(tile, bit)
    return tile


class Neighbours:
    def __init__(self, nb, nw, send, recv):
        self.send, self.recv = send, recv
        b, x = lax.axis_index("blocks"), lax.axis_index("wide")
        self.b, self.x = b, x
        self.top, self.inner, self.above = x == nw - 1, x < nw - 1, x > 0
        self.east, self.west = lax.rem(b + 1, nb), lax.rem(b + nb - 1, nb)
        self.fold = nb - 1 - b
        self.fold_east = lax.rem(2 * nb - 2 - b, nb)
        self.fold_west = lax.rem(nb - b, nb)
        self.own_east = jnp.logical_and(self.top, self.fold_east == b)
        self.own_west = jnp.logical_and(self.top, self.fold_west == b)
        self.far_east = jnp.logical_and(self.top, self.fold_east != b)
        self.far_west = jnp.logical_and(self.top, self.fold_west != b)

    def barrier(self):
        sem = pltpu.get_barrier_semaphore()

        def greet(b, x):
            pl.semaphore_signal(sem, inc=1, device_id=(b, x), device_id_type=MESH)

        b, x = self.b, self.x
        greet(self.east, x)
        greet(self.west, x)

        @pl.when(self.inner)
        def _():
            greet(b, x + 1)
            greet(self.east, x + 1)
            greet(self.west, x + 1)

        @pl.when(self.top)
        def _():
            greet(self.fold, x)

        @pl.when(self.far_east)
        def _():
            greet(self.fold_east, x)

        @pl.when(self.far_west)
        def _():
            greet(self.fold_west, x)

        @pl.when(self.above)
        def _():
            greet(b, x - 1)
            greet(self.east, x - 1)
            greet(self.west, x - 1)

        own = jnp.logical_or(self.own_east, self.own_west)

        @pl.when(x == 0)
        def _():
            pl.semaphore_wait(sem, 5)

        @pl.when(own)
        def _():
            pl.semaphore_wait(sem, 7)

        @pl.when(jnp.logical_and(self.above, jnp.logical_not(own)))
        def _():
            pl.semaphore_wait(sem, 8)

    def copy(self, src, dst, way, slot, b, x):
        return pltpu.make_async_remote_copy(
            src_ref=src,
            dst_ref=dst,
            send_sem=self.send.at[way],
            recv_sem=self.recv.at[slot],
            device_id=(b, x),
            device_id_type=MESH,
        )

    def wire(self, north, south, east, west, rn, rs, rw, re):
        b, x = self.b, self.x
        top_rows, low_rows = pl.ds(ROWS - 8, 8), pl.ds(0, 8)
        mid, lo, hi = pl.ds(8, ROWS), pl.ds(0, 8), pl.ds(ROWS + 8, 8)
        c = self.copy
        return dict(
            always=[
                c(east, rw.at[mid], 0, 0, self.east, x),
                c(west, re.at[mid], 1, 1, self.west, x),
            ],
            inner=[
                c(north, rs, 2, 2, b, x + 1),
                c(east.at[top_rows], rw.at[lo], 4, 4, self.east, x + 1),
                c(west.at[top_rows], re.at[lo], 5, 5, self.west, x + 1),
            ],
            above=[
                c(south, rn, 3, 3, b, x - 1),
                c(east.at[low_rows], rw.at[hi], 6, 6, self.east, x - 1),
                c(west.at[low_rows], re.at[hi], 7, 7, self.west, x - 1),
            ],
            top=[c(north, rn, 2, 3, self.fold, x)],
            far_east=[c(east.at[top_rows], re.at[hi], 4, 7, self.fold_east, x)],
            far_west=[c(west.at[top_rows], rw.at[hi], 5, 6, self.fold_west, x)],
        )

    def start(self, wires, north, south, east, west, rn, rs, rw, re):
        def go(name, cond):
            @pl.when(cond)
            def _():
                for copy in wires[name]:
                    copy.start()

        go("inner", self.inner)
        go("top", self.top)
        go("above", self.above)
        go("far_east", self.far_east)
        go("far_west", self.far_west)
        for copy in wires["always"]:
            copy.start()

        @pl.when(self.own_east)
        def _():
            re[pl.ds(ROWS + 8, 8), :] = east[pl.ds(ROWS - 8, 8), :]

        @pl.when(self.own_west)
        def _():
            rw[pl.ds(ROWS + 8, 8), :] = west[pl.ds(ROWS - 8, 8), :]

    def finish(self, wires):
        w = wires
        for copy in w["always"]:
            copy.wait_recv()
            copy.wait_send()
        w["top"][0].wait_recv()

        @pl.when(self.above)
        def _():
            for copy in w["inner"]:
                copy.wait_recv()
            for copy in w["above"]:
                copy.wait_send()

        @pl.when(jnp.logical_not(self.own_east))
        def _():
            w["far_east"][0].wait_recv()
            w["far_east"][0].wait_send()

        @pl.when(jnp.logical_not(self.own_west))
        def _():
            w["far_west"][0].wait_recv()
            w["far_west"][0].wait_send()

        w["top"][0].wait_send()


def block_row(flags, row, tile):
    low, high = (128 * tile) // (BLOCK * LEVELS), (128 * tile + 127) // (BLOCK * LEVELS)
    value = jnp.full((8, 128), flags[row, low].astype(jnp.float32))
    if low != high:
        value = jnp.where(
            lanes_of() < BLOCK * LEVELS * high - 128 * tile,
            value,
            flags[row, high].astype(jnp.float32),
        )
    return value


def exchange_state_kernel(
    nb, nw, flags, t, s, u, v, hn, hs, hw, he,
    edge_rows, edge_cols, npack, spack, wpack, epack, rn, rs, rw, re, load, send, recv,
):
    fields = (t, s, u, v)
    loads = []
    for f, field in enumerate(fields):
        for side, at in enumerate((0, ROWS - 8)):
            loads.append(pltpu.make_async_copy(
                field.at[pl.ds(at, 8), :], edge_rows.at[f, side], load.at[4 * f + side]))
        for side, at in enumerate((0, LANES - 128)):
            loads.append(pltpu.make_async_copy(
                field.at[:, pl.ds(at, 128)], edge_cols.at[f, side], load.at[4 * f + 2 + side]))
    for copy in loads:
        copy.start()
    near = Neighbours(nb, nw, send, recv)
    near.barrier()
    for copy in loads:
        copy.wait()

    lane = lanes_of()
    for k in range(TILES):
        at = pl.ds(128 * k, 128)
        low, high = block_row(flags, 0, k), block_row(flags, 1, k)
        for f in range(4):
            spack[pl.ds(2 * f, 2), at] = (edge_rows[f, 0, :, at] * low)[0:2]
            npack[pl.ds(2 * f, 2), at] = (edge_rows[f, 1, :, at] * high)[6:8]
    for row, pack in ((0, spack), (1, npack)):
        tail = jnp.zeros((8, 128), jnp.float32)
        for j in range(4):
            tail = jnp.where(lane // 32 == j, flags[row, j].astype(jnp.float32), tail)
        pack[:, pl.ds(LANES, 128)] = tail
    lane_c, row_c = lanes_of((ROWS, 128)), rows_of((ROWS, 128))
    for side, col, pack in ((0, 0, wpack), (1, 3, epack)):
        w = jnp.where(row_c < BLOCK, flags[0, col].astype(jnp.float32), flags[1, col].astype(jnp.float32))
        out = w
        for f in range(4):
            shift = (16 * f + (16 if side else 0)) % 128
            moved = pltpu.roll(edge_cols[f, side], shift, 1) if shift else edge_cols[f, side]
            out = jnp.where(lane_c // 16 == f, moved * w, out)
        pack[...] = out

    wires = near.wire(npack, spack, epack, wpack, rn, rs, rw, re)
    near.start(wires, npack, spack, epack, wpack, rn, rs, rw, re)
    near.finish(wires)

    hs[...] = rs[...]
    hw[...] = rw[...]
    he[...] = re[...]

    @pl.when(near.x == 0)
    def _():
        hs[...] = jnp.zeros(hs.shape, jnp.float32)
        hw[0:8, :] = jnp.zeros((8, 128), jnp.float32)
        he[0:8, :] = jnp.zeros((8, 128), jnp.float32)

    @pl.when(near.inner)
    def _():
        hn[...] = rn[...]

    @pl.when(near.top)
    def _():
        sign = jnp.where(rows_of() < 4, 1.0, -1.0)
        for k in range(TILES):
            tile = turn_lanes(rn[:, pl.ds(128 * (TILES - 1 - k), 128)], (8, 16, 32, 64))
            hn[:, pl.ds(128 * k, 128)] = sign * row_xor(tile, 1)
        hn[:, pl.ds(LANES, 128)] = turn_lanes(rn[:, pl.ds(LANES, 128)], (32, 64))
        flow = jnp.where(lanes_of() // 32 == 1, -1.0, 1.0)
        for got, out in ((rw, hw), (re, he)):
            out[pl.ds(ROWS + 8, 8), :] = flow * turn_rows(lane_xor(got[pl.ds(ROWS + 8, 8), :], 8))


def expand(tile, part):
    index = lanes_of() // LEVELS + 16 * part
    return jnp.take_along_axis(tile, index, axis=1, mode="promise_in_bounds")


def baroclinic_kernel(
    flags, ktab, btab, sel, hn, hs, hw, he, t, s, u, v,
    tn, sn, un, vn, um, vm,
    field, once, part, wet, mix, fade, out, load, store,
):
    loads = [
        [
            pltpu.make_async_copy(
                src.at[:, pl.ds(128 * k, 128)], field.at[f, k, pl.ds(PAD, ROWS), :], load.at[f, k])
            for k in range(TILES)
        ]
        for f, src in enumerate((t, s, u, v))
    ]
    for some in loads:
        for copy in some:
            copy.start()
    lane, sub = lanes_of(), rows_of()

    low_tiles = [block_row(flags, 0, k) for k in range(TILES)]
    high_tiles = [block_row(flags, 1, k) for k in range(TILES)]
    for k in range(TILES):
        def fill(e, carry, k=k):
            base = pl.multiple_of(8 * e, 8)
            wet[k, pl.ds(base, 8), :] = jnp.where(sub + base < PAD + BLOCK, low_tiles[k], high_tiles[k])
            return carry
        lax.fori_loop(2, 2 + TILES, fill, 0)
        low, high = (128 * k) // (BLOCK * LEVELS), (128 * k + 127) // (BLOCK * LEVELS)
        for got, base in ((hs, PAD - 8), (hn, PAD + ROWS)):
            tail = got[:, pl.ds(LANES, 128)]
            value = jnp.broadcast_to(tail[:, 32 * low:32 * low + 1], (8, 128))
            if low != high:
                value = jnp.where(lane < BLOCK * LEVELS * high - 128 * k, value,
                                  jnp.broadcast_to(tail[:, 32 * high:32 * high + 1], (8, 128)))
            wet[k, pl.ds(base, 8), :] = value
    lane_h = lanes_of((ROWS + 16, 128))
    ends = pl.ds(PAD - 8, ROWS + 16)
    west, east = hw[...], he[...]
    wet[TILES, ends, :] = jnp.where(lane_h < 64, pltpu.roll(east, 64, 1), west)
    for f in range(4):
        right = pltpu.roll(east, (128 - 16 * f) % 128, 1) if f else east
        field[f, TILES, ends, :] = jnp.where(lane_h < 64, right, pltpu.roll(west, 112 - 16 * f, 1))
        for k in range(TILES):
            field[f, k, PAD - 2:PAD, :] = hs[2 * f:2 * f + 2, 128 * k:128 * k + 128]
            field[f, k, PAD + ROWS:PAD + ROWS + 2, :] = hn[2 * f:2 * f + 2, 128 * k:128 * k + 128]

    for half, width in ((0, 128), (1, COLS - 128)):
        index = sel[:, 128 * half:128 * half + width]
        kappa = jnp.full(index.shape, ktab[0])
        bihar = jnp.full(index.shape, btab[0])
        for n in range(1, 8):
            kappa = jnp.where(index == n, ktab[n], kappa)
            bihar = jnp.where(index == n, btab[n], bihar)
        mix[0, half, PAD:PAD + ROWS, 0:width] = kappa
        mix[1, half, PAD:PAD + ROWS, 0:width] = bihar

    for some in loads:
        for copy in some:
            copy.wait()

    def mask(e, carry):
        rows = pl.ds(pl.multiple_of(8 * e, 8), 8)
        for k in range(TILES):
            w = wet[k, rows, :]
            for f in range(4):
                field[f, k, rows, :] = field[f, k, rows, :] * w
        return carry

    lax.fori_loop(2, 2 + TILES, mask, 0)

    def first(e, carry):
        base = pl.multiple_of(8 * e, 8)
        here, above, below = pl.ds(base, 8), pl.ds(base + 1, 8), pl.ds(base - 1, 8)
        turned = {}

        def ring(ref, key, k):
            if (key, k) not in turned:
                tile = ref[k, here, :]
                turned[key, k] = (tile, pltpu.roll(tile, 128 - LEVELS, 1), pltpu.roll(tile, LEVELS, 1))
            return turned[key, k]

        def around(ref, key, k):
            tile, left, right = ring(ref, key, k)
            east = jnp.where(lane < 128 - LEVELS, left, ring(ref, key, (k + 1) % RING)[1])
            west = jnp.where(lane < LEVELS, ring(ref, key, (k - 1) % RING)[2], right)
            return tile, east, west, ref[k, above, :], ref[k, below, :]

        for k in range(RING):
            w, we, ww, wn, ws = around(wet, "wet", k)
            count = w * ((we + ww) + (wn + ws))
            if k < TILES:
                kappa = expand(mix[0, k // 8, here, :], k % 8)
                bihar = expand(mix[1, k // 8, here, :], k % 8)
                both = kappa + bihar * count
                fade[k, here, :] = bihar * w
                zonal = 0.05 * ring(field.at[2], 2, k)[0]
                merid = 0.05 * ring(field.at[3], 3, k)[0]
            for f in range(4):
                c, fe, fw, fn, fs = around(field.at[f], f, k)
                lap = w * ((fe + fw) + (fn + fs)) - count * c
                once[f, k, here, :] = lap
                if k < TILES:
                    part[f, k, here, :] = (c - (zonal * (fe - fw) + merid * (fn - fs))) + both * lap
        return carry

    lax.fori_loop(1, 3 + TILES, first, 0)

    def second(e, carry):
        base = pl.multiple_of(8 * e, 8)
        here, above, below = pl.ds(base, 8), pl.ds(base + 1, 8), pl.ds(base - 1, 8)
        rows = pl.ds(pl.multiple_of(base - PAD, 8), 8)
        turned = {}

        def ring(f, k):
            if (f, k) not in turned:
                tile = once[f, k, here, :]
                turned[f, k] = (pltpu.roll(tile, 128 - LEVELS, 1), pltpu.roll(tile, LEVELS, 1))
            return turned[f, k]

        for f in range(4):
            for k in range(TILES):
                left, right = ring(f, k)
                east = jnp.where(lane < 128 - LEVELS, left, ring(f, (k + 1) % RING)[0])
                west = jnp.where(lane < LEVELS, ring(f, (k - 1) % RING)[1], right)
                total = (east + west) + (once[f, k, above, :] + once[f, k, below, :])
                out[f, rows, 128 * k:128 * k + 128] = part[f, k, here, :] - fade[k, here, :] * total
        for f, ref in enumerate((tn, sn, un, vn)):
            pltpu.make_async_copy(out.at[f, rows, :], ref.at[rows, :], store.at[f]).start()
        return carry

    lax.fori_loop(2, 2 + TILES, second, 0)

    span = 128 * LEVELS
    pick = jnp.where(
        lax.broadcasted_iota(jnp.int32, (span, 128), 0) // LEVELS
        == lax.broadcasted_iota(jnp.int32, (span, 128), 1),
        1.0 / LEVELS, 0.0).astype(jnp.bfloat16)
    for f, mean in ((2, um), (3, vm)):
        for half in range(2):
            width = span if half == 0 else LANES - span
            rest = out[f, :, span * half:span * half + width]
            total = None
            for _ in range(3):
                piece = rest.astype(jnp.bfloat16)
                rest = rest - piece.astype(jnp.float32)
                term = jnp.dot(piece, pick[:width], preferred_element_type=jnp.float32)
                total = term if total is None else total + term
            mean[:, 128 * half:128 * half + 128] = total

    for f, ref in enumerate((tn, sn, un, vn)):
        pltpu.make_async_copy(out.at[f], ref, store.at[f]).wait()


def substeps_kernel(
    nb, nw, flags, um, vm, zavg, mavg, elev, height, zonal, merid,
    plane, wpack, epack, rn, rs, rw, re, send, recv,
):
    near = Neighbours(nb, nw, send, recv)
    near.barrier()
    shape = (ROWS, COLS)
    row, col = rows_of(shape), lanes_of(shape)
    w = jnp.zeros(shape, jnp.float32)
    for i in range(2):
        for j in range(4):
            here = jnp.logical_and(row // BLOCK == i, col // BLOCK == j)
            w = jnp.where(here, flags[i, j].astype(jnp.float32), w)
    plane[:, :, 128:256] = jnp.zeros((4, ROWS + 16, 128), jnp.float32)
    plane[0, 0:ROWS, 0:COLS] = w * (zavg[...] + um[:, 0:COLS])
    plane[1, 0:ROWS, 0:COLS] = w * (mavg[...] + vm[:, 0:COLS])
    plane[2, 0:ROWS, 0:COLS] = w * elev[...]
    plane[3, 0:ROWS, 0:COLS] = w
    lane = lanes_of((ROWS, 128))
    right = jnp.zeros((ROWS, 128), jnp.float32)
    left = jnp.zeros((ROWS, 128), jnp.float32)
    for p in range(4):
        right = jnp.where(lane // 8 == p, pltpu.roll(plane[p, 0:ROWS, 128:256], 8 * p + 24, 1), right)
        first = plane[p, 0:ROWS, 0:128]
        left = jnp.where(lane // 8 == p, pltpu.roll(first, 8 * p, 1) if p else first, left)
    epack[...] = right
    wpack[...] = left

    north, south = plane.at[:, pl.ds(ROWS - 8, 8), :], plane.at[:, pl.ds(0, 8), :]
    wires = near.wire(north, south, epack, wpack, rn, rs, rw, re)
    near.start(wires, north, south, epack, wpack, rn, rs, rw, re)
    near.finish(wires)

    @pl.when(near.x == 0)
    def _():
        rs[...] = jnp.zeros(rs.shape, jnp.float32)
        rw[0:8, :] = jnp.zeros((8, 128), jnp.float32)
        re[0:8, :] = jnp.zeros((8, 128), jnp.float32)

    @pl.when(near.top)
    def _():
        reverse = (1, 2, 4, 8, 16, 32, 64)
        for p in range(4):
            sign = -1.0 if p < 2 else 1.0
            first = sign * turn_rows(turn_lanes(rn[p, :, 128:256], reverse))
            last = sign * turn_rows(turn_lanes(rn[p, :, 0:128], reverse))
            rn[p] = pltpu.roll(jnp.concatenate([first, last], axis=1), COLS, 1)
        flow = jnp.where(lanes_of() < 16, -1.0, 1.0)
        for got in (rw, re):
            tile = got[pl.ds(ROWS + 8, 8), :]
            got[pl.ds(ROWS + 8, 8), :] = flow * turn_rows(turn_lanes(tile, (1, 2, 4)))

    plane[:, ROWS:ROWS + 8, :] = rn[...]
    plane[:, ROWS + 8:ROWS + 16, :] = rs[...]
    spans = ((0, 8, ROWS), (ROWS, ROWS + 8, 8), (ROWS + 8, 0, 8))
    for to, at, count in spans:
        lane = lanes_of((count, 128))
        west, east = rw[at:at + count, :], re[at:at + count, :]
        for p in range(4):
            halo = jnp.where(lane < 120, pltpu.roll(east, 112 - 8 * p, 1), pltpu.roll(west, 120 - 8 * p, 1))
            plane[p, to:to + count, 128:256] = jnp.where(lane < 112, plane[p, to:to + count, 128:256], halo)

    zt, mt, h, w = plane[0], plane[1], plane[2], plane[3]
    across, along = 256, ROWS + 16
    for _ in range(NSUB):
        spread = (pltpu.roll(zt, across - 1, 1) - pltpu.roll(zt, 1, 1)) + (
            pltpu.roll(mt, along - 1, 0) - pltpu.roll(mt, 1, 0))
        h = h - 0.3 * w * spread
        zt = w * (zt - 0.3 * (pltpu.roll(h, across - 1, 1) - pltpu.roll(h, 1, 1)))
        mt = w * (mt - 0.3 * (pltpu.roll(h, along - 1, 0) - pltpu.roll(h, 1, 0)))
    height[...] = h[0:ROWS]
    zonal[...] = zt[0:ROWS]
    merid[...] = mt[0:ROWS]


def finish_kernel(un, vn, um, vm, zt, mt, h, zonal, merid, height, zonal_t, merid_t):
    for new, mean, after, to in ((un, um, zt, zonal), (vn, vm, mt, merid)):
        count = new.shape[0]
        for r in range(0, count, 8):
            for half in range(2):
                at = slice(128 * half, 128 * half + 128)
                change = after[r:r + 8, at] - mean[r:r + 8, at]
                for k in range(8 * half, min(8 * half + 8, TILES)):
                    to[r:r + 8, 128 * k:128 * k + 128] = (
                        new[r:r + 8, 128 * k:128 * k + 128] + expand(change, k % 8))
    height[...] = h[:, 0:COLS]
    zonal_t[...] = zt[:, 0:COLS]
    merid_t[...] = mt[:, 0:COLS]


def per_device(nb, nw, t, s, u, v, elev, zavg, mavg, flags, sel, ktab, btab):
    f32 = jnp.float32
    vmem = pl.BlockSpec(memory_space=pltpu.VMEM)
    smem = pl.BlockSpec(memory_space=pltpu.SMEM)
    hbm = pl.BlockSpec(memory_space=pl.ANY)
    side = jax.ShapeDtypeStruct((ROWS + 16, 128), f32)
    cap = jax.ShapeDtypeStruct((8, LANES + 128), f32)
    hn, hs, hw, he = pl.pallas_call(
        functools.partial(exchange_state_kernel, nb, nw),
        out_shape=(cap, cap, side, side),
        in_specs=[smem] + [hbm] * 4,
        out_specs=(vmem,) * 4,
        scratch_shapes=[
            pltpu.VMEM((4, 2, 8, LANES), f32),
            pltpu.VMEM((4, 2, ROWS, 128), f32),
            pltpu.VMEM((8, LANES + 128), f32),
            pltpu.VMEM((8, LANES + 128), f32),
            pltpu.VMEM((ROWS, 128), f32),
            pltpu.VMEM((ROWS, 128), f32),
            pltpu.VMEM((8, LANES + 128), f32),
            pltpu.VMEM((8, LANES + 128), f32),
            pltpu.VMEM((ROWS + 16, 128), f32),
            pltpu.VMEM((ROWS + 16, 128), f32),
            pltpu.SemaphoreType.DMA((16,)),
            pltpu.SemaphoreType.DMA((8,)),
            pltpu.SemaphoreType.DMA((8,)),
        ],
        compiler_params=pltpu.CompilerParams(
            collective_id=0, has_side_effects=True, vmem_limit_bytes=VMEM_BYTES),
        name="exchange_state",
    )(flags, t, s, u, v)

    big = jax.ShapeDtypeStruct((ROWS, LANES), f32)
    plane = jax.ShapeDtypeStruct((ROWS, 256), f32)
    tn, sn, un, vn, um, vm = pl.pallas_call(
        baroclinic_kernel,
        out_shape=(big,) * 4 + (plane,) * 2,
        in_specs=[smem] * 3 + [vmem] * 5 + [hbm] * 4,
        out_specs=(hbm,) * 4 + (vmem,) * 2,
        scratch_shapes=[
            pltpu.VMEM((4, RING, BAND, 128), f32),
            pltpu.VMEM((4, RING, BAND, 128), f32),
            pltpu.VMEM((4, TILES, BAND, 128), f32),
            pltpu.VMEM((RING, BAND, 128), f32),
            pltpu.VMEM((2, 2, BAND, 128), f32),
            pltpu.VMEM((TILES, BAND, 128), f32),
            pltpu.VMEM((4, ROWS, LANES), f32),
            pltpu.SemaphoreType.DMA((4, TILES)),
            pltpu.SemaphoreType.DMA((4,)),
        ],
        compiler_params=pltpu.CompilerParams(vmem_limit_bytes=VMEM_BYTES),
        name="baroclinic",
    )(flags, ktab, btab, sel, hn, hs, hw, he, t, s, u, v)

    height, zt, mt = pl.pallas_call(
        functools.partial(substeps_kernel, nb, nw),
        out_shape=(plane,) * 3,
        in_specs=[smem] + [vmem] * 5,
        out_specs=(vmem,) * 3,
        scratch_shapes=[
            pltpu.VMEM((4, ROWS + 16, 256), f32),
            pltpu.VMEM((ROWS, 128), f32),
            pltpu.VMEM((ROWS, 128), f32),
            pltpu.VMEM((4, 8, 256), f32),
            pltpu.VMEM((4, 8, 256), f32),
            pltpu.VMEM((ROWS + 16, 128), f32),
            pltpu.VMEM((ROWS + 16, 128), f32),
            pltpu.SemaphoreType.DMA((8,)),
            pltpu.SemaphoreType.DMA((8,)),
        ],
        compiler_params=pltpu.CompilerParams(
            collective_id=1, has_side_effects=True, vmem_limit_bytes=VMEM_BYTES),
        name="substeps",
    )(flags, um, vm, zavg, mavg, elev)

    step = 24
    wide = pl.BlockSpec((step, LANES), lambda i: (i, 0))
    flat = pl.BlockSpec((step, 256), lambda i: (i, 0))
    last = pl.BlockSpec((step, COLS), lambda i: (i, 0))
    small = jax.ShapeDtypeStruct((ROWS, COLS), f32)
    zonal, merid, height, zt, mt = pl.pallas_call(
        finish_kernel,
        grid=(ROWS // step,),
        out_shape=(big, big, small, small, small),
        in_specs=[wide, wide] + [flat] * 5,
        out_specs=(wide, wide, last, last, last),
        compiler_params=pltpu.CompilerParams(vmem_limit_bytes=VMEM_BYTES),
        name="finish",
    )(un, vn, um, vm, zt, mt, height)
    return tn, sn, zonal, merid, height, zt, mt


def solution(mesh):
    grid = P("wide", "blocks")
    return jax.shard_map(
        functools.partial(per_device, mesh.shape["blocks"], mesh.shape["wide"]),
        mesh=mesh,
        in_specs=(grid,) * 9 + (P(), P()),
        out_specs=(grid,) * 7,
        check_vma=False,
    )
```

profile of v0, /device:TPU:7, one launch (start us, length us, event | category | flops | bytes accessed | tf_op | source)
XLA Modules:
  0.0 45.9 jit_solution(3216953489660982815)
XLA Ops:
  0.6 13.1 %exchange_state.1 = (f32[8,2048]{1,0:T(8,128)}, f32[8,2048]{1,0:T(8,128)}, f32[136,128]{1,0:T(8,128)}, f32[136,128]{1,0:T(8,128)}) custom-call(s32[2,4]{1,0:T(2,128)} %flags.5, f32[120,1920]{1,0:T(8,128)} %t.3, f32[120,1920]{1,0:T(8,128)} %s.3, f32[120,1920]{1,0:T(8,128)} %u.3, f32[120,1920]{1,0:T(8,128)} %v.3), custom_call_target="tpu_custom_call" | custom-call | tf_op jit(solution)/shard_map/exchange_state/pallas_call | solution.py:540
  13.7 14.9 %baroclinic.1 = (f32[120,1920]{1,0:T(8,128)}, f32[120,1920]{1,0:T(8,128)}, f32[120,1920]{1,0:T(8,128)}, f32[120,1920]{1,0:T(8,128)}, f32[120,256]{1,0:T(8,128)}, /*index=5*/f32[120,256]{1,0:T(8,128)}) custom-call(s32[2,4]{1,0:T(2,128)} %flags.5, f32[8]{0:T(128)} %ktab.1, f32[8]{0:T(128)} %btab.1, s32[120,240]{1,0:T(8,128)} %sel.1, ...), custom_call_target="tpu_custom_call" | custom-call | tf_op jit(solution)/shard_map/baroclinic/pallas_call | solution.py:567
  28.6 12.2 %substeps.1 = (f32[120,256]{1,0:T(8,128)}, f32[120,256]{1,0:T(8,128)}, f32[120,256]{1,0:T(8,128)}) custom-call(s32[2,4]{1,0:T(2,128)} %flags.5, f32[120,256]{1,0:T(8,128)} %get-tuple-element.33.um, f32[120,256]{1,0:T(8,128)} %get-tuple-element.34.vm, f32[120,240]{1,0:T(8,128)} %zavg.1, f32[120,240]{1,0:T(8,128)} %mavg.1, f32[120,240]{1,0:T(8,128)} %elev.1), custom_call_target="tpu_custom_call" | custom-call | tf_op jit(solution)/shard_map/substeps/pallas_call | solution.py:587
  40.8 5.1 %finish.1 = (f32[120,1920]{1,0:T(8,128)}, f32[120,1920]{1,0:T(8,128)}, f32[120,240]{1,0:T(8,128)}, f32[120,240]{1,0:T(8,128)}, f32[120,240]{1,0:T(8,128)}) custom-call(f32[120,1920]{1,0:T(8,128)} %get-tuple-element.31.un, f32[120,1920]{1,0:T(8,128)} %get-tuple-element.32.vn, f32[120,256]{1,0:T(8,128)} %get-tuple-element.33.um, ...), custom_call_target="tpu_custom_call" | custom-call | tf_op jit(solution)/shard_map/finish/pallas_call | solution.py:613
where the time goes:
time: 46.7 us; the launch traced here: 45.9 us
  Pallas kernels  45.3 us (97%)
  between operations  0.66 us (1%)
    pallas_call x1, Pallas kernels, per_device(): pl.pallas_call(baroclinic_kernel, out_shape=(big,) * 4 + (plane,) * 2, in...  14.9 us
    pallas_call x1, Pallas kernels, per_device(): pl.pallas_call(functools.partial(exchange_state_kernel, nb, nw), out_shap...  13.1 us
    pallas_call x1, Pallas kernels, per_device(): pl.pallas_call(functools.partial(substeps_kernel, nb, nw), out_shape=(pla...  12.2 us
    pallas_call x1, Pallas kernels, per_device(): pl.pallas_call(finish_kernel, grid=(ROWS // step,), out_shape=(big, big,...  5.14 us

commit v1 on v0

v1 whole, which is shorter than its diff:
```python
import functools

import jax
import jax.numpy as jnp
from jax import lax
from jax.experimental import pallas as pl
from jax.experimental.pallas import tpu as pltpu
from jax.sharding import PartitionSpec as P

BLOCK = 60
LEVELS = 8
NSUB = 4
ROWS = 120
COLS = 240
LANES = COLS * LEVELS
TILES = LANES // 128
RING = TILES + 1
PAD = 16
BAND = ROWS + 2 * PAD
MESH = pl.DeviceIdType.MESH
VMEM_BYTES = 56 * 1024 * 1024


def lanes_of(shape=(8, 128)):
    return lax.broadcasted_iota(jnp.int32, shape, 1)


def rows_of(shape=(8, 128)):
    return lax.broadcasted_iota(jnp.int32, shape, 0)


def lane_xor(tile, bit):
    keep = (lanes_of(tile.shape) // bit) % 2 == 0
    return jnp.where(keep, pltpu.roll(tile, 128 - bit, 1), pltpu.roll(tile, bit, 1))


def row_xor(tile, bit):
    keep = (rows_of(tile.shape) // bit) % 2 == 0
    return jnp.where(keep, pltpu.roll(tile, 8 - bit, 0), pltpu.roll(tile, bit, 0))


def turn_lanes(tile, bits):
    for bit in bits:
        tile = lane_xor(tile, bit)
    return tile


def turn_rows(tile):
    for bit in (1, 2, 4):
        tile = row_xor(tile, bit)
    return tile


class Neighbours:
    def __init__(self, nb, nw):
        b, x = lax.axis_index("blocks"), lax.axis_index("wide")
        self.b, self.x = b, x
        self.top, self.inner, self.above = x == nw - 1, x < nw - 1, x > 0
        self.east, self.west = lax.rem(b + 1, nb), lax.rem(b + nb - 1, nb)
        self.fold = nb - 1 - b
        self.fold_east = lax.rem(2 * nb - 2 - b, nb)
        self.fold_west = lax.rem(nb - b, nb)
        self.own_east = jnp.logical_and(self.top, self.fold_east == b)
        self.own_west = jnp.logical_and(self.top, self.fold_west == b)
        self.far_east = jnp.logical_and(self.top, self.fold_east != b)
        self.far_west = jnp.logical_and(self.top, self.fold_west != b)

    def greet(self):
        sem = pltpu.get_barrier_semaphore()

        def greet(b, x):
            pl.semaphore_signal(sem, inc=1, device_id=(b, x), device_id_type=MESH)

        b, x = self.b, self.x
        greet(self.east, x)
        greet(self.west, x)

        @pl.when(self.inner)
        def _():
            greet(b, x + 1)
            greet(self.east, x + 1)
            greet(self.west, x + 1)

        @pl.when(self.top)
        def _():
            greet(self.fold, x)

        @pl.when(self.far_east)
        def _():
            greet(self.fold_east, x)

        @pl.when(self.far_west)
        def _():
            greet(self.fold_west, x)

        @pl.when(self.above)
        def _():
            greet(b, x - 1)
            greet(self.east, x - 1)
            greet(self.west, x - 1)

    def meet(self):
        sem = pltpu.get_barrier_semaphore()
        x = self.x
        own = jnp.logical_or(self.own_east, self.own_west)

        @pl.when(x == 0)
        def _():
            pl.semaphore_wait(sem, 5)

        @pl.when(own)
        def _():
            pl.semaphore_wait(sem, 7)

        @pl.when(jnp.logical_and(self.above, jnp.logical_not(own)))
        def _():
            pl.semaphore_wait(sem, 8)

    def wire(self, north, south, east, west, rn, rs, rw, re, send, recv):
        b, x = self.b, self.x
        top_rows, low_rows = pl.ds(ROWS - 8, 8), pl.ds(0, 8)
        mid, lo, hi = pl.ds(8, ROWS), pl.ds(0, 8), pl.ds(ROWS + 8, 8)

        def c(src, dst, way, slot, to_b, to_x):
            return pltpu.make_async_remote_copy(
                src_ref=src, dst_ref=dst, send_sem=send.at[way], recv_sem=recv.at[slot],
                device_id=(to_b, to_x), device_id_type=MESH)

        return dict(
            always=[
                c(east, rw.at[mid], 0, 0, self.east, x),
                c(west, re.at[mid], 1, 1, self.west, x),
            ],
            inner=[
                c(north, rs, 2, 2, b, x + 1),
                c(east.at[top_rows], rw.at[lo], 4, 4, self.east, x + 1),
                c(west.at[top_rows], re.at[lo], 5, 5, self.west, x + 1),
            ],
            above=[
                c(south, rn, 3, 3, b, x - 1),
                c(east.at[low_rows], rw.at[hi], 6, 6, self.east, x - 1),
                c(west.at[low_rows], re.at[hi], 7, 7, self.west, x - 1),
            ],
            top=[c(north, rn, 2, 3, self.fold, x)],
            far_east=[c(east.at[top_rows], re.at[hi], 4, 7, self.fold_east, x)],
            far_west=[c(west.at[top_rows], rw.at[hi], 5, 6, self.fold_west, x)],
        )

    def start(self, wires, east, west, rw, re):
        def go(name, cond):
            @pl.when(cond)
            def _():
                for copy in wires[name]:
                    copy.start()

        go("inner", self.inner)
        go("top", self.top)
        go("above", self.above)
        go("far_east", self.far_east)
        go("far_west", self.far_west)
        for copy in wires["always"]:
            copy.start()

        @pl.when(self.own_east)
        def _():
            re[pl.ds(ROWS + 8, 8), :] = east[pl.ds(ROWS - 8, 8), :]

        @pl.when(self.own_west)
        def _():
            rw[pl.ds(ROWS + 8, 8), :] = west[pl.ds(ROWS - 8, 8), :]

    def finish(self, wires):
        w = wires
        for copy in w["always"]:
            copy.wait_recv()
            copy.wait_send()
        w["top"][0].wait_recv()

        @pl.when(self.above)
        def _():
            for copy in w["inner"]:
                copy.wait_recv()
            for copy in w["above"]:
                copy.wait_send()

        @pl.when(jnp.logical_not(self.own_east))
        def _():
            w["far_east"][0].wait_recv()
            w["far_east"][0].wait_send()

        @pl.when(jnp.logical_not(self.own_west))
        def _():
            w["far_west"][0].wait_recv()
            w["far_west"][0].wait_send()

        w["top"][0].wait_send()


def block_row(flags, row, tile):
    low, high = (128 * tile) // (BLOCK * LEVELS), (128 * tile + 127) // (BLOCK * LEVELS)
    value = jnp.full((8, 128), flags[row, low].astype(jnp.float32))
    if low != high:
        value = jnp.where(
            lanes_of() < BLOCK * LEVELS * high - 128 * tile,
            value,
            flags[row, high].astype(jnp.float32),
        )
    return value


def expand(tile, part):
    index = lanes_of() // LEVELS + 16 * part
    return jnp.take_along_axis(tile, index, axis=1, mode="promise_in_bounds")


def step_kernel(
    nb, nw, flags_in, ktab_in, btab_in, sel_in, t, s, u, v, zavg_in, mavg_in, elev_in,
    tn, sn, un, vn, du, dv, height, zonal, merid,
    flags, ktab, btab, sel, zavg, mavg, elev,
    edge_rows, edge_cols, npack, spack, wpack, epack, rn, rs, rw, re,
    field, once, part, wet, count, both, fade, mix,
    plane, wpack2, epack2, rn2, rs2, rw2, re2,
    small, load, send, recv, send2, recv2,
):
    sources = (t, s, u, v)
    results = (tn, sn, un, vn)
    near = Neighbours(nb, nw)
    near.greet()

    tables = [
        pltpu.make_async_copy(src, dst, small.at[i])
        for i, (src, dst) in enumerate(
            ((flags_in, flags), (ktab_in, ktab), (btab_in, btab), (sel_in, sel),
             (zavg_in, zavg), (mavg_in, mavg), (elev_in, elev)))
    ]
    edges = []
    for f, src in enumerate(sources):
        for side, at in enumerate((0, ROWS - 8)):
            edges.append(pltpu.make_async_copy(
                src.at[pl.ds(at, 8), :], edge_rows.at[f, side], small.at[8 + 4 * f + side]))
        for side, at in enumerate((0, LANES - 128)):
            edges.append(pltpu.make_async_copy(
                src.at[:, pl.ds(at, 128)], edge_cols.at[f, side], small.at[10 + 4 * f + side]))
    loads = [
        [
            pltpu.make_async_copy(
                src.at[:, pl.ds(128 * k, 128)], field.at[f, k, pl.ds(PAD, ROWS), :], load.at[f, k])
            for k in range(TILES)
        ]
        for f, src in enumerate(sources)
    ]
    tables[0].start()
    for copy in edges:
        copy.start()
    for copy in tables[1:]:
        copy.start()
    for f in (2, 3, 0, 1):
        for copy in loads[f]:
            copy.start()

    lane, sub = lanes_of(), rows_of()
    tables[0].wait()
    for copy in edges:
        copy.wait()
    for k in range(TILES):
        at = pl.ds(128 * k, 128)
        low, high = block_row(flags, 0, k), block_row(flags, 1, k)
        for f in range(4):
            spack[pl.ds(2 * f, 2), at] = (edge_rows[f, 0, :, at] * low)[0:2]
            npack[pl.ds(2 * f, 2), at] = (edge_rows[f, 1, :, at] * high)[6:8]
    for row, pack in ((0, spack), (1, npack)):
        tail = jnp.zeros((8, 128), jnp.float32)
        for j in range(4):
            tail = jnp.where(lane // 32 == j, flags[row, j].astype(jnp.float32), tail)
        pack[:, pl.ds(LANES, 128)] = tail
    lane_c, row_c = lanes_of((ROWS, 128)), rows_of((ROWS, 128))
    for side, col, pack in ((0, 0, wpack), (1, 3, epack)):
        w = jnp.where(row_c < BLOCK, flags[0, col].astype(jnp.float32), flags[1, col].astype(jnp.float32))
        packed = w
        for f in range(4):
            shift = (16 * f + (16 if side else 0)) % 128
            moved = pltpu.roll(edge_cols[f, side], shift, 1) if shift else edge_cols[f, side]
            packed = jnp.where(lane_c // 16 == f, moved * w, packed)
        pack[...] = packed
    near.meet()
    wires = near.wire(npack, spack, epack, wpack, rn, rs, rw, re, send, recv)
    near.start(wires, epack, wpack, rw, re)

    def fill(e, carry):
        base = pl.multiple_of(8 * e, 8)
        lower = sub + base < PAD + BLOCK
        for k in range(TILES):
            wet[k, pl.ds(base, 8), :] = jnp.where(lower, block_row(flags, 0, k), block_row(flags, 1, k))
        return carry

    lax.fori_loop(2, 2 + ROWS // 8, fill, 0)
    for copy in tables[1:]:
        copy.wait()
    for half, width in ((0, 128), (1, COLS - 128)):
        index = sel[:, 128 * half:128 * half + width]
        kappa = jnp.full(index.shape, ktab[0])
        bihar = jnp.full(index.shape, btab[0])
        for n in range(1, 8):
            kappa = jnp.where(index == n, ktab[n], kappa)
            bihar = jnp.where(index == n, btab[n], bihar)
        mix[0, half, PAD:PAD + ROWS, 0:width] = kappa
        mix[1, half, PAD:PAD + ROWS, 0:width] = bihar

    def around(ref, turned, key, k, base):
        here, above, below = pl.ds(base, 8), pl.ds(base + 1, 8), pl.ds(base - 1, 8)

        def ring(k):
            if (key, k) not in turned:
                tile = ref[k, here, :]
                turned[key, k] = (tile, pltpu.roll(tile, 128 - LEVELS, 1), pltpu.roll(tile, LEVELS, 1))
            return turned[key, k]

        tile, left, right = ring(k)
        east = jnp.where(lane < 128 - LEVELS, left, ring((k + 1) % RING)[1])
        west = jnp.where(lane < LEVELS, ring((k - 1) % RING)[2], right)
        return tile, east, west, ref[k, above, :], ref[k, below, :]

    def weigh(e, tiles):
        base = pl.multiple_of(8 * e, 8)
        here = pl.ds(base, 8)
        turned = {}
        for k in tiles:
            w, we, ww, wn, ws = around(wet, turned, "wet", k, base)
            total = w * ((we + ww) + (wn + ws))
            count[k, here, :] = total
            if k < TILES:
                kappa = expand(mix[0, k // 8, here, :], k % 8)
                bihar = expand(mix[1, k // 8, here, :], k % 8)
                both[k, here, :] = kappa + bihar * total
                fade[k, here, :] = bihar * w

    def mask(e, which):
        rows = pl.ds(pl.multiple_of(8 * e, 8), 8)
        for k in range(TILES):
            w = wet[k, rows, :]
            for f in which:
                field[f, k, rows, :] = field[f, k, rows, :] * w

    def first(e, tiles, which):
        base = pl.multiple_of(8 * e, 8)
        here = pl.ds(base, 8)
        turned = {}
        for k in tiles:
            w, total = wet[k, here, :], count[k, here, :]
            if k < TILES:
                mixing = both[k, here, :]
                zonal_own = 0.05 * field[2, k, here, :]
                merid_own = 0.05 * field[3, k, here, :]
            for f in which:
                c, fe, fw, fn, fs = around(field.at[f], turned, f, k, base)
                lap = w * ((fe + fw) + (fn + fs)) - total * c
                once[f, k, here, :] = lap
                if k < TILES:
                    part[f, k, here, :] = (
                        c - (zonal_own * (fe - fw) + merid_own * (fn - fs))) + mixing * lap

    def second(e, tiles, which):
        base = pl.multiple_of(8 * e, 8)
        here = pl.ds(base, 8)
        rows = pl.ds(pl.multiple_of(base - PAD, 8), 8)
        turned = {}
        for k in tiles:
            for f in which:
                _, le, lw, ln, ls = around(once.at[f], turned, f, k, base)
                results[f][rows, 128 * k:128 * k + 128] = (
                    part[f, k, here, :] - fade[k, here, :] * ((le + lw) + (ln + ls)))

    def each(low, high, *steps):
        def body(e, carry):
            for step in steps:
                step(e)
            return carry
        lax.fori_loop(low, high, body, 0)

    end = 2 + ROWS // 8
    flows, tracers = (2, 3), (0, 1)
    inside, everywhere, rim = range(TILES), range(RING), (0, TILES - 1, TILES)

    each(2, end, lambda e: weigh(e, inside))
    for f in flows:
        for copy in loads[f]:
            copy.wait()
    each(2, end, lambda e: mask(e, flows))
    each(2, end, lambda e: first(e, inside, flows))
    each(3, end - 1, lambda e: second(e, range(1, TILES - 1), flows))

    near.finish(wires)

    @pl.when(near.x == 0)
    def _():
        rs[...] = jnp.zeros(rs.shape, jnp.float32)
        rw[0:8, :] = jnp.zeros((8, 128), jnp.float32)
        re[0:8, :] = jnp.zeros((8, 128), jnp.float32)

    @pl.when(near.top)
    def _():
        sign = jnp.where(sub < 4, 1.0, -1.0)
        tiles = [rn[:, pl.ds(128 * (TILES - 1 - k), 128)] for k in range(TILES)]
        for k in range(TILES):
            rn[:, pl.ds(128 * k, 128)] = sign * row_xor(turn_lanes(tiles[k], (8, 16, 32, 64)), 1)
        rn[:, pl.ds(LANES, 128)] = turn_lanes(rn[:, pl.ds(LANES, 128)], (32, 64))
        flow = jnp.where(lane // 32 == 1, -1.0, 1.0)
        for got in (rw, re):
            tile = got[pl.ds(ROWS + 8, 8), :]
            got[pl.ds(ROWS + 8, 8), :] = flow * turn_rows(lane_xor(tile, 8))

    for k in range(TILES):
        low, high = (128 * k) // (BLOCK * LEVELS), (128 * k + 127) // (BLOCK * LEVELS)
        for got, base in ((rs, PAD - 8), (rn, PAD + ROWS)):
            tail = got[:, pl.ds(LANES, 128)]
            value = jnp.broadcast_to(tail[:, 32 * low:32 * low + 1], (8, 128))
            if low != high:
                value = jnp.where(lane < BLOCK * LEVELS * high - 128 * k, value,
                                  jnp.broadcast_to(tail[:, 32 * high:32 * high + 1], (8, 128)))
            wet[k, pl.ds(base, 8), :] = value
    lane_h = lanes_of((ROWS + 16, 128))
    ends = pl.ds(PAD - 8, ROWS + 16)
    west, east = rw[...], re[...]
    wet[TILES, ends, :] = jnp.where(lane_h < 64, pltpu.roll(east, 64, 1), west)
    for f in range(4):
        right = pltpu.roll(east, (128 - 16 * f) % 128, 1) if f else east
        field[f, TILES, ends, :] = jnp.where(lane_h < 64, right, pltpu.roll(west, 112 - 16 * f, 1))
        for k in range(TILES):
            field[f, k, PAD - 2:PAD, :] = rs[2 * f:2 * f + 2, 128 * k:128 * k + 128]
            field[f, k, PAD + ROWS:PAD + ROWS + 2, :] = rn[2 * f:2 * f + 2, 128 * k:128 * k + 128]

    def brink(i):
        return 1 + i + (end - 4) * (i // 2)

    each(0, 4, lambda i: weigh(brink(i), everywhere))
    each(3, end - 1, lambda e: weigh(e, rim))
    each(0, 4, lambda i: first(brink(i), everywhere, flows))
    each(3, end - 1, lambda e: first(e, rim, flows))
    each(0, 2, lambda i: second(2 + i * (end - 3), inside, flows))
    each(3, end - 1, lambda e: second(e, rim[:2], flows))

    span = 128 * LEVELS
    pick = jnp.where(
        lax.broadcasted_iota(jnp.int32, (span, 128), 0) // LEVELS
        == lax.broadcasted_iota(jnp.int32, (span, 128), 1),
        1.0 / LEVELS, 0.0).astype(jnp.bfloat16)

    def average(i, carry):
        rows = pl.ds(pl.multiple_of(40 * i, 8), 40)
        for new, mean in ((un, du), (vn, dv)):
            for half in range(2):
                width = span if half == 0 else LANES - span
                values = new[rows, span * half:span * half + width]
                coarse = values.astype(jnp.bfloat16)
                fine = (values - coarse.astype(jnp.float32)).astype(jnp.bfloat16)
                mean[rows, 128 * half:128 * half + 128] = (
                    jnp.dot(coarse, pick[:width], preferred_element_type=jnp.float32)
                    + jnp.dot(fine, pick[:width], preferred_element_type=jnp.float32))
        return carry

    lax.fori_loop(0, ROWS // 40, average, 0)

    shape = (ROWS, COLS)
    row, col = rows_of(shape), lanes_of(shape)
    w = jnp.zeros(shape, jnp.float32)
    for i in range(2):
        for j in range(4):
            here = jnp.logical_and(row // BLOCK == i, col // BLOCK == j)
            w = jnp.where(here, flags[i, j].astype(jnp.float32), w)
    plane[:, :, 128:256] = jnp.zeros((4, ROWS + 16, 128), jnp.float32)
    plane[0, 0:ROWS, 0:COLS] = w * (zavg[...] + du[:, 0:COLS])
    plane[1, 0:ROWS, 0:COLS] = w * (mavg[...] + dv[:, 0:COLS])
    plane[2, 0:ROWS, 0:COLS] = w * elev[...]
    plane[3, 0:ROWS, 0:COLS] = w
    right = jnp.zeros((ROWS, 128), jnp.float32)
    left = jnp.zeros((ROWS, 128), jnp.float32)
    for p in range(4):
        right = jnp.where(lane_c // 8 == p, pltpu.roll(plane[p, 0:ROWS, 128:256], 8 * p + 24, 1), right)
        begin = plane[p, 0:ROWS, 0:128]
        left = jnp.where(lane_c // 8 == p, pltpu.roll(begin, 8 * p, 1) if p else begin, left)
    epack2[...] = right
    wpack2[...] = left
    north, south = plane.at[:, pl.ds(ROWS - 8, 8), :], plane.at[:, pl.ds(0, 8), :]
    wires2 = near.wire(north, south, epack2, wpack2, rn2, rs2, rw2, re2, send2, recv2)
    near.start(wires2, epack2, wpack2, rw2, re2)

    for f in tracers:
        for copy in loads[f]:
            copy.wait()
    each(2, end, lambda e: mask(e, tracers))
    each(1, end + 1, lambda e: first(e, everywhere, tracers))
    each(2, end, lambda e: second(e, inside, tracers))

    near.finish(wires2)

    @pl.when(near.x == 0)
    def _():
        rs2[...] = jnp.zeros(rs2.shape, jnp.float32)
        rw2[0:8, :] = jnp.zeros((8, 128), jnp.float32)
        re2[0:8, :] = jnp.zeros((8, 128), jnp.float32)

    @pl.when(near.top)
    def _():
        reverse = (1, 2, 4, 8, 16, 32, 64)
        for p in range(4):
            sign = -1.0 if p < 2 else 1.0
            start = sign * turn_rows(turn_lanes(rn2[p, :, 128:256], reverse))
            last = sign * turn_rows(turn_lanes(rn2[p, :, 0:128], reverse))
            rn2[p] = pltpu.roll(jnp.concatenate([start, last], axis=1), COLS, 1)
        flow = jnp.where(lane < 16, -1.0, 1.0)
        for got in (rw2, re2):
            tile = got[pl.ds(ROWS + 8, 8), :]
            got[pl.ds(ROWS + 8, 8), :] = flow * turn_rows(turn_lanes(tile, (1, 2, 4)))

    plane[:, ROWS:ROWS + 8, :] = rn2[...]
    plane[:, ROWS + 8:ROWS + 16, :] = rs2[...]
    for to, at, number in ((0, 8, ROWS), (ROWS, ROWS + 8, 8), (ROWS + 8, 0, 8)):
        lane_p = lanes_of((number, 128))
        west, east = rw2[at:at + number, :], re2[at:at + number, :]
        for p in range(4):
            halo = jnp.where(lane_p < 120, pltpu.roll(east, 112 - 8 * p, 1), pltpu.roll(west, 120 - 8 * p, 1))
            plane[p, to:to + number, 128:256] = jnp.where(
                lane_p < 112, plane[p, to:to + number, 128:256], halo)

    zt, mt, h, w = plane[0], plane[1], plane[2], plane[3]
    across, along = 256, ROWS + 16
    for _ in range(NSUB):
        spread = (pltpu.roll(zt, across - 1, 1) - pltpu.roll(zt, 1, 1)) + (
            pltpu.roll(mt, along - 1, 0) - pltpu.roll(mt, 1, 0))
        h = h - 0.3 * w * spread
        zt = w * (zt - 0.3 * (pltpu.roll(h, across - 1, 1) - pltpu.roll(h, 1, 1)))
        mt = w * (mt - 0.3 * (pltpu.roll(h, along - 1, 0) - pltpu.roll(h, 1, 0)))
    zt, mt = zt[0:ROWS], mt[0:ROWS]
    du[...] = zt - du[...]
    dv[...] = mt - dv[...]
    height[...] = h[0:ROWS, 0:COLS]
    zonal[...] = zt[:, 0:COLS]
    merid[...] = mt[:, 0:COLS]


def finish_kernel(
    tn, sn, un, vn, du, dv, height, zonal, merid,
    t_out, s_out, u_out, v_out, height_out, zonal_out, merid_out, done, sems,
):
    copies = [
        pltpu.make_async_copy(src, dst, sems.at[i])
        for i, (src, dst) in enumerate(
            ((tn, t_out), (sn, s_out), (height, height_out), (zonal, zonal_out), (merid, merid_out)))
    ]
    for copy in copies:
        copy.start()
    step = 24
    for i in range(ROWS // step):
        for f, (new, change, out) in enumerate(((un, du, u_out), (vn, dv, v_out))):
            for r in range(step * i, step * i + step, 8):
                for half in range(2):
                    tile = change[r:r + 8, 128 * half:128 * half + 128]
                    for k in range(8 * half, min(8 * half + 8, TILES)):
                        at = slice(128 * k, 128 * k + 128)
                        done[f, r:r + 8, at] = new[r:r + 8, at] + expand(tile, k % 8)
            rows = pl.ds(step * i, step)
            copies.append(pltpu.make_async_copy(done.at[f, rows, :], out.at[rows, :], sems.at[5 + 2 * i + f]))
            copies[-1].start()
    for copy in copies:
        copy.wait()


def per_device(nb, nw, t, s, u, v, elev, zavg, mavg, flags, sel, ktab, btab):
    f32 = jnp.float32
    vmem = pl.BlockSpec(memory_space=pltpu.VMEM)
    hbm = pl.BlockSpec(memory_space=pl.ANY)
    scratch = lambda *shape: pltpu.VMEM(shape, f32)
    dma = lambda *shape: pltpu.SemaphoreType.DMA(shape)
    parts = pl.pallas_call(
        functools.partial(step_kernel, nb, nw),
        out_shape=(pltpu.VMEM((ROWS, LANES), f32),) * 4
        + (pltpu.VMEM((ROWS, 256), f32),) * 2
        + (pltpu.VMEM((ROWS, COLS), f32),) * 3,
        in_specs=[hbm] * 11,
        out_specs=(vmem,) * 9,
        scratch_shapes=[
            pltpu.SMEM((2, 4), jnp.int32),
            pltpu.SMEM((8,), f32),
            pltpu.SMEM((8,), f32),
            pltpu.VMEM((ROWS, COLS), jnp.int32),
            scratch(ROWS, COLS), scratch(ROWS, COLS), scratch(ROWS, COLS),
            scratch(4, 2, 8, LANES), scratch(4, 2, ROWS, 128),
            scratch(8, LANES + 128), scratch(8, LANES + 128), scratch(ROWS, 128), scratch(ROWS, 128),
            scratch(8, LANES + 128), scratch(8, LANES + 128), scratch(ROWS + 16, 128), scratch(ROWS + 16, 128),
            scratch(4, RING, BAND, 128), scratch(4, RING, BAND, 128), scratch(4, TILES, BAND, 128),
            scratch(RING, BAND, 128), scratch(RING, BAND, 128),
            scratch(TILES, BAND, 128), scratch(TILES, BAND, 128), scratch(2, 2, BAND, 128),
            scratch(4, ROWS + 16, 256), scratch(ROWS, 128), scratch(ROWS, 128),
            scratch(4, 8, 256), scratch(4, 8, 256), scratch(ROWS + 16, 128), scratch(ROWS + 16, 128),
            dma(24), dma(4, TILES), dma(8), dma(8), dma(8), dma(8),
        ],
        compiler_params=pltpu.CompilerParams(
            collective_id=0, has_side_effects=True, vmem_limit_bytes=VMEM_BYTES),
        name="step",
    )(flags, ktab, btab, sel, t, s, u, v, zavg, mavg, elev)
    parts = [pltpu.with_memory_space_constraint(part, pltpu.VMEM) for part in parts]

    big = jax.ShapeDtypeStruct((ROWS, LANES), f32)
    flat = jax.ShapeDtypeStruct((ROWS, COLS), f32)
    return pl.pallas_call(
        finish_kernel,
        out_shape=(big,) * 4 + (flat,) * 3,
        in_specs=[vmem] * 9,
        out_specs=(hbm,) * 7,
        scratch_shapes=[scratch(2, ROWS, LANES), dma(15)],
        compiler_params=pltpu.CompilerParams(vmem_limit_bytes=VMEM_BYTES),
        name="finish",
    )(*parts)


def solution(mesh):
    grid = P("wide", "blocks")
    return jax.shard_map(
        functools.partial(per_device, mesh.shape["blocks"], mesh.shape["wide"]),
        mesh=mesh,
        in_specs=(grid,) * 9 + (P(), P()),
        out_specs=(grid,) * 7,
        check_vma=False,
    )
```

time: 46.7 us -> 32.3 us (0.69); the launches traced: 45.9 us -> 32.2 us
  Pallas kernels: 45.3 us -> 31.6 us
    pallas_call x4 -> x2, Pallas kernels: 45.3 us -> 31.6 us  [the longest x1 29.4 us: per_device(): pl.pallas_call(functools.partial(step_kernel, nb, nw), out_shape=(pltpu.V...]
where the time goes in v1:
time: 32.3 us; the launch traced here: 32.2 us
  Pallas kernels  31.6 us (98%)
  between operations  0.64 us (2%)
    pallas_call x1, Pallas kernels, per_device(): pl.pallas_call(functools.partial(step_kernel, nb, nw), out_shape=(pltpu.V...  29.4 us
    pallas_call x1, Pallas kernels, per_device(): pl.pallas_call(finish_kernel, out_shape=(big,) * 4 + (flat,) * 3, in_spec...  2.16 us

profile of v1, /device:TPU:7, one launch (start us, length us, event | category | flops | bytes accessed | tf_op | source)
XLA Modules:
  0.0 32.2 jit_solution(5060818957627169991)
XLA Ops:
  0.6 29.4 %step.1 = (f32[120,1920]{1,0:T(8,128)S(1)}, f32[120,1920]{1,0:T(8,128)S(1)}, f32[120,1920]{1,0:T(8,128)S(1)}, f32[120,1920]{1,0:T(8,128)S(1)}, f32[120,256]{1,0:...) custom-call(s32[2,4]{1,0:T(2,128)} %flags_in.1, ...), custom_call_target="tpu_custom_call" | custom-call | tf_op jit(solution)/shard_map/step/pallas_call | solution.py:574
  30.1 2.2 %finish.1 = (f32[120,1920]{1,0:T(8,128)}, f32[120,1920]{1,0:T(8,128)}, f32[120,1920]{1,0:T(8,128)}, f32[120,1920]{1,0:T(8,128)}, f32[120,240]{1,0:T(8,128)}, /*index=5*/f32[120,240]{1,0:T(8,128)}, f32[120,240]{1,0:T(8,128)}) custom-call(f32[120,1920]{1,0:T(8,128)S(1)} %get-tuple-element.16.tn, f32[120,1920]{1,0:T(8,128)S(1)} %get-tuple-element.17.sn, ...), custom_call_target="tpu_custom_call" | custom-call | tf_op jit(solution)/shard_map/finish/pallas_call | solution.py:605

commit v2 on v1

v2 whole, which is shorter than its diff:
```python
import functools

import jax
import jax.numpy as jnp
from jax import lax
from jax.experimental import pallas as pl
from jax.experimental.pallas import tpu as pltpu
from jax.sharding import PartitionSpec as P

BLOCK = 60
LEVELS = 8
NSUB = 4
ROWS = 120
COLS = 240
LANES = COLS * LEVELS
TILES = LANES // 128
RING = TILES + 1
PAD = 16
BAND = ROWS + 2 * PAD
MESH = pl.DeviceIdType.MESH
VMEM_BYTES = 56 * 1024 * 1024


def lanes_of(shape=(8, 128)):
    return lax.broadcasted_iota(jnp.int32, shape, 1)


def rows_of(shape=(8, 128)):
    return lax.broadcasted_iota(jnp.int32, shape, 0)


def lane_xor(tile, bit):
    keep = (lanes_of(tile.shape) // bit) % 2 == 0
    return jnp.where(keep, pltpu.roll(tile, 128 - bit, 1), pltpu.roll(tile, bit, 1))


def row_xor(tile, bit):
    keep = (rows_of(tile.shape) // bit) % 2 == 0
    return jnp.where(keep, pltpu.roll(tile, 8 - bit, 0), pltpu.roll(tile, bit, 0))


def turn_lanes(tile, bits):
    for bit in bits:
        tile = lane_xor(tile, bit)
    return tile


def turn_rows(tile):
    for bit in (1, 2, 4):
        tile = row_xor(tile, bit)
    return tile


class Neighbours:
    def __init__(self, nb, nw):
        b, x = lax.axis_index("blocks"), lax.axis_index("wide")
        self.b, self.x = b, x
        self.top, self.inner, self.above = x == nw - 1, x < nw - 1, x > 0
        self.east, self.west = lax.rem(b + 1, nb), lax.rem(b + nb - 1, nb)
        self.fold = nb - 1 - b
        self.fold_east = lax.rem(2 * nb - 2 - b, nb)
        self.fold_west = lax.rem(nb - b, nb)
        self.own_east = jnp.logical_and(self.top, self.fold_east == b)
        self.own_west = jnp.logical_and(self.top, self.fold_west == b)
        self.far_east = jnp.logical_and(self.top, self.fold_east != b)
        self.far_west = jnp.logical_and(self.top, self.fold_west != b)

    def greet(self):
        sem = pltpu.get_barrier_semaphore()

        def greet(b, x):
            pl.semaphore_signal(sem, inc=1, device_id=(b, x), device_id_type=MESH)

        b, x = self.b, self.x
        greet(self.east, x)
        greet(self.west, x)

        @pl.when(self.inner)
        def _():
            greet(b, x + 1)
            greet(self.east, x + 1)
            greet(self.west, x + 1)

        @pl.when(self.top)
        def _():
            greet(self.fold, x)

        @pl.when(self.far_east)
        def _():
            greet(self.fold_east, x)

        @pl.when(self.far_west)
        def _():
            greet(self.fold_west, x)

        @pl.when(self.above)
        def _():
            greet(b, x - 1)
            greet(self.east, x - 1)
            greet(self.west, x - 1)

    def meet(self):
        sem = pltpu.get_barrier_semaphore()
        x = self.x
        own = jnp.logical_or(self.own_east, self.own_west)

        @pl.when(x == 0)
        def _():
            pl.semaphore_wait(sem, 5)

        @pl.when(own)
        def _():
            pl.semaphore_wait(sem, 7)

        @pl.when(jnp.logical_and(self.above, jnp.logical_not(own)))
        def _():
            pl.semaphore_wait(sem, 8)

    def wire(self, north, south, east, west, rn, rs, rw, re, send, recv):
        b, x = self.b, self.x
        top_rows, low_rows = pl.ds(ROWS - 8, 8), pl.ds(0, 8)
        mid, lo, hi = pl.ds(8, ROWS), pl.ds(0, 8), pl.ds(ROWS + 8, 8)

        def c(src, dst, way, slot, to_b, to_x):
            return pltpu.make_async_remote_copy(
                src_ref=src, dst_ref=dst, send_sem=send.at[way], recv_sem=recv.at[slot],
                device_id=(to_b, to_x), device_id_type=MESH)

        return dict(
            always=[
                c(east, rw.at[mid], 0, 0, self.east, x),
                c(west, re.at[mid], 1, 1, self.west, x),
            ],
            inner=[
                c(north, rs, 2, 2, b, x + 1),
                c(east.at[top_rows], rw.at[lo], 4, 4, self.east, x + 1),
                c(west.at[top_rows], re.at[lo], 5, 5, self.west, x + 1),
            ],
            above=[
                c(south, rn, 3, 3, b, x - 1),
                c(east.at[low_rows], rw.at[hi], 6, 6, self.east, x - 1),
                c(west.at[low_rows], re.at[hi], 7, 7, self.west, x - 1),
            ],
            top=[c(north, rn, 2, 3, self.fold, x)],
            far_east=[c(east.at[top_rows], re.at[hi], 4, 7, self.fold_east, x)],
            far_west=[c(west.at[top_rows], rw.at[hi], 5, 6, self.fold_west, x)],
        )

    def start(self, wires, east, west, rw, re):
        def go(name, cond):
            @pl.when(cond)
            def _():
                for copy in wires[name]:
                    copy.start()

        go("inner", self.inner)
        go("top", self.top)
        go("above", self.above)
        go("far_east", self.far_east)
        go("far_west", self.far_west)
        for copy in wires["always"]:
            copy.start()

        @pl.when(self.own_east)
        def _():
            re[pl.ds(ROWS + 8, 8), :] = east[pl.ds(ROWS - 8, 8), :]

        @pl.when(self.own_west)
        def _():
            rw[pl.ds(ROWS + 8, 8), :] = west[pl.ds(ROWS - 8, 8), :]

    def finish(self, wires):
        w = wires
        for copy in w["always"]:
            copy.wait_recv()
            copy.wait_send()
        w["top"][0].wait_recv()

        @pl.when(self.above)
        def _():
            for copy in w["inner"]:
                copy.wait_recv()
            for copy in w["above"]:
                copy.wait_send()

        @pl.when(jnp.logical_not(self.own_east))
        def _():
            w["far_east"][0].wait_recv()
            w["far_east"][0].wait_send()

        @pl.when(jnp.logical_not(self.own_west))
        def _():
            w["far_west"][0].wait_recv()
            w["far_west"][0].wait_send()

        w["top"][0].wait_send()


def block_row(flags, row, tile):
    low, high = (128 * tile) // (BLOCK * LEVELS), (128 * tile + 127) // (BLOCK * LEVELS)
    value = jnp.full((8, 128), flags[row, low].astype(jnp.float32))
    if low != high:
        value = jnp.where(
            lanes_of() < BLOCK * LEVELS * high - 128 * tile,
            value,
            flags[row, high].astype(jnp.float32),
        )
    return value


def expand(tile, part):
    index = lanes_of() // LEVELS + 16 * part
    return jnp.take_along_axis(tile, index, axis=1, mode="promise_in_bounds")


def step_kernel(
    nb, nw, flags_in, ktab_in, btab_in, sel_in, t, s, u, v, zavg_in, mavg_in, elev_in,
    tn, sn, un, vn, du, dv, height, zonal, merid,
    flags, ktab, btab, sel, zavg, mavg, elev,
    raw, npack, spack, wpack, epack, rn, rs, rw, re,
    field, once, part, wet, count, wide_k, wide_b, mix, pick, mean,
    plane, wpack2, epack2, rn2, rs2, rw2, re2,
    small, load, send, recv, send2, recv2,
):
    sources = (t, s, u, v)
    results = (tn, sn, un, vn)
    near = Neighbours(nb, nw)
    near.greet()

    tables = [
        pltpu.make_async_copy(src, dst, small.at[i])
        for i, (src, dst) in enumerate(
            ((flags_in, flags), (ktab_in, ktab), (btab_in, btab), (sel_in, sel),
             (zavg_in, zavg), (mavg_in, mavg), (elev_in, elev)))
    ]
    loads = [pltpu.make_async_copy(src, raw.at[f], load.at[f]) for f, src in enumerate(sources)]
    tables[0].start()
    for copy in loads:
        copy.start()
    for copy in tables[1:]:
        copy.start()

    lane, sub = lanes_of(), rows_of()
    end = 2 + ROWS // 8
    middle = 2 + BLOCK // 8
    split = BLOCK % 8
    early, late = range(2, middle), range(middle + 1, end)
    flows, tracers = (2, 3), (0, 1)
    inside, everywhere, rim = range(TILES), range(RING), (0, TILES - 1, TILES)

    tables[0].wait()
    lows = [block_row(flags, 0, k) for k in inside] + [jnp.zeros((8, 128), jnp.float32)]
    highs = [block_row(flags, 1, k) for k in inside] + [jnp.zeros((8, 128), jnp.float32)]

    def beside(tiles, k):
        left = pltpu.roll(tiles[k], 128 - LEVELS, 1)
        next_left = pltpu.roll(tiles[(k + 1) % RING], 128 - LEVELS, 1)
        right = pltpu.roll(tiles[k], LEVELS, 1)
        last_right = pltpu.roll(tiles[(k - 1) % RING], LEVELS, 1)
        return jnp.where(lane < 128 - LEVELS, left, next_left) + jnp.where(lane < LEVELS, last_right, right)

    for k in inside:
        low, high = lows[k], highs[k]
        side_low, side_high = beside(lows, k), beside(highs, k)
        count_low, count_high = low * (side_low + (low + low)), high * (side_high + (high + high))
        mixed = jnp.where(sub < split, low, high)
        north = jnp.where(sub < split - 1, low, high)
        south = jnp.where(sub < split + 1, low, high)
        for e in early:
            wet[k, 8 * e:8 * e + 8, :] = low
            count[k, 8 * e:8 * e + 8, :] = count_low
        for e in late:
            wet[k, 8 * e:8 * e + 8, :] = high
            count[k, 8 * e:8 * e + 8, :] = count_high
        wet[k, 8 * middle:8 * middle + 8, :] = mixed
        count[k, 8 * middle:8 * middle + 8, :] = mixed * (
            jnp.where(sub < split, side_low, side_high) + (north + south))

    for copy in loads:
        copy.wait()
    for k in inside:
        at = slice(128 * k, 128 * k + 128)
        south, north = jnp.zeros((8, 128), jnp.float32), jnp.zeros((8, 128), jnp.float32)
        for f in range(4):
            below, above = raw[f, 0:8, at], raw[f, ROWS - 8:ROWS, at]
            south = jnp.where(sub // 2 == f, pltpu.roll(below, 2 * f, 0) if f else below, south)
            north = jnp.where(sub // 2 == f, pltpu.roll(above, 2 * f + 2, 0) if f < 3 else above, north)
        spack[k] = south * lows[k]
        npack[k] = north * highs[k]
    for row, pack in ((0, spack), (1, npack)):
        tail = jnp.zeros((8, 128), jnp.float32)
        for j in range(4):
            tail = jnp.where(lane // 32 == j, flags[row, j].astype(jnp.float32), tail)
        pack[TILES] = tail
    lane_c, row_c = lanes_of((ROWS, 128)), rows_of((ROWS, 128))
    for side, col, pack in ((0, 0, wpack), (1, 3, epack)):
        w = jnp.where(row_c < BLOCK, flags[0, col].astype(jnp.float32), flags[1, col].astype(jnp.float32))
        packed = jnp.ones((ROWS, 128), jnp.float32)
        for f in range(4):
            shift = (16 * f + (16 if side else 0)) % 128
            tile = raw[f, :, (LANES - 128) * side:(LANES - 128) * side + 128]
            packed = jnp.where(lane_c // 16 == f, pltpu.roll(tile, shift, 1) if shift else tile, packed)
        pack[...] = packed * w
    near.meet()
    into = pl.ds(8, 8)
    wires = near.wire(
        npack, spack, epack, wpack, rn.at[:, into, :], rs.at[:, into, :], rw, re, send, recv)
    near.start(wires, epack, wpack, rw, re)

    for copy in tables[1:]:
        copy.wait()
    for half, width in ((0, 128), (1, COLS - 128)):
        for r in range(0, ROWS, 40):
            index = sel[r:r + 40, 128 * half:128 * half + width]
            kappa = jnp.full(index.shape, ktab[0])
            bihar = jnp.full(index.shape, btab[0])
            for n in range(1, 8):
                hit = index == n
                kappa = jnp.where(hit, ktab[n], kappa)
                bihar = jnp.where(hit, btab[n], bihar)
            mix[0, half, PAD + r:PAD + r + 40, 0:width] = kappa
            mix[1, half, PAD + r:PAD + r + 40, 0:width] = bihar

    own = pl.ds(PAD, ROWS)
    for half, width in ((0, 128), (1, COLS - 128)):
        w = jnp.zeros((ROWS, 128), jnp.float32)
        for i in range(2):
            for j in range(4):
                here = jnp.logical_and(row_c // BLOCK == i, (lane_c + 128 * half) // BLOCK == j)
                w = jnp.where(here, flags[i, j].astype(jnp.float32), w)
        if width < 128:
            for p in range(3):
                plane[p, half, own, :] = jnp.zeros((ROWS, 128), jnp.float32)
        plane[3, half, own, :] = w
        at = slice(128 * half, 128 * half + width)
        for p, ref in ((0, zavg), (1, mavg), (2, elev)):
            plane[p, half, own, 0:width] = w[:, 0:width] * ref[:, at]

    def pack_planes(which, right, left):
        for p in which:
            right = jnp.where(lane_c // 8 == p, pltpu.roll(plane[p, 1, own, :], 8 * p + 24, 1), right)
            begin = plane[p, 0, own, :]
            left = jnp.where(lane_c // 8 == p, pltpu.roll(begin, 8 * p, 1) if p else begin, left)
        epack2[...] = right
        wpack2[...] = left

    pack_planes((2, 3), jnp.zeros((ROWS, 128), jnp.float32), jnp.zeros((ROWS, 128), jnp.float32))
    span = 128 * LEVELS
    pick[...] = jnp.where(
        lax.broadcasted_iota(jnp.int32, (span, 128), 0) // LEVELS
        == lax.broadcasted_iota(jnp.int32, (span, 128), 1),
        1.0 / LEVELS, 0.0).astype(jnp.bfloat16)

    def around(ref, turned, key, k, base):
        here, above, below = pl.ds(base, 8), pl.ds(base + 1, 8), pl.ds(base - 1, 8)

        def ring(k):
            if (key, k) not in turned:
                tile = ref[k, here, :]
                turned[key, k] = (tile, pltpu.roll(tile, 128 - LEVELS, 1), pltpu.roll(tile, LEVELS, 1))
            return turned[key, k]

        tile, left, right = ring(k)
        east = jnp.where(lane < 128 - LEVELS, left, ring((k + 1) % RING)[1])
        west = jnp.where(lane < LEVELS, ring((k - 1) % RING)[2], right)
        return tile, east, west, ref[k, above, :], ref[k, below, :]

    def at_tile(e):
        return 8 * e if isinstance(e, int) else pl.multiple_of(8 * e, 8)

    def weigh(e, tiles, same):
        base = at_tile(e)
        turned = {}
        for k in tiles:
            w, we, ww, wn, ws = around(wet, turned, "wet", k, base)
            total = w * ((we + ww) + (wn + ws))
            for to in same:
                count[k, 8 * to:8 * to + 8, :] = total

    def mask(e, which):
        base = at_tile(e)
        rows, here = pl.ds(base - PAD, 8), pl.ds(base, 8)
        for k in inside:
            w = wet[k, here, :]
            for f in which:
                field[f, k, here, :] = raw[f, rows, 128 * k:128 * k + 128] * w

    def first(e, tiles, which, fresh=False, whole=True):
        base = at_tile(e)
        here = pl.ds(base, 8)
        turned = {}
        for k in tiles:
            w, total = wet[k, here, :], count[k, here, :]
            full = whole and k < TILES
            if full:
                if fresh:
                    kappa = expand(mix[0, k // 8, here, :], k % 8)
                    bihar = expand(mix[1, k // 8, here, :], k % 8)
                    wide_k[k, here, :] = kappa
                    wide_b[k, here, :] = bihar
                else:
                    kappa, bihar = wide_k[k, here, :], wide_b[k, here, :]
                mixing = kappa + bihar * total
                zonal_own = 0.05 * field[2, k, here, :]
                merid_own = 0.05 * field[3, k, here, :]
            for f in which:
                c, fe, fw, fn, fs = around(field.at[f], turned, f, k, base)
                lap = w * ((fe + fw) + (fn + fs)) - total * c
                once[f, k, here, :] = lap
                if full:
                    part[f, k, here, :] = (
                        c - (zonal_own * (fe - fw) + merid_own * (fn - fs))) + mixing * lap

    def second(e, tiles, which):
        base = at_tile(e)
        here, rows = pl.ds(base, 8), pl.ds(base - PAD, 8)
        turned = {}
        for k in tiles:
            fade = wide_b[k, here, :] * wet[k, here, :]
            for f in which:
                _, le, lw, ln, ls = around(once.at[f], turned, f, k, base)
                results[f][rows, 128 * k:128 * k + 128] = (
                    part[f, k, here, :] - fade * ((le + lw) + (ln + ls)))

    def by_three(low, high, step):
        def body(i, carry):
            for j in range(3):
                step(low + 3 * i + j)
            return carry
        lax.fori_loop(0, (high - low) // 3, body, 0)

    by_three(2, end, lambda e: mask(e, flows))
    by_three(2, end, lambda e: first(e, inside, flows, fresh=True))
    by_three(3, end - 2, lambda e: second(e, range(1, TILES - 1), flows))
    second(end - 2, range(1, TILES - 1), flows)

    near.finish(wires)

    @pl.when(near.x == 0)
    def _():
        rs[:, 8:16, :] = jnp.zeros((RING, 8, 128), jnp.float32)
        rw[0:8, :] = jnp.zeros((8, 128), jnp.float32)
        re[0:8, :] = jnp.zeros((8, 128), jnp.float32)

    @pl.when(near.top)
    def _():
        sign = jnp.where(sub < 4, 1.0, -1.0)
        tiles = [rn[TILES - 1 - k, 8:16, :] for k in inside]
        for k in inside:
            rn[k, 8:16, :] = sign * row_xor(turn_lanes(tiles[k], (8, 16, 32, 64)), 1)
        rn[TILES, 8:16, :] = turn_lanes(rn[TILES, 8:16, :], (32, 64))
        flow = jnp.where(lane // 32 == 1, -1.0, 1.0)
        for got in (rw, re):
            tile = got[ROWS + 8:ROWS + 16, :]
            got[ROWS + 8:ROWS + 16, :] = flow * turn_rows(lane_xor(tile, 8))

    for got, base in ((rs, PAD - 8), (rn, PAD + ROWS)):
        tail = got[TILES, 8:16, :]
        flag = [jnp.broadcast_to(tail[:, 32 * j:32 * j + 1], (8, 128)) for j in range(4)]
        for k in inside:
            low, high = (128 * k) // (BLOCK * LEVELS), (128 * k + 127) // (BLOCK * LEVELS)
            value = flag[low]
            if low != high:
                value = jnp.where(lane < BLOCK * LEVELS * high - 128 * k, value, flag[high])
            wet[k, base:base + 8, :] = value
    lane_h = lanes_of((ROWS + 16, 128))
    ends = slice(PAD - 8, PAD + ROWS + 8)
    west, east = rw[...], re[...]
    wet[TILES, ends, :] = jnp.where(lane_h < 64, pltpu.roll(east, 64, 1), west)

    def halo(which):
        west, east = rw[...], re[...]
        for f in which:
            right = pltpu.roll(east, (128 - 16 * f) % 128, 1) if f else east
            field[f, TILES, ends, :] = jnp.where(lane_h < 64, right, pltpu.roll(west, 112 - 16 * f, 1))
            for k in inside:
                field[f, k, PAD - 8:PAD, :] = rs[k, 2 * f + 2:2 * f + 10, :]
                field[f, k, PAD + ROWS:PAD + ROWS + 8, :] = rn[k, 2 * f + 8:2 * f + 16, :]

    halo(flows)

    for e in (1, 2, end - 1, end):
        weigh(e, everywhere, (e,))
    weigh(3, rim, early[1:])
    weigh(middle, rim, (middle,))
    weigh(middle + 1, rim, late[:-1])
    for e in (1, 2, end - 1, end):
        first(e, everywhere, flows, whole=1 < e < end)
    for e in range(3, end - 1):
        first(e, rim, flows)
    for e in (2, end - 1):
        second(e, inside, flows)
    for e in range(3, end - 1):
        second(e, rim[:2], flows)

    for half in range(2):
        width = span if half == 0 else LANES - span
        pieces = []
        for new in (un, vn):
            values = new[:, span * half:span * half + width]
            coarse = values.astype(jnp.bfloat16)
            pieces += [coarse, (values - coarse.astype(jnp.float32)).astype(jnp.bfloat16)]
        means = jnp.dot(
            jnp.concatenate(pieces, axis=0), pick[0:width, :], preferred_element_type=jnp.float32)
        for f in range(2):
            value = means[256 * f:256 * f + ROWS] + means[256 * f + 128:256 * f + 128 + ROWS]
            mean[f, half] = value
            plane[f, half, own, :] = plane[f, half, own, :] + value

    pack_planes((0, 1), epack2[...], wpack2[...])
    north = plane.at[:, :, pl.ds(PAD + ROWS - 8, 8), :]
    south = plane.at[:, :, pl.ds(PAD, 8), :]
    wires2 = near.wire(north, south, epack2, wpack2, rn2, rs2, rw2, re2, send2, recv2)
    near.start(wires2, epack2, wpack2, rw2, re2)

    halo(tracers)
    by_three(2, end, lambda e: mask(e, tracers))
    for e in (1, end):
        first(e, everywhere, tracers, whole=False)
    by_three(2, end, lambda e: first(e, everywhere, tracers))
    by_three(2, end, lambda e: second(e, inside, tracers))

    near.finish(wires2)

    @pl.when(near.x == 0)
    def _():
        rs2[...] = jnp.zeros(rs2.shape, jnp.float32)
        rw2[0:8, :] = jnp.zeros((8, 128), jnp.float32)
        re2[0:8, :] = jnp.zeros((8, 128), jnp.float32)

    @pl.when(near.top)
    def _():
        reverse = (1, 2, 4, 8, 16, 32, 64)
        for p in range(4):
            sign = -1.0 if p < 2 else 1.0
            start = sign * turn_rows(turn_lanes(rn2[p, 1], reverse))
            last = sign * turn_rows(turn_lanes(rn2[p, 0], reverse))
            start, last = pltpu.roll(start, 112, 1), pltpu.roll(last, 112, 1)
            rn2[p, 0] = jnp.where(lane < 112, start, last)
            rn2[p, 1] = jnp.where(lane < 112, last, start)
        flow = jnp.where(lane < 16, -1.0, 1.0)
        for got in (rw2, re2):
            tile = got[ROWS + 8:ROWS + 16, :]
            got[ROWS + 8:ROWS + 16, :] = flow * turn_rows(turn_lanes(tile, (1, 2, 4)))

    for p in range(4):
        for half in range(2):
            plane[p, half, PAD - 8:PAD, :] = rs2[p, half]
            plane[p, half, PAD + ROWS:PAD + ROWS + 8, :] = rn2[p, half]
    west, east = rw2[...], re2[...]
    for p in range(4):
        beyond = jnp.where(lane_h < 120, pltpu.roll(east, 112 - 8 * p, 1), pltpu.roll(west, 120 - 8 * p, 1))
        plane[p, 1, ends, :] = jnp.where(lane_h < 112, plane[p, 1, ends, :], beyond)

    def pair(p, e):
        tiles = [plane[p, half, 8 * e:8 * e + 8, :] for half in range(2)]
        left = [pltpu.roll(tile, 127, 1) for tile in tiles]
        right = [pltpu.roll(tile, 1, 1) for tile in tiles]
        return tiles, [
            jnp.where(lane < 127, left[half], left[1 - half]) - jnp.where(lane < 1, right[1 - half], right[half])
            for half in range(2)
        ]

    def rows_apart(p, half, e):
        return plane[p, half, 8 * e + 1:8 * e + 9, :] - plane[p, half, 8 * e - 1:8 * e + 7, :]

    for _ in range(NSUB):
        for e in range(1, end + 1):
            _, across = pair(0, e)
            for half in range(2):
                here = (half, slice(8 * e, 8 * e + 8), slice(None))
                spread = across[half] + rows_apart(1, half, e)
                plane[(2,) + here] = plane[(2,) + here] - 0.3 * plane[(3,) + here] * spread
        for e in range(1, end + 1):
            _, across = pair(2, e)
            for half in range(2):
                here = (half, slice(8 * e, 8 * e + 8), slice(None))
                w = plane[(3,) + here]
                plane[(0,) + here] = w * (plane[(0,) + here] - 0.3 * across[half])
                plane[(1,) + here] = w * (plane[(1,) + here] - 0.3 * rows_apart(2, half, e))
    for half, width in ((0, 128), (1, COLS - 128)):
        at = slice(128 * half, 128 * half + 128)
        du[:, at] = plane[0, half, own, :] - mean[0, half]
        dv[:, at] = plane[1, half, own, :] - mean[1, half]
        at = slice(128 * half, 128 * half + width)
        for p, ref in ((0, zonal), (1, merid), (2, height)):
            ref[:, at] = plane[p, half, own, 0:width]


def finish_kernel(
    tn, sn, un, vn, du, dv, height, zonal, merid,
    t_out, s_out, u_out, v_out, height_out, zonal_out, merid_out, done, sems,
):
    copies = [
        pltpu.make_async_copy(src, dst, sems.at[i])
        for i, (src, dst) in enumerate(
            ((tn, t_out), (sn, s_out), (height, height_out), (zonal, zonal_out), (merid, merid_out)))
    ]
    for copy in copies:
        copy.start()
    step = 24
    for i in range(ROWS // step):
        for f, (new, change, out) in enumerate(((un, du, u_out), (vn, dv, v_out))):
            for r in range(step * i, step * i + step, 8):
                for half in range(2):
                    tile = change[r:r + 8, 128 * half:128 * half + 128]
                    for k in range(8 * half, min(8 * half + 8, TILES)):
                        at = slice(128 * k, 128 * k + 128)
                        done[f, r:r + 8, at] = new[r:r + 8, at] + expand(tile, k % 8)
            rows = pl.ds(step * i, step)
            copies.append(pltpu.make_async_copy(done.at[f, rows, :], out.at[rows, :], sems.at[5 + 2 * i + f]))
            copies[-1].start()
    for copy in copies:
        copy.wait()


def per_device(nb, nw, t, s, u, v, elev, zavg, mavg, flags, sel, ktab, btab):
    f32 = jnp.float32
    vmem = pl.BlockSpec(memory_space=pltpu.VMEM)
    hbm = pl.BlockSpec(memory_space=pl.ANY)
    scratch = lambda *shape: pltpu.VMEM(shape, f32)
    dma = lambda *shape: pltpu.SemaphoreType.DMA(shape)
    parts = pl.pallas_call(
        functools.partial(step_kernel, nb, nw),
        out_shape=(pltpu.VMEM((ROWS, LANES), f32),) * 2
        + (pltpu.VMEM((ROWS + 8, LANES), f32),) * 2
        + (pltpu.VMEM((ROWS, 256), f32),) * 2
        + (pltpu.VMEM((ROWS, COLS), f32),) * 3,
        in_specs=[hbm] * 11,
        out_specs=(vmem,) * 9,
        scratch_shapes=[
            pltpu.SMEM((2, 4), jnp.int32),
            pltpu.SMEM((8,), f32),
            pltpu.SMEM((8,), f32),
            pltpu.VMEM((ROWS, COLS), jnp.int32),
            scratch(ROWS, COLS), scratch(ROWS, COLS), scratch(ROWS, COLS),
            scratch(4, ROWS, LANES),
            scratch(RING, 8, 128), scratch(RING, 8, 128), scratch(ROWS, 128), scratch(ROWS, 128),
            scratch(RING, 24, 128), scratch(RING, 24, 128), scratch(ROWS + 16, 128), scratch(ROWS + 16, 128),
            scratch(4, RING, BAND, 128), scratch(4, RING, BAND, 128), scratch(4, TILES, BAND, 128),
            scratch(RING, BAND, 128), scratch(RING, BAND, 128),
            scratch(TILES, BAND, 128), scratch(TILES, BAND, 128), scratch(2, 2, BAND, 128),
            pltpu.VMEM((128 * LEVELS, 128), jnp.bfloat16), scratch(2, 2, ROWS, 128),
            scratch(4, 2, BAND, 128), scratch(ROWS, 128), scratch(ROWS, 128),
            scratch(4, 2, 8, 128), scratch(4, 2, 8, 128), scratch(ROWS + 16, 128), scratch(ROWS + 16, 128),
            dma(7), dma(4), dma(8), dma(8), dma(8), dma(8),
        ],
        compiler_params=pltpu.CompilerParams(
            collective_id=0, has_side_effects=True, vmem_limit_bytes=VMEM_BYTES),
        name="step",
    )(flags, ktab, btab, sel, t, s, u, v, zavg, mavg, elev)
    parts = [pltpu.with_memory_space_constraint(part, pltpu.VMEM) for part in parts]

    big = jax.ShapeDtypeStruct((ROWS, LANES), f32)
    flat = jax.ShapeDtypeStruct((ROWS, COLS), f32)
    return pl.pallas_call(
        finish_kernel,
        out_shape=(big,) * 4 + (flat,) * 3,
        in_specs=[vmem] * 9,
        out_specs=(hbm,) * 7,
        scratch_shapes=[scratch(2, ROWS, LANES), dma(15)],
        compiler_params=pltpu.CompilerParams(vmem_limit_bytes=VMEM_BYTES),
        name="finish",
    )(*parts)


def solution(mesh):
    grid = P("wide", "blocks")
    return jax.shard_map(
        functools.partial(per_device, mesh.shape["blocks"], mesh.shape["wide"]),
        mesh=mesh,
        in_specs=(grid,) * 9 + (P(), P()),
        out_specs=(grid,) * 7,
        check_vma=False,
    )
```

time: 32.3 us -> 24.4 us (0.76)
  Pallas kernels: 31.6 us -> 23.4 us
    pallas_call x1, Pallas kernels: 29.4 us -> 21.2 us  [per_device(): pl.pallas_call(functools.partial(step_kernel, nb, nw), out_shape=(pltpu.V...]
where the time goes in v2:
time: 24.4 us; the launch traced here: 24 us
  Pallas kernels  23.4 us (96%)
  between operations  0.64 us (3%)
    pallas_call x1, Pallas kernels, per_device(): pl.pallas_call(functools.partial(step_kernel, nb, nw), out_shape=(pltpu.V...  21.2 us
    pallas_call x1, Pallas kernels, per_device(): pl.pallas_call(finish_kernel, out_shape=(big,) * 4 + (flat,) * 3, in_spec...  2.16 us

profile of v2, /device:TPU:7, one launch (start us, length us, event | category | flops | bytes accessed | tf_op | source)
XLA Modules:
  0.0 24.0 jit_solution(5506815038005857686)
XLA Ops:
  0.6 21.2 %step.1 = (f32[120,1920]{1,0:T(8,128)S(1)}, f32[120,1920]{1,0:T(8,128)S(1)}, f32[128,1920]{1,0:T(8,128)S(1)}, f32[128,1920]{1,0:T(8,128)S(1)}, f32[120,256]{1,0:...) custom-call(s32[2,4]{1,0:T(2,128)} %flags_in.1, ...), custom_call_target="tpu_custom_call" | custom-call | tf_op jit(solution)/shard_map/step/pallas_call | solution.py:623
  21.8 2.2 %finish.1 = (f32[120,1920]{1,0:T(8,128)}, f32[120,1920]{1,0:T(8,128)}, f32[120,1920]{1,0:T(8,128)}, f32[120,1920]{1,0:T(8,128)}, f32[120,240]{1,0:T(8,128)}, /*index=5*/f32[120,240]{1,0:T(8,128)}, f32[120,240]{1,0:T(8,128)}) custom-call(f32[120,1920]{1,0:T(8,128)S(1)} %get-tuple-element.16.tn, f32[120,1920]{1,0:T(8,128)S(1)} %get-tuple-element.17.sn, ...), custom_call_target="tpu_custom_call" | custom-call | tf_op jit(solution)/shard_map/finish/pallas_call | solution.py:656

commit v3 on v2

v3 whole, which is shorter than its diff:
```python
import functools

import jax
import jax.numpy as jnp
from jax import lax
from jax.experimental import pallas as pl
from jax.experimental.pallas import tpu as pltpu
from jax.sharding import PartitionSpec as P

BLOCK = 60
LEVELS = 8
NSUB = 4
ROWS = 120
COLS = 240
LANES = COLS * LEVELS
TILES = LANES // 128
RING = TILES + 1
PAD = 16
BAND = ROWS + 2 * PAD
MESH = pl.DeviceIdType.MESH
VMEM_BYTES = 56 * 1024 * 1024


def lanes_of(shape=(8, 128)):
    return lax.broadcasted_iota(jnp.int32, shape, 1)


def rows_of(shape=(8, 128)):
    return lax.broadcasted_iota(jnp.int32, shape, 0)


def pick_lanes(tile, index):
    return jnp.take_along_axis(tile, index, axis=1, mode="promise_in_bounds")


def row_xor(tile, bit):
    keep = (rows_of(tile.shape) // bit) % 2 == 0
    return jnp.where(keep, pltpu.roll(tile, 8 - bit, 0), pltpu.roll(tile, bit, 0))


def turn_rows(tile):
    for bit in (1, 2, 4):
        tile = row_xor(tile, bit)
    return tile


class Neighbours:
    def __init__(self, nb, nw):
        b, x = lax.axis_index("blocks"), lax.axis_index("wide")
        self.b, self.x = b, x
        self.top, self.inner, self.above = x == nw - 1, x < nw - 1, x > 0
        self.east, self.west = lax.rem(b + 1, nb), lax.rem(b + nb - 1, nb)
        self.fold = nb - 1 - b
        self.fold_east = lax.rem(2 * nb - 2 - b, nb)
        self.fold_west = lax.rem(nb - b, nb)
        self.own_east = jnp.logical_and(self.top, self.fold_east == b)
        self.own_west = jnp.logical_and(self.top, self.fold_west == b)
        self.far_east = jnp.logical_and(self.top, self.fold_east != b)
        self.far_west = jnp.logical_and(self.top, self.fold_west != b)

    def greet(self):
        sem = pltpu.get_barrier_semaphore()

        def greet(b, x):
            pl.semaphore_signal(sem, inc=1, device_id=(b, x), device_id_type=MESH)

        b, x = self.b, self.x
        greet(self.east, x)
        greet(self.west, x)

        @pl.when(self.inner)
        def _():
            greet(b, x + 1)
            greet(self.east, x + 1)
            greet(self.west, x + 1)

        @pl.when(self.top)
        def _():
            greet(self.fold, x)

        @pl.when(self.far_east)
        def _():
            greet(self.fold_east, x)

        @pl.when(self.far_west)
        def _():
            greet(self.fold_west, x)

        @pl.when(self.above)
        def _():
            greet(b, x - 1)
            greet(self.east, x - 1)
            greet(self.west, x - 1)

    def meet(self):
        sem = pltpu.get_barrier_semaphore()
        x = self.x
        own = jnp.logical_or(self.own_east, self.own_west)

        @pl.when(x == 0)
        def _():
            pl.semaphore_wait(sem, 5)

        @pl.when(own)
        def _():
            pl.semaphore_wait(sem, 7)

        @pl.when(jnp.logical_and(self.above, jnp.logical_not(own)))
        def _():
            pl.semaphore_wait(sem, 8)

    def wire(self, north, south, east, west, rn, rs, rw, re, send, recv):
        b, x = self.b, self.x

        def c(src, dst, way, slot, to_b, to_x):
            return pltpu.make_async_remote_copy(
                src_ref=src, dst_ref=dst, send_sem=send.at[way], recv_sem=recv.at[slot],
                device_id=(to_b, to_x), device_id_type=MESH)

        return dict(
            always=[
                c(east[0], rw[0], 0, 0, self.east, x),
                c(west[0], re[0], 1, 1, self.west, x),
            ],
            inner=[
                c(east[1], rw[1], 4, 4, self.east, x + 1),
                c(west[1], re[1], 5, 5, self.west, x + 1),
                c(north, rs, 2, 2, b, x + 1),
            ],
            above=[
                c(east[2], rw[2], 6, 6, self.east, x - 1),
                c(west[2], re[2], 7, 7, self.west, x - 1),
                c(south, rn, 3, 3, b, x - 1),
            ],
            top=[c(north, rn, 2, 3, self.fold, x)],
            far_east=[c(east[1], re[2], 4, 7, self.fold_east, x)],
            far_west=[c(west[1], rw[2], 5, 6, self.fold_west, x)],
        )

    def start(self, wires, east, west, rw, re):
        def go(name, cond):
            @pl.when(cond)
            def _():
                for copy in wires[name]:
                    copy.start()

        for copy in wires["always"]:
            copy.start()
        go("far_east", self.far_east)
        go("far_west", self.far_west)
        go("top", self.top)
        go("inner", self.inner)
        go("above", self.above)

        @pl.when(self.own_east)
        def _():
            re[2][...] = east[1][...]

        @pl.when(self.own_west)
        def _():
            rw[2][...] = west[1][...]

    def finish(self, wires):
        w = wires
        for copy in w["always"]:
            copy.wait_recv()
            copy.wait_send()
        w["top"][0].wait_recv()

        @pl.when(self.above)
        def _():
            for copy in w["inner"]:
                copy.wait_recv()
            for copy in w["above"]:
                copy.wait_send()

        @pl.when(jnp.logical_not(self.own_east))
        def _():
            w["far_east"][0].wait_recv()
            w["far_east"][0].wait_send()

        @pl.when(jnp.logical_not(self.own_west))
        def _():
            w["far_west"][0].wait_recv()
            w["far_west"][0].wait_send()

        w["top"][0].wait_send()


def block_row(flags, row, tile):
    low, high = (128 * tile) // (BLOCK * LEVELS), (128 * tile + 127) // (BLOCK * LEVELS)
    value = jnp.full((8, 128), flags[row, low].astype(jnp.float32))
    if low != high:
        value = jnp.where(
            lanes_of() < BLOCK * LEVELS * high - 128 * tile,
            value,
            flags[row, high].astype(jnp.float32),
        )
    return value


def expand(tile, part):
    index = lanes_of() // LEVELS + 16 * part
    return pick_lanes(tile, index)


def halves(values):
    coarse = values.astype(jnp.bfloat16)
    return [coarse, (values - coarse.astype(jnp.float32)).astype(jnp.bfloat16)]


def step_kernel(
    nb, nw, flags_in, ktab_in, btab_in, sel_in, t, s, u, v, zavg_in, mavg_in, elev_in,
    tn, sn, un, vn, du, dv, height, zonal, merid,
    flags, ktab, btab, sel, zavg, mavg, elev,
    raw, npack, spack, wpack, epack, rn, rs, rw, re,
    field, once, part, wet, count, wide_k, wide_b, pick, spread_out, mean, base_plane,
    end_field, end_own, end_k, end_b, end_wet, end_side, end_once, end_part, end_new,
    plane, wpack2, epack2, rn2, rs2, rw2, re2,
    small, load, send, recv, send2, recv2,
):
    f32, bf16 = jnp.float32, jnp.bfloat16
    sources = (t, s, u, v)
    results = (tn, sn, un, vn)
    near = Neighbours(nb, nw)
    near.greet()

    tables = [
        pltpu.make_async_copy(src, dst, small.at[i])
        for i, (src, dst) in enumerate(
            ((flags_in, flags), (ktab_in, ktab), (btab_in, btab), (sel_in, sel),
             (elev_in, elev), (zavg_in, zavg), (mavg_in, mavg)))
    ]
    loads = [pltpu.make_async_copy(src, raw.at[f], load.at[f]) for f, src in enumerate(sources)]
    for copy in tables:
        copy.start()
    for copy in loads:
        copy.start()

    lane, sub = lanes_of(), rows_of()
    lane_c, row_c = lanes_of((ROWS, 128)), rows_of((ROWS, 128))
    lane_h = lanes_of((ROWS + 16, 128))
    end = 2 + ROWS // 8
    middle = 2 + BLOCK // 8
    split = BLOCK % 8
    early, late = range(2, middle), range(middle + 1, end)
    flows, tracers = (2, 3), (0, 1)
    inside, everywhere, rim = range(TILES), range(RING), (0, TILES - 1, TILES)
    ends = slice(PAD - 8, PAD + ROWS + 8)
    own = pl.ds(PAD, ROWS)
    span = 128 * LEVELS

    pick[...] = jnp.where(
        lax.broadcasted_iota(jnp.int32, (span, 128), 0) // LEVELS
        == lax.broadcasted_iota(jnp.int32, (span, 128), 1), 1.0 / LEVELS, 0.0).astype(bf16)
    spread_out[...] = jnp.where(
        lax.broadcasted_iota(jnp.int32, (256, span), 0) % 128
        == lax.broadcasted_iota(jnp.int32, (256, span), 1) // LEVELS, 1.0, 0.0).astype(bf16)

    tables[0].wait()
    lows = [block_row(flags, 0, k) for k in inside]
    highs = [block_row(flags, 1, k) for k in inside]

    def beside(tiles, k):
        left = pltpu.roll(tiles[k], 128 - LEVELS, 1)
        next_left = pltpu.roll(tiles[(k + 1) % TILES], 128 - LEVELS, 1)
        right = pltpu.roll(tiles[k], LEVELS, 1)
        last_right = pltpu.roll(tiles[(k - 1) % TILES], LEVELS, 1)
        return jnp.where(lane < 128 - LEVELS, left, next_left) + jnp.where(lane < LEVELS, last_right, right)

    for k in inside:
        low, high = lows[k], highs[k]
        side_low, side_high = beside(lows, k), beside(highs, k)
        count_low, count_high = low * (side_low + (low + low)), high * (side_high + (high + high))
        mixed = jnp.where(sub < split, low, high)
        north = jnp.where(sub < split - 1, low, high)
        south = jnp.where(sub < split + 1, low, high)
        for e in early:
            wet[k, 8 * e:8 * e + 8, :] = low
            count[k, 8 * e:8 * e + 8, :] = count_low
        for e in late:
            wet[k, 8 * e:8 * e + 8, :] = high
            count[k, 8 * e:8 * e + 8, :] = count_high
        wet[k, 8 * middle:8 * middle + 8, :] = mixed
        count[k, 8 * middle:8 * middle + 8, :] = mixed * (
            jnp.where(sub < split, side_low, side_high) + (north + south))

    for copy in tables[1:]:
        copy.wait()
    for half, width in ((0, 128), (1, COLS - 128)):
        w = jnp.zeros((ROWS, 128), f32)
        for i in range(2):
            for j in range(4):
                here = jnp.logical_and(row_c // BLOCK == i, (lane_c + 128 * half) // BLOCK == j)
                w = jnp.where(here, flags[i, j].astype(f32), w)
        plane[3, half, own, :] = w
        if width < 128:
            plane[2, half, own, :] = jnp.zeros((ROWS, 128), f32)
            base_plane[:, half] = jnp.zeros((2, ROWS, 128), f32)
        at = slice(128 * half, 128 * half + width)
        plane[2, half, own, 0:width] = w[:, 0:width] * elev[:, at]
        base_plane[0, half, :, 0:width] = w[:, 0:width] * zavg[:, at]
        base_plane[1, half, :, 0:width] = w[:, 0:width] * mavg[:, at]

    for half, width in ((0, 128), (1, COLS - 128)):
        index = sel[:, 128 * half:128 * half + width]
        if width < 128:
            index = jnp.concatenate([index, jnp.zeros((ROWS, 128 - width), jnp.int32)], axis=1)
        kappa = jnp.full(index.shape, ktab[0])
        bihar = jnp.full(index.shape, btab[0])
        for n in range(1, 8):
            hit = index == n
            kappa = jnp.where(hit, ktab[n], kappa)
            bihar = jnp.where(hit, btab[n], bihar)
        for table, to in ((kappa, wide_k), (bihar, wide_b)):
            wide = jnp.dot(
                jnp.concatenate(halves(table), axis=1), spread_out[...], preferred_element_type=f32)
            for k in range(8 * half, min(8 * half + 8, TILES)):
                to[k, own, :] = wide[:, 128 * (k % 8):128 * (k % 8) + 128]

    for copy in loads:
        copy.wait()
    for k in inside:
        at = slice(128 * k, 128 * k + 128)
        south, north = jnp.zeros((8, 128), f32), jnp.zeros((8, 128), f32)
        for f in range(4):
            below, above = raw[f, 0:8, at], raw[f, ROWS - 8:ROWS, at]
            south = jnp.where(sub // 2 == f, pltpu.roll(below, 2 * f, 0) if f else below, south)
            north = jnp.where(sub // 2 == f, pltpu.roll(above, 2 * f + 2, 0) if f < 3 else above, north)
        spack[k] = south * wet[k, PAD:PAD + 8, :]
        npack[k] = north * wet[k, PAD + ROWS - 8:PAD + ROWS, :]
    for row, pack, at in ((0, spack, PAD), (1, npack, PAD + ROWS - 8)):
        tail = jnp.zeros((8, 128), f32)
        for j in range(4):
            tail = jnp.where(lane // 32 == j, flags[row, j].astype(f32), tail)
        pack[TILES] = tail
        for half in range(2):
            pack[RING + half] = plane[2, half, at:at + 8, :]
    for side, pack in ((0, wpack), (1, epack)):
        w = wet[(TILES - 1) * side, own, :]
        packed = jnp.ones((ROWS, 128), f32)
        for f in range(4):
            shift = (16 * f + 64 * side) % 128
            tile = raw[f, :, (LANES - 128) * side:(LANES - 128) * side + 128]
            place = lane_c // 16 == f + 3 * side
            packed = jnp.where(place, pltpu.roll(tile, shift, 1) if shift else tile, packed)
        packed = packed * w
        top = pltpu.roll(plane[2, side, own, :], 24 if side else 64, 1)
        pack[...] = jnp.where(lane_c // 8 == (0 if side else 8), top, packed)
    near.meet()
    into = pl.ds(8, 8)

    def three(ref):
        return ref, ref.at[pl.ds(ROWS - 8, 8)], ref.at[pl.ds(0, 8)]

    def spots(ref):
        return ref.at[pl.ds(8, ROWS)], ref.at[pl.ds(0, 8)], ref.at[pl.ds(ROWS + 8, 8)]

    east, west, from_west, from_east = three(epack), three(wpack), spots(rw), spots(re)
    wires = near.wire(
        npack, spack, east, west, rn.at[:, into, :], rs.at[:, into, :], from_west, from_east, send, recv)
    near.start(wires, east, west, from_west, from_east)

    def around(ref, turned, key, k, base, ring_size):
        here, above, below = pl.ds(base, 8), pl.ds(base + 1, 8), pl.ds(base - 1, 8)

        def ring(k):
            if (key, k) not in turned:
                tile = ref[k, here, :]
                turned[key, k] = (tile, pltpu.roll(tile, 128 - LEVELS, 1), pltpu.roll(tile, LEVELS, 1))
            return turned[key, k]

        tile, left, right = ring(k)
        east = jnp.where(lane < 128 - LEVELS, left, ring((k + 1) % ring_size)[1])
        west = jnp.where(lane < LEVELS, ring((k - 1) % ring_size)[2], right)
        return tile, east, west, ref[k, above, :], ref[k, below, :]

    def at_tile(e):
        return 8 * e if isinstance(e, int) else pl.multiple_of(8 * e, 8)

    def weigh(base, tiles, same, ring_size=RING):
        turned = {}
        for k in tiles:
            w, we, ww, wn, ws = around(wet, turned, "wet", k, base, ring_size)
            total = w * ((we + ww) + (wn + ws))
            for to in same:
                count[k, to:to + 8, :] = total

    def mask(e, which):
        base = at_tile(e)
        rows, here = pl.ds(base - PAD, 8), pl.ds(base, 8)
        for k in inside:
            w = wet[k, here, :]
            for f in which:
                field[f, k, here, :] = raw[f, rows, 128 * k:128 * k + 128] * w

    def first(base, tiles, which, ring_size, whole=True):
        here = pl.ds(base, 8)
        turned = {}
        for k in tiles:
            w, total = wet[k, here, :], count[k, here, :]
            full = whole and k < TILES
            if full:
                mixing = wide_k[k, here, :] + wide_b[k, here, :] * total
                zonal_own = 0.05 * field[2, k, here, :]
                merid_own = 0.05 * field[3, k, here, :]
            for f in which:
                c, fe, fw, fn, fs = around(field.at[f], turned, f, k, base, ring_size)
                lap = w * ((fe + fw) + (fn + fs)) - total * c
                once[f, k, here, :] = lap
                if full:
                    part[f, k, here, :] = (
                        c - (zonal_own * (fe - fw) + merid_own * (fn - fs))) + mixing * lap

    def second(e, tiles, which, ring_size):
        base = at_tile(e)
        here, rows = pl.ds(base, 8), pl.ds(base - PAD, 8)
        turned = {}
        for k in tiles:
            fade = wide_b[k, here, :] * wet[k, here, :]
            for f in which:
                _, le, lw, ln, ls = around(once.at[f], turned, f, k, base, ring_size)
                results[f][rows, 128 * k:128 * k + 128] = (
                    part[f, k, here, :] - fade * ((le + lw) + (ln + ls)))

    def by_three(low, high, step):
        def body(i, carry):
            for j in range(3):
                step(low + 3 * i + j)
            return carry
        lax.fori_loop(0, (high - low) // 3, body, 0)

    def turn(f, tile_lane=None):
        at = lane if tile_lane is None else tile_lane
        return (at - 16 * f + 32 + 128) % 128

    def bring(f, last, begin):
        return jnp.where(turn(f) < 64, pltpu.roll(last, 16 * f, 1), pltpu.roll(begin, 64 + 16 * f, 1))

    def bring_field(base):
        here = pl.ds(base, 8)
        for f in flows:
            end_field[f - 2, here, :] = bring(f, field[f, TILES - 1, here, :], field[f, 0, here, :])

    def bring_rest(e):
        base = at_tile(e)
        here = pl.ds(base, 8)
        bring_field(base)
        for i in range(2):
            flow = 0.05 * end_field[i, here, :]
            end_own[i, i, here, :] = flow
            end_own[1 - i, i, here, :] = pltpu.roll(flow, 112 if i else 16, 1)
        for src, to in ((wide_k, end_k), (wide_b, end_b)):
            tile = bring(2, src[TILES - 1, here, :], src[0, here, :])
            to[0, here, :] = tile
            to[1, here, :] = pltpu.roll(tile, 16, 1)

    by_three(2, end, lambda e: mask(e, flows))
    by_three(2, end, lambda e: first(at_tile(e), inside, flows, TILES))
    by_three(3, end - 2, lambda e: second(e, inside, flows, TILES))
    second(end - 2, inside, flows, TILES)
    by_three(2, end, bring_rest)
    for half in range(2):
        width = span if half == 0 else LANES - span
        pieces = halves(un[:, span * half:span * half + width]) + halves(vn[:, span * half:span * half + width])
        means = jnp.dot(jnp.concatenate(pieces, axis=0), pick[0:width, :], preferred_element_type=f32)
        for i in range(2):
            mean[i, half] = means[256 * i:256 * i + ROWS] + means[256 * i + 128:256 * i + 128 + ROWS]

    near.finish(wires)

    @pl.when(near.x == 0)
    def _():
        rs[:, 8:16, :] = jnp.zeros((RING + 2, 8, 128), f32)
        rw[0:8, :] = jnp.zeros((8, 128), f32)
        re[0:8, :] = jnp.zeros((8, 128), f32)

    @pl.when(near.top)
    def _():
        sign = jnp.where(sub < 4, 1.0, -1.0)
        tiles = [rn[TILES - 1 - k, 8:16, :] for k in inside]
        for k in inside:
            rn[k, 8:16, :] = sign * row_xor(pick_lanes(tiles[k], lane + 120 - 16 * (lane // 8)), 1)
        rn[TILES, 8:16, :] = pick_lanes(rn[TILES, 8:16, :], lane + 96 - 64 * (lane // 32))
        start = turn_rows(pick_lanes(rn[RING + 1, 8:16, :], (239 - lane) % 128))
        last = turn_rows(pick_lanes(rn[RING, 8:16, :], (239 - lane) % 128))
        rn[RING, 8:16, :] = jnp.where(lane < 112, start, last)
        rn[RING + 1, 8:16, :] = jnp.where(lane < 112, last, start)
        swap = lane + 8 - 16 * ((lane // 8) % 2)
        index = jnp.where(
            lane < 8, 71 - lane, jnp.where(jnp.logical_and(lane >= 48, lane < 112), swap - 48, 100))
        tile = turn_rows(pick_lanes(rw[ROWS + 8:ROWS + 16, :], index))
        rw[ROWS + 8:ROWS + 16, :] = jnp.where(jnp.logical_and(lane >= 80, lane < 112), -tile, tile)
        index = jnp.where(lane < 64, swap + 48, jnp.where(lane < 72, 71 - lane, 20))
        tile = turn_rows(pick_lanes(re[ROWS + 8:ROWS + 16, :], index))
        re[ROWS + 8:ROWS + 16, :] = jnp.where(jnp.logical_and(lane >= 32, lane < 64), -tile, tile)

    halo_flags = []
    for got, base in ((rs, PAD - 8), (rn, PAD + ROWS)):
        tail = got[TILES, 8:16, :]
        flag = [jnp.broadcast_to(tail[:, 32 * j:32 * j + 1], (8, 128)) for j in range(4)]
        halo_flags.append(flag)
        for k in inside:
            low, high = (128 * k) // (BLOCK * LEVELS), (128 * k + 127) // (BLOCK * LEVELS)
            value = flag[low]
            if low != high:
                value = jnp.where(lane < BLOCK * LEVELS * high - 128 * k, value, flag[high])
            wet[k, base:base + 8, :] = value

    def halo_rows(which):
        for f in which:
            for k in inside:
                field[f, k, PAD - 8:PAD, :] = rs[k, 2 * f + 2:2 * f + 10, :]
                field[f, k, PAD + ROWS:PAD + ROWS + 8, :] = rn[k, 2 * f + 8:2 * f + 16, :]

    halo_rows(flows)

    for e in (1, end):
        bring_field(8 * e)
    for e in range(1, end + 1):
        here, rows = slice(8 * e, 8 * e + 8), slice(8 * e - 8, 8 * e)
        east, west = re[rows, :], rw[rows, :]
        wet_east = jnp.broadcast_to(east[:, 100:101], (8, 128))
        wet_west = jnp.broadcast_to(west[:, 20:21], (8, 128))
        last, begin = wet[TILES - 1, here, :], wet[0, here, :]
        for f in flows:
            at = turn(f)
            end_wet[f - 2, here, :] = jnp.where(
                at < 64, jnp.where(at < 32, last, wet_east), jnp.where(at < 96, wet_west, begin))
            end_side[f - 2, here, :] = jnp.where(
                at < 64, last + jnp.where(at < 24, last, wet_east), begin + jnp.where(at < 104, wet_west, begin))
            end_field[f - 2, here, :] = jnp.where(
                at // 16 == 2, east, jnp.where(at // 16 == 5, west, end_field[f - 2, here, :]))
    for base in range(PAD - 1, PAD + ROWS + 1, 8):
        here, above, below = slice(base, base + 8), slice(base + 1, base + 9), slice(base - 1, base + 7)
        for i in range(2):
            w = end_wet[i, here, :]
            total = w * (end_side[i, here, :] + (end_wet[i, above, :] + end_wet[i, below, :]))
            c, fn, fs = end_field[i, here, :], end_field[i, above, :], end_field[i, below, :]
            fe, fw = pltpu.roll(c, 128 - LEVELS, 1), pltpu.roll(c, LEVELS, 1)
            lap = w * ((fe + fw) + (fn + fs)) - total * c
            end_once[i, here, :] = lap
            end_part[i, here, :] = (
                c - (end_own[i, 0, here, :] * (fe - fw) + end_own[i, 1, here, :] * (fn - fs))
            ) + (end_k[i, here, :] + end_b[i, here, :] * total) * lap
    for e in range(2, end):
        here = slice(8 * e, 8 * e + 8)
        for i in range(2):
            lap = end_once[i, here, :]
            total = (pltpu.roll(lap, 128 - LEVELS, 1) + pltpu.roll(lap, LEVELS, 1)) + (
                end_once[i, 8 * e + 1:8 * e + 9, :] + end_once[i, 8 * e - 1:8 * e + 7, :])
            end_new[i, 8 * e - PAD:8 * e - PAD + 8, :] = (
                end_part[i, here, :] - end_b[i, here, :] * end_wet[i, here, :] * total)

    for base in (PAD - 4, PAD + ROWS - 4):
        weigh(base, inside, (base,), TILES)
        first(base, inside, flows, TILES)
    for e in (2, end - 1):
        second(e, inside, flows, TILES)

    for half in range(2):
        width = span if half == 0 else LANES - span
        at = slice(span * half, span * half + width)
        pieces = []
        for new in (un, vn):
            pieces += halves(jnp.concatenate([new[0:8, at], new[ROWS - 8:ROWS, at]], axis=0))
        means = jnp.dot(jnp.concatenate(pieces, axis=0), pick[0:width, :], preferred_element_type=f32)
        for i in range(2):
            value = means[32 * i:32 * i + 16] + means[32 * i + 16:32 * i + 32]
            mean[i, half, 0:8, :] = value[0:8]
            mean[i, half, ROWS - 8:ROWS, :] = value[8:16]
    from_lane = lax.broadcasted_iota(jnp.int32, (128, 256), 0)
    to_lane = lax.broadcasted_iota(jnp.int32, (128, 256), 1)
    for i in range(2):
        cell = turn(i + 2, from_lane) // LEVELS
        hit = jnp.logical_or(
            jnp.logical_and(cell - 12 == to_lane, to_lane < 2),
            jnp.logical_and(cell - 2 == to_lane - (COLS - 2), to_lane >= COLS - 2))
        hit = jnp.logical_and(hit, to_lane < COLS)
        matrix = jnp.where(hit, 1.0 / LEVELS, 0.0).astype(bf16)
        means = jnp.dot(
            jnp.concatenate(halves(end_new[i]), axis=0), matrix, preferred_element_type=f32)
        value = means[0:ROWS] + means[128:128 + ROWS]
        mean[i, 0] = jnp.where(lane_c < 2, value[:, 0:128], mean[i, 0])
        mean[i, 1] = jnp.where(lane_c // 2 == (COLS - 2 - 128) // 2, value[:, 128:256], mean[i, 1])
        for half in range(2):
            plane[i, half, own, :] = base_plane[i, half] + mean[i, half]

    for pack, side, shift in ((wpack2, 0, 0), (epack2, 1, 24)):
        for r in range(2):
            packed = jnp.zeros((8, 128), f32)
            for g in range(8 - r):
                rows = slice(PAD + 16 * g + 8 * r, PAD + 16 * g + 8 * r + 8)
                for p in range(2):
                    turned = pltpu.roll(plane[p, side, rows, :], (16 * g + 8 * p + shift) % 128, 1)
                    packed = jnp.where(lane // 8 == 2 * g + p, turned, packed)
            pack[8 * r:8 * r + 8, :] = packed

    def three2(ref):
        return ref, ref.at[pl.ds(0, 8)], ref.at[pl.ds(0, 8)]

    def spots2(ref):
        return ref.at[pl.ds(0, 16)], ref.at[pl.ds(16, 8)], ref.at[pl.ds(24, 8)]

    north = plane.at[pl.ds(0, 2), :, pl.ds(PAD + ROWS - 8, 8), :]
    south = plane.at[pl.ds(0, 2), :, pl.ds(PAD, 8), :]
    east, west, from_west, from_east = three2(epack2), three2(wpack2), spots2(rw2), spots2(re2)
    wires2 = near.wire(north, south, east, west, rn2, rs2, from_west, from_east, send2, recv2)
    near.start(wires2, east, west, from_west, from_east)

    for e in range(2, end):
        rows = slice(8 * e - PAD, 8 * e - PAD + 8)
        for i in range(2):
            tile, new, f = end_new[i, rows, :], (un, vn)[i], i + 2
            begin = pltpu.roll(tile, (64 - 16 * f) % 128, 1)
            last = pltpu.roll(tile, 128 - 16 * f, 1)
            new[rows, 0:128] = jnp.where(lane < 16, begin, new[rows, 0:128])
            new[rows, LANES - 128:LANES] = jnp.where(lane >= 112, last, new[rows, LANES - 128:LANES])

    halo_rows(tracers)
    west, east = rw[...], re[...]
    wet_east = jnp.broadcast_to(east[:, 100:101], (ROWS + 16, 128))
    wet_west = jnp.broadcast_to(west[:, 20:21], (ROWS + 16, 128))
    wet[TILES, ends, :] = jnp.where(lane_h < 64, wet_east, wet_west)
    for f in tracers:
        right = pltpu.roll(east, 128 - 16 * f, 1) if f else east
        field[f, TILES, ends, :] = jnp.where(lane_h < 64, right, pltpu.roll(west, 64 - 16 * f, 1))
    for e in (1, 2, end - 1, end):
        weigh(8 * e, everywhere, (8 * e,))
    weigh(8 * 3, rim, [8 * e for e in early[1:]])
    weigh(8 * middle, rim, (8 * middle,))
    weigh(8 * (middle + 1), rim, [8 * e for e in late[:-1]])
    by_three(2, end, lambda e: mask(e, tracers))
    for e in (1, end):
        first(8 * e, everywhere, tracers, RING, whole=False)
    by_three(2, end, lambda e: first(at_tile(e), everywhere, tracers, RING))
    by_three(2, end, lambda e: second(e, inside, tracers, RING))

    for (got, flag), at in zip(((rs, halo_flags[0]), (rn, halo_flags[1])), (PAD - 8, PAD + ROWS)):
        for half in range(2):
            plane[2, half, at:at + 8, :] = got[RING + half, 8:16, :]
        plane[3, 0, at:at + 8, :] = jnp.where(
            lane < BLOCK, flag[0], jnp.where(lane < 2 * BLOCK, flag[1], flag[2]))
        plane[3, 1, at:at + 8, :] = jnp.where(lane < 3 * BLOCK - 128, flag[2], flag[3])
    for p, beyond in (
        (2, jnp.where(lane_h < 120, pltpu.roll(east, 48, 1), pltpu.roll(west, 120, 1))),
        (3, jnp.where(lane_h < 120, wet_east, wet_west)),
    ):
        plane[p, 1, ends, :] = jnp.where(lane_h < 112, plane[p, 1, ends, :], beyond)

    near.finish(wires2)

    @pl.when(near.x == 0)
    def _():
        rs2[...] = jnp.zeros(rs2.shape, f32)
        rw2[16:24, :] = jnp.zeros((8, 128), f32)
        re2[16:24, :] = jnp.zeros((8, 128), f32)

    @pl.when(near.top)
    def _():
        for p in range(2):
            start = -turn_rows(pick_lanes(rn2[p, 1], (239 - lane) % 128))
            last = -turn_rows(pick_lanes(rn2[p, 0], (239 - lane) % 128))
            rn2[p, 0] = jnp.where(lane < 112, start, last)
            rn2[p, 1] = jnp.where(lane < 112, last, start)
        for got in (rw2, re2):
            got[24:32, :] = -turn_rows(pick_lanes(got[24:32, :], 112 + (lane // 8 % 2) * 8 + 7 - lane % 8))

    for p in range(2):
        for half in range(2):
            plane[p, half, PAD - 8:PAD, :] = rs2[p, half]
            plane[p, half, PAD + ROWS:PAD + ROWS + 8, :] = rn2[p, half]
    for e in range(1, end + 1):
        here = slice(8 * e, 8 * e + 8)
        g = 7 if e == 1 else 0 if e == end else (e - 2) // 2
        at = 16 if e == 1 else 24 if e == end else 8 * (e % 2)
        for p in range(2):
            beyond = jnp.where(
                lane < 120,
                pltpu.roll(re2[at:at + 8, :], (112 - 16 * g - 8 * p) % 128, 1),
                pltpu.roll(rw2[at:at + 8, :], (120 - 16 * g - 8 * p) % 128, 1))
            plane[p, 1, here, :] = jnp.where(lane < 112, plane[p, 1, here, :], beyond)

    def across(p, e):
        tiles = [plane[p, half, 8 * e:8 * e + 8, :] for half in range(2)]
        left = [pltpu.roll(tile, 127, 1) for tile in tiles]
        right = [pltpu.roll(tile, 1, 1) for tile in tiles]
        return [
            jnp.where(lane < 127, left[half], left[1 - half]) - jnp.where(lane < 1, right[1 - half], right[half])
            for half in range(2)
        ]

    def rows_apart(p, half, e):
        return plane[p, half, 8 * e + 1:8 * e + 9, :] - plane[p, half, 8 * e - 1:8 * e + 7, :]

    for n in range(NSUB):
        for e in range(1, end + 1):
            zonal_slope = across(0, e)
            for half in range(2):
                here = (half, slice(8 * e, 8 * e + 8), slice(None))
                flow = zonal_slope[half] + rows_apart(1, half, e)
                plane[(2,) + here] = plane[(2,) + here] - 0.3 * plane[(3,) + here] * flow
        inner = 1 if n == NSUB - 1 else 0
        for e in range(1 + inner, end + 1 - inner):
            zonal_slope = across(2, e)
            for half in range(2):
                here = (half, slice(8 * e, 8 * e + 8), slice(None))
                w = plane[(3,) + here]
                plane[(0,) + here] = w * (plane[(0,) + here] - 0.3 * zonal_slope[half])
                plane[(1,) + here] = w * (plane[(1,) + here] - 0.3 * rows_apart(2, half, e))
    for half, width in ((0, 128), (1, COLS - 128)):
        at = slice(128 * half, 128 * half + 128)
        du[:, at] = plane[0, half, own, :] - mean[0, half]
        dv[:, at] = plane[1, half, own, :] - mean[1, half]
        at = slice(128 * half, 128 * half + width)
        for p, ref in ((0, zonal), (1, merid), (2, height)):
            ref[:, at] = plane[p, half, own, 0:width]


def finish_kernel(
    tn, sn, un, vn, du, dv, height, zonal, merid,
    t_out, s_out, u_out, v_out, height_out, zonal_out, merid_out, done, sems,
):
    copies = [
        pltpu.make_async_copy(src, dst, sems.at[i])
        for i, (src, dst) in enumerate(
            ((tn, t_out), (sn, s_out), (height, height_out), (zonal, zonal_out), (merid, merid_out)))
    ]
    for copy in copies:
        copy.start()
    step = 24
    for i in range(ROWS // step):
        for f, (new, change, out) in enumerate(((un, du, u_out), (vn, dv, v_out))):
            for r in range(step * i, step * i + step, 8):
                for half in range(2):
                    tile = change[r:r + 8, 128 * half:128 * half + 128]
                    for k in range(8 * half, min(8 * half + 8, TILES)):
                        at = slice(128 * k, 128 * k + 128)
                        done[f, r:r + 8, at] = new[r:r + 8, at] + expand(tile, k % 8)
            rows = pl.ds(step * i, step)
            copies.append(pltpu.make_async_copy(done.at[f, rows, :], out.at[rows, :], sems.at[5 + 2 * i + f]))
            copies[-1].start()
    for copy in copies:
        copy.wait()


def per_device(nb, nw, t, s, u, v, elev, zavg, mavg, flags, sel, ktab, btab):
    f32 = jnp.float32
    vmem = pl.BlockSpec(memory_space=pltpu.VMEM)
    hbm = pl.BlockSpec(memory_space=pl.ANY)
    scratch = lambda *shape: pltpu.VMEM(shape, f32)
    dma = lambda *shape: pltpu.SemaphoreType.DMA(shape)
    parts = pl.pallas_call(
        functools.partial(step_kernel, nb, nw),
        out_shape=(pltpu.VMEM((ROWS, LANES), f32),) * 2
        + (pltpu.VMEM((ROWS + 8, LANES), f32),) * 2
        + (pltpu.VMEM((ROWS, 256), f32),) * 2
        + (pltpu.VMEM((ROWS, COLS), f32),) * 3,
        in_specs=[hbm] * 11,
        out_specs=(vmem,) * 9,
        scratch_shapes=[
            pltpu.SMEM((2, 4), jnp.int32),
            pltpu.SMEM((8,), f32),
            pltpu.SMEM((8,), f32),
            pltpu.VMEM((ROWS, COLS), jnp.int32),
            scratch(ROWS, COLS), scratch(ROWS, COLS), scratch(ROWS, COLS),
            scratch(4, ROWS, LANES),
            scratch(RING + 2, 8, 128), scratch(RING + 2, 8, 128), scratch(ROWS, 128), scratch(ROWS, 128),
            scratch(RING + 2, 24, 128), scratch(RING + 2, 24, 128),
            scratch(ROWS + 16, 128), scratch(ROWS + 16, 128),
            scratch(4, RING, BAND, 128), scratch(4, RING, BAND, 128), scratch(4, TILES, BAND, 128),
            scratch(RING, BAND, 128), scratch(RING, BAND, 128),
            scratch(TILES, BAND, 128), scratch(TILES, BAND, 128),
            pltpu.VMEM((128 * LEVELS, 128), jnp.bfloat16), pltpu.VMEM((256, 128 * LEVELS), jnp.bfloat16),
            scratch(2, 2, ROWS, 128), scratch(2, 2, ROWS, 128),
            scratch(2, BAND, 128), scratch(2, 2, BAND, 128), scratch(2, BAND, 128), scratch(2, BAND, 128),
            scratch(2, BAND, 128), scratch(2, BAND, 128), scratch(2, BAND, 128), scratch(2, BAND, 128),
            scratch(2, 128, 128),
            scratch(4, 2, BAND, 128), scratch(16, 128), scratch(16, 128),
            scratch(2, 2, 8, 128), scratch(2, 2, 8, 128), scratch(32, 128), scratch(32, 128),
            dma(7), dma(4), dma(8), dma(8), dma(8), dma(8),
        ],
        compiler_params=pltpu.CompilerParams(
            collective_id=0, has_side_effects=True, vmem_limit_bytes=VMEM_BYTES),
        name="step",
    )(flags, ktab, btab, sel, t, s, u, v, zavg, mavg, elev)
    parts = [pltpu.with_memory_space_constraint(part, pltpu.VMEM) for part in parts]

    big = jax.ShapeDtypeStruct((ROWS, LANES), f32)
    flat = jax.ShapeDtypeStruct((ROWS, COLS), f32)
    return pl.pallas_call(
        finish_kernel,
        out_shape=(big,) * 4 + (flat,) * 3,
        in_specs=[vmem] * 9,
        out_specs=(hbm,) * 7,
        scratch_shapes=[scratch(2, ROWS, LANES), dma(15)],
        compiler_params=pltpu.CompilerParams(vmem_limit_bytes=VMEM_BYTES),
        name="finish",
    )(*parts)


def solution(mesh):
    grid = P("wide", "blocks")
    return jax.shard_map(
        functools.partial(per_device, mesh.shape["blocks"], mesh.shape["wide"]),
        mesh=mesh,
        in_specs=(grid,) * 9 + (P(), P()),
        out_specs=(grid,) * 7,
        check_vma=False,
    )
```

time: 24.4 us -> 22.2 us (0.910); the launches traced: 24 us -> 22.1 us
  Pallas kernels: 23.4 us -> 21.5 us
    pallas_call x1, Pallas kernels: 21.2 us -> 19.3 us  [per_device(): pl.pallas_call(functools.partial(step_kernel, nb, nw), out_shape=(pltpu.V...]
where the time goes in v3:
time: 22.2 us; the launch traced here: 22.1 us
  Pallas kernels  21.5 us (97%)
  between operations  0.64 us (3%)
    pallas_call x1, Pallas kernels, per_device(): pl.pallas_call(functools.partial(step_kernel, nb, nw), out_shape=(pltpu.V...  19.3 us
    pallas_call x1, Pallas kernels, per_device(): pl.pallas_call(finish_kernel, out_shape=(big,) * 4 + (flat,) * 3, in_spec...  2.16 us

profile of v3, /device:TPU:7, one launch (start us, length us, event | category | flops | bytes accessed | tf_op | source)
XLA Modules:
  0.0 22.1 jit_solution(12901319359180727888)
XLA Ops:
  0.6 19.3 %step.1 = (f32[120,1920]{1,0:T(8,128)S(1)}, f32[120,1920]{1,0:T(8,128)S(1)}, f32[128,1920]{1,0:T(8,128)S(1)}, f32[128,1920]{1,0:T(8,128)S(1)}, f32[120,256]{1,0:...) custom-call(s32[2,4]{1,0:T(2,128)} %flags_in.1, ...), custom_call_target="tpu_custom_call" | custom-call | tf_op jit(solution)/shard_map/step/pallas_call | solution.py:753
  19.9 2.2 %finish.1 = (f32[120,1920]{1,0:T(8,128)}, f32[120,1920]{1,0:T(8,128)}, f32[120,1920]{1,0:T(8,128)}, f32[120,1920]{1,0:T(8,128)}, f32[120,240]{1,0:T(8,128)}, /*index=5*/f32[120,240]{1,0:T(8,128)}, f32[120,240]{1,0:T(8,128)}) custom-call(f32[120,1920]{1,0:T(8,128)S(1)} %get-tuple-element.16.tn, f32[120,1920]{1,0:T(8,128)S(1)} %get-tuple-element.17.sn, ...), custom_call_target="tpu_custom_call" | custom-call | tf_op jit(solution)/shard_map/finish/pallas_call | solution.py:791

commit v4 on v3

--- a/solution.py
+++ b/solution.py
@@ -49,10 +49,11 @@
         b, x = lax.axis_index("blocks"), lax.axis_index("wide")
         self.b, self.x = b, x
         self.top, self.inner, self.above = x == nw - 1, x < nw - 1, x > 0
-        self.east, self.west = lax.rem(b + 1, nb), lax.rem(b + nb - 1, nb)
+        first, last = b == 0, b == nb - 1
+        self.east, self.west = jnp.where(last, 0, b + 1), jnp.where(first, nb - 1, b - 1)
         self.fold = nb - 1 - b
-        self.fold_east = lax.rem(2 * nb - 2 - b, nb)
-        self.fold_west = lax.rem(nb - b, nb)
+        self.fold_east = jnp.where(last, nb - 1, nb - 2 - b)
+        self.fold_west = jnp.where(first, 0, nb - b)
         self.own_east = jnp.logical_and(self.top, self.fold_east == b)
         self.own_west = jnp.logical_and(self.top, self.fold_west == b)
         self.far_east = jnp.logical_and(self.top, self.fold_east != b)
@@ -160,31 +161,46 @@
         def _():
             rw[2][...] = west[1][...]
 
-    def finish(self, wires):
+    def arrived(self, wires):
         w = wires
         for copy in w["always"]:
             copy.wait_recv()
-            copy.wait_send()
         w["top"][0].wait_recv()
 
         @pl.when(self.above)
         def _():
             for copy in w["inner"]:
                 copy.wait_recv()
-            for copy in w["above"]:
+
+        @pl.when(jnp.logical_not(self.own_east))
+        def _():
+            w["far_east"][0].wait_recv()
+
+        @pl.when(jnp.logical_not(self.own_west))
+        def _():
+            w["far_west"][0].wait_recv()
+
+    def sent(self, *every):
+        for w in every:
+            for copy in w["always"]:
                 copy.wait_send()
+            w["top"][0].wait_send()
+
+        @pl.when(self.above)
+        def _():
+            for w in every:
+                for copy in w["above"]:
+                    copy.wait_send()
 
         @pl.when(jnp.logical_not(self.own_east))
         def _():
-            w["far_east"][0].wait_recv()
-            w["far_east"][0].wait_send()
+            for w in every:
+                w["far_east"][0].wait_send()
 
         @pl.when(jnp.logical_not(self.own_west))
         def _():
-            w["far_west"][0].wait_recv()
-            w["far_west"][0].wait_send()
-
-        w["top"][0].wait_send()
+            for w in every:
+                w["far_west"][0].wait_send()
 
 
 def block_row(flags, row, tile):
@@ -213,11 +229,12 @@
     nb, nw, flags_in, ktab_in, btab_in, sel_in, t, s, u, v, zavg_in, mavg_in, elev_in,
     tn, sn, un, vn, du, dv, height, zonal, merid,
     flags, ktab, btab, sel, zavg, mavg, elev,
-    raw, npack, spack, wpack, epack, rn, rs, rw, re,
-    field, once, part, wet, count, wide_k, wide_b, pick, spread_out, mean, base_plane,
-    end_field, end_own, end_k, end_b, end_wet, end_side, end_once, end_part, end_new,
-    plane, wpack2, epack2, rn2, rs2, rw2, re2,
-    small, load, send, recv, send2, recv2,
+    edge_rows, edge_cols, raw, npack, spack, wpack, epack, rn, rs, rw, re,
+    npack_b, spack_b, wpack_b, epack_b, rn_b, rs_b, rw_b, re_b,
+    field, once, part, wet, count, wide_k, wide_b, pick, end_pick, spread_out, mean, base_plane,
+    end_field, end_own, end_k, end_b, end_wet, end_side, end_once, end_part, end_new, wet_beyond, shifted,
+    plane, npack2, spack2, wpack2, epack2, rn2, rs2, rw2, re2,
+    small, load, send, recv, send_b, recv_b, send2, recv2,
 ):
     f32, bf16 = jnp.float32, jnp.bfloat16
     sources = (t, s, u, v)
@@ -232,9 +249,22 @@
              (elev_in, elev), (zavg_in, zavg), (mavg_in, mavg)))
     ]
     loads = [pltpu.make_async_copy(src, raw.at[f], load.at[f]) for f, src in enumerate(sources)]
-    for copy in tables:
+    edges = []
+    for i, src in enumerate((u, v)):
+        for side, at in enumerate((0, ROWS - 8)):
+            edges.append(pltpu.make_async_copy(
+                src.at[pl.ds(at, 8), :], edge_rows.at[i, side], small.at[7 + 4 * i + side]))
+        for side, at in enumerate((0, LANES - 128)):
+            edges.append(pltpu.make_async_copy(
+                src.at[:, pl.ds(at, 128)], edge_cols.at[i, side], small.at[9 + 4 * i + side]))
+    tables[0].start()
+    for copy in edges:
         copy.start()
-    for copy in loads:
+    for copy in tables[1:4]:
+        copy.start()
+    for f in (2, 3, 0, 1):
+        loads[f].start()
+    for copy in tables[4:]:
         copy.start()
 
     lane, sub = lanes_of(), rows_of()
@@ -253,6 +283,15 @@
     pick[...] = jnp.where(
         lax.broadcasted_iota(jnp.int32, (span, 128), 0) // LEVELS
         == lax.broadcasted_iota(jnp.int32, (span, 128), 1), 1.0 / LEVELS, 0.0).astype(bf16)
+    from_lane = lax.broadcasted_iota(jnp.int32, (128, 256), 0)
+    to_lane = lax.broadcasted_iota(jnp.int32, (128, 256), 1)
+    for i in range(2):
+        cell = (from_lane - 16 * (i + 2) + 32 + 128) % 128 // LEVELS
+        hit = jnp.logical_or(
+            jnp.logical_and(cell - 12 == to_lane, to_lane < 2),
+            jnp.logical_and(cell - 2 == to_lane - (COLS - 2), to_lane >= COLS - 2))
+        hit = jnp.logical_and(hit, to_lane < COLS)
+        end_pick[i] = jnp.where(hit, 1.0 / LEVELS, 0.0).astype(bf16)
     spread_out[...] = jnp.where(
         lax.broadcasted_iota(jnp.int32, (256, span), 0) % 128
         == lax.broadcasted_iota(jnp.int32, (256, span), 1) // LEVELS, 1.0, 0.0).astype(bf16)
@@ -260,6 +299,7 @@
     tables[0].wait()
     lows = [block_row(flags, 0, k) for k in inside]
     highs = [block_row(flags, 1, k) for k in inside]
+
 
     def beside(tiles, k):
         left = pltpu.roll(tiles[k], 128 - LEVELS, 1)
@@ -285,7 +325,85 @@
         count[k, 8 * middle:8 * middle + 8, :] = mixed * (
             jnp.where(sub < split, side_low, side_high) + (north + south))
 
-    for copy in tables[1:]:
+
+    def pack_rows(packs, both, last):
+        tiles = [[], []]
+        for m in range(RING // 2):
+            for side in range(2):
+                packed = last[side]
+                for k in (2 * m, 2 * m + 1):
+                    if k >= TILES:
+                        continue
+                    for i in range(2):
+                        row = 4 * (k % 2) + 2 * i
+                        tile = both(i, side, k)
+                        shift = (row + 2 * side) % 8
+                        packed = jnp.where(sub // 2 == row // 2, pltpu.roll(tile, shift, 0) if shift else tile, packed)
+                w = (lows, highs)[side]
+                upper = w[2 * m + 1] if 2 * m + 1 < TILES else jnp.ones((8, 128), f32)
+                packs[side][m] = packed * jnp.where(sub < 4, w[2 * m], upper)
+
+    for copy in edges:
+        copy.wait()
+    tails = []
+    for row in range(2):
+        tail = jnp.zeros((8, 128), f32)
+        for j in range(4):
+            tail = jnp.where(lane // 32 == j, flags[row, j].astype(f32), tail)
+        tails.append(tail)
+    pack_rows((spack, npack), lambda i, side, k: edge_rows[i, side, :, 128 * k:128 * k + 128], tails)
+    lane_a, row_a = lanes_of((64, 128)), rows_of((64, 128))
+    lane_b = lanes_of((ROWS - 64, 128))
+    for side, pack, to in ((0, wpack, 32), (1, epack, 80)):
+        col = 3 * side
+        w_a = jnp.where(row_a < BLOCK, flags[0, col].astype(f32), flags[1, col].astype(f32))
+        w_b = jnp.full((ROWS - 64, 128), flags[1, col].astype(f32))
+        parts_of = []
+        for rows, at, lanes_in, w in ((slice(0, 64), to, lane_a, w_a), (slice(64, ROWS), (to + 64) % 128, lane_b, w_b)):
+            packed = jnp.ones(w.shape, f32)
+            for i in range(2):
+                shift = (at + 16 * i - 112 * side) % 128
+                packed = jnp.where(
+                    lanes_in // 16 == at // 16 + i, pltpu.roll(edge_cols[i, side, rows, :], shift, 1), packed)
+            parts_of.append(packed * w)
+        at = (to + 64) % 128 // 16
+        theirs = jnp.logical_or(lane_b // 8 == 1, jnp.logical_or(lane_b // 16 == at, lane_b // 16 == at + 1))
+        pack[0:ROWS - 64, :] = jnp.where(theirs, parts_of[1], parts_of[0][0:ROWS - 64])
+        pack[ROWS - 64:64, :] = parts_of[0][ROWS - 64:64]
+
+    for copy in tables[1:4]:
+        copy.wait()
+    for half, width in ((0, 128), (1, COLS - 128)):
+        index = sel[:, 128 * half:128 * half + width]
+        if width < 128:
+            index = jnp.concatenate([index, jnp.zeros((ROWS, 128 - width), jnp.int32)], axis=1)
+        kappa = jnp.full(index.shape, ktab[0])
+        bihar = jnp.full(index.shape, btab[0])
+        for n in range(1, 8):
+            hit = index == n
+            kappa = jnp.where(hit, ktab[n], kappa)
+            bihar = jnp.where(hit, btab[n], bihar)
+        for table, to in ((kappa, wide_k), (bihar, wide_b)):
+            wide = jnp.dot(
+                jnp.concatenate(halves(table), axis=1), spread_out[...], preferred_element_type=f32)
+            for k in range(8 * half, min(8 * half + 8, TILES)):
+                to[k, own, :] = wide[:, 128 * (k % 8):128 * (k % 8) + 128]
+
+    near.meet()
+    into = pl.ds(8, 8)
+
+    def three(ref):
+        return ref, ref.at[pl.ds(ROWS - 8 - 64, 8)], ref.at[pl.ds(0, 8)]
+
+    def spots(ref):
+        return ref.at[pl.ds(0, 64)], ref.at[pl.ds(64, 8)], ref.at[pl.ds(72, 8)]
+
+    east, west, from_west, from_east = three(epack), three(wpack), spots(rw), spots(re)
+    wires = near.wire(
+        npack, spack, east, west, rn.at[:, into, :], rs.at[:, into, :], from_west, from_east, send, recv)
+    near.start(wires, east, west, from_west, from_east)
+
+    for copy in tables[4:]:
         copy.wait()
     for half, width in ((0, 128), (1, COLS - 128)):
         w = jnp.zeros((ROWS, 128), f32)
@@ -302,44 +420,17 @@
         base_plane[0, half, :, 0:width] = w[:, 0:width] * zavg[:, at]
         base_plane[1, half, :, 0:width] = w[:, 0:width] * mavg[:, at]
 
-    for half, width in ((0, 128), (1, COLS - 128)):
-        index = sel[:, 128 * half:128 * half + width]
-        if width < 128:
-            index = jnp.concatenate([index, jnp.zeros((ROWS, 128 - width), jnp.int32)], axis=1)
-        kappa = jnp.full(index.shape, ktab[0])
-        bihar = jnp.full(index.shape, btab[0])
-        for n in range(1, 8):
-            hit = index == n
-            kappa = jnp.where(hit, ktab[n], kappa)
-            bihar = jnp.where(hit, btab[n], bihar)
-        for table, to in ((kappa, wide_k), (bihar, wide_b)):
-            wide = jnp.dot(
-                jnp.concatenate(halves(table), axis=1), spread_out[...], preferred_element_type=f32)
-            for k in range(8 * half, min(8 * half + 8, TILES)):
-                to[k, own, :] = wide[:, 128 * (k % 8):128 * (k % 8) + 128]
-
     for copy in loads:
         copy.wait()
-    for k in inside:
-        at = slice(128 * k, 128 * k + 128)
-        south, north = jnp.zeros((8, 128), f32), jnp.zeros((8, 128), f32)
-        for f in range(4):
-            below, above = raw[f, 0:8, at], raw[f, ROWS - 8:ROWS, at]
-            south = jnp.where(sub // 2 == f, pltpu.roll(below, 2 * f, 0) if f else below, south)
-            north = jnp.where(sub // 2 == f, pltpu.roll(above, 2 * f + 2, 0) if f < 3 else above, north)
-        spack[k] = south * wet[k, PAD:PAD + 8, :]
-        npack[k] = north * wet[k, PAD + ROWS - 8:PAD + ROWS, :]
-    for row, pack, at in ((0, spack, PAD), (1, npack, PAD + ROWS - 8)):
-        tail = jnp.zeros((8, 128), f32)
-        for j in range(4):
-            tail = jnp.where(lane // 32 == j, flags[row, j].astype(f32), tail)
-        pack[TILES] = tail
+    pack_rows((spack_b, npack_b), lambda i, side, k: raw[i, (ROWS - 8) * side:(ROWS - 8) * side + 8, 128 * k:128 * k + 128],
+              [jnp.zeros((8, 128), f32)] * 2)
+    for pack, at in ((spack_b, PAD), (npack_b, PAD + ROWS - 8)):
         for half in range(2):
-            pack[RING + half] = plane[2, half, at:at + 8, :]
-    for side, pack in ((0, wpack), (1, epack)):
+            pack[RING // 2 + half] = plane[2, half, at:at + 8, :]
+    for side, pack in ((0, wpack_b), (1, epack_b)):
         w = wet[(TILES - 1) * side, own, :]
-        packed = jnp.ones((ROWS, 128), f32)
-        for f in range(4):
+        packed = jnp.zeros((ROWS, 128), f32)
+        for f in range(2):
             shift = (16 * f + 64 * side) % 128
             tile = raw[f, :, (LANES - 128) * side:(LANES - 128) * side + 128]
             place = lane_c // 16 == f + 3 * side
@@ -347,19 +438,17 @@
         packed = packed * w
         top = pltpu.roll(plane[2, side, own, :], 24 if side else 64, 1)
         pack[...] = jnp.where(lane_c // 8 == (0 if side else 8), top, packed)
-    near.meet()
-    into = pl.ds(8, 8)
-
-    def three(ref):
+
+    def three_b(ref):
         return ref, ref.at[pl.ds(ROWS - 8, 8)], ref.at[pl.ds(0, 8)]
 
-    def spots(ref):
+    def spots_b(ref):
         return ref.at[pl.ds(8, ROWS)], ref.at[pl.ds(0, 8)], ref.at[pl.ds(ROWS + 8, 8)]
 
-    east, west, from_west, from_east = three(epack), three(wpack), spots(rw), spots(re)
-    wires = near.wire(
-        npack, spack, east, west, rn.at[:, into, :], rs.at[:, into, :], from_west, from_east, send, recv)
-    near.start(wires, east, west, from_west, from_east)
+    east, west, from_west, from_east = three_b(epack_b), three_b(wpack_b), spots_b(rw_b), spots_b(re_b)
+    wires_b = near.wire(
+        npack_b, spack_b, east, west, rn_b.at[:, into, :], rs_b.at[:, into, :], from_west, from_east, send_b, recv_b)
+    near.start(wires_b, east, west, from_west, from_east)
 
     def around(ref, turned, key, k, base, ring_size):
         here, above, below = pl.ds(base, 8), pl.ds(base + 1, 8), pl.ds(base - 1, 8)
@@ -455,11 +544,16 @@
             to[0, here, :] = tile
             to[1, here, :] = pltpu.roll(tile, 16, 1)
 
-    by_three(2, end, lambda e: mask(e, flows))
+    for f in flows:
+        for k in inside:
+            for ref in (field, once):
+                ref[f, k, PAD - 8:PAD, :] = jnp.zeros((8, 128), f32)
+                ref[f, k, PAD + ROWS:PAD + ROWS + 8, :] = jnp.zeros((8, 128), f32)
+    by_three(2, end, lambda e: mask(e, (0, 1, 2, 3)))
     by_three(2, end, lambda e: first(at_tile(e), inside, flows, TILES))
-    by_three(3, end - 2, lambda e: second(e, inside, flows, TILES))
-    second(end - 2, inside, flows, TILES)
-    by_three(2, end, bring_rest)
+    by_three(2, end, lambda e: second(e, inside, flows, TILES))
+    for e in range(2, end):
+        bring_rest(e)
     for half in range(2):
         width = span if half == 0 else LANES - span
         pieces = halves(un[:, span * half:span * half + width]) + halves(vn[:, span * half:span * half + width])
@@ -467,38 +561,35 @@
         for i in range(2):
             mean[i, half] = means[256 * i:256 * i + ROWS] + means[256 * i + 128:256 * i + 128 + ROWS]
 
-    near.finish(wires)
+    near.arrived(wires)
 
     @pl.when(near.x == 0)
     def _():
-        rs[:, 8:16, :] = jnp.zeros((RING + 2, 8, 128), f32)
-        rw[0:8, :] = jnp.zeros((8, 128), f32)
-        re[0:8, :] = jnp.zeros((8, 128), f32)
+        rs[:, 8:16, :] = jnp.zeros((RING // 2, 8, 128), f32)
+        rw[64:72, :] = jnp.zeros((8, 128), f32)
+        re[64:72, :] = jnp.zeros((8, 128), f32)
+
+    swap = lane + 8 - 16 * ((lane // 8) % 2)
+
+    def mirror_rows(ref, sign):
+        turned = [sign * row_xor(pick_lanes(ref[m, 8:16, :], lane + 120 - 16 * (lane // 8)), 1) for m in range(RING // 2)]
+        tail = pick_lanes(ref[RING // 2 - 1, 8:16, :], lane + 96 - 64 * (lane // 32))
+        for m in range(RING // 2):
+            lower = turned[RING // 2 - 1 - m]
+            upper = turned[RING // 2 - 2 - m] if m < RING // 2 - 1 else tail
+            ref[m, 8:16, :] = jnp.where(sub < 4, lower, upper)
 
     @pl.when(near.top)
     def _():
-        sign = jnp.where(sub < 4, 1.0, -1.0)
-        tiles = [rn[TILES - 1 - k, 8:16, :] for k in inside]
-        for k in inside:
-            rn[k, 8:16, :] = sign * row_xor(pick_lanes(tiles[k], lane + 120 - 16 * (lane // 8)), 1)
-        rn[TILES, 8:16, :] = pick_lanes(rn[TILES, 8:16, :], lane + 96 - 64 * (lane // 32))
-        start = turn_rows(pick_lanes(rn[RING + 1, 8:16, :], (239 - lane) % 128))
-        last = turn_rows(pick_lanes(rn[RING, 8:16, :], (239 - lane) % 128))
-        rn[RING, 8:16, :] = jnp.where(lane < 112, start, last)
-        rn[RING + 1, 8:16, :] = jnp.where(lane < 112, last, start)
-        swap = lane + 8 - 16 * ((lane // 8) % 2)
-        index = jnp.where(
-            lane < 8, 71 - lane, jnp.where(jnp.logical_and(lane >= 48, lane < 112), swap - 48, 100))
-        tile = turn_rows(pick_lanes(rw[ROWS + 8:ROWS + 16, :], index))
-        rw[ROWS + 8:ROWS + 16, :] = jnp.where(jnp.logical_and(lane >= 80, lane < 112), -tile, tile)
-        index = jnp.where(lane < 64, swap + 48, jnp.where(lane < 72, 71 - lane, 20))
-        tile = turn_rows(pick_lanes(re[ROWS + 8:ROWS + 16, :], index))
-        re[ROWS + 8:ROWS + 16, :] = jnp.where(jnp.logical_and(lane >= 32, lane < 64), -tile, tile)
+        mirror_rows(rn, -1.0)
+        for got, low, off in ((rw, 80, 16), (re, 32, -16)):
+            index = jnp.where(jnp.logical_and(lane >= low, lane < low + 32), swap + off, 8)
+            tile = turn_rows(pick_lanes(got[72:80, :], index))
+            got[72:80, :] = jnp.where(lane < 16, tile, -tile)
 
     halo_flags = []
     for got, base in ((rs, PAD - 8), (rn, PAD + ROWS)):
-        tail = got[TILES, 8:16, :]
-        flag = [jnp.broadcast_to(tail[:, 32 * j:32 * j + 1], (8, 128)) for j in range(4)]
+        flag = [jnp.broadcast_to(got[RING // 2 - 1, 12:13, 32 * j:32 * j + 1], (8, 128)) for j in range(4)]
         halo_flags.append(flag)
         for k in inside:
             low, high = (128 * k) // (BLOCK * LEVELS), (128 * k + 127) // (BLOCK * LEVELS)
@@ -507,21 +598,28 @@
                 value = jnp.where(lane < BLOCK * LEVELS * high - 128 * k, value, flag[high])
             wet[k, base:base + 8, :] = value
 
-    def halo_rows(which):
-        for f in which:
+    def halo_rows(which, south, north):
+        for i, f in enumerate(which):
             for k in inside:
-                field[f, k, PAD - 8:PAD, :] = rs[k, 2 * f + 2:2 * f + 10, :]
-                field[f, k, PAD + ROWS:PAD + ROWS + 8, :] = rn[k, 2 * f + 8:2 * f + 16, :]
-
-    halo_rows(flows)
+                row = 8 + 4 * (k % 2) + 2 * i
+                field[f, k, PAD - 8:PAD, :] = south[k // 2, row - 6:row + 2, :]
+                field[f, k, PAD + ROWS:PAD + ROWS + 8, :] = north[k // 2, row:row + 8, :]
+
+    halo_rows(flows, rs, rn)
 
     for e in (1, end):
         bring_field(8 * e)
     for e in range(1, end + 1):
-        here, rows = slice(8 * e, 8 * e + 8), slice(8 * e - 8, 8 * e)
-        east, west = re[rows, :], rw[rows, :]
-        wet_east = jnp.broadcast_to(east[:, 100:101], (8, 128))
-        wet_west = jnp.broadcast_to(west[:, 20:21], (8, 128))
+        here = slice(8 * e, 8 * e + 8)
+        at = 64 if e == 1 else 72 if e == end else 8 * ((e - 2) % 8)
+        east, west = re[at:at + 8, :], rw[at:at + 8, :]
+        further = e == 1 or 10 <= e < end
+        wet_east = jnp.broadcast_to(east[:, 8 * further:8 * further + 1], (8, 128))
+        wet_west = jnp.broadcast_to(west[:, 8 * further:8 * further + 1], (8, 128))
+        wet_beyond[0, here, :] = wet_east
+        wet_beyond[1, here, :] = wet_west
+        if further:
+            east, west = pltpu.roll(east, 64, 1), pltpu.roll(west, 64, 1)
         last, begin = wet[TILES - 1, here, :], wet[0, here, :]
         for f in flows:
             at = turn(f)
@@ -552,11 +650,52 @@
             end_new[i, 8 * e - PAD:8 * e - PAD + 8, :] = (
                 end_part[i, here, :] - end_b[i, here, :] * end_wet[i, here, :] * total)
 
-    for base in (PAD - 4, PAD + ROWS - 4):
-        weigh(base, inside, (base,), TILES)
-        first(base, inside, flows, TILES)
-    for e in (2, end - 1):
-        second(e, inside, flows, TILES)
+    def sides(ref, k, south, north):
+        return jnp.where(sub < 4, ref[k, south:south + 8, :], ref[k, north:north + 8, :])
+
+    def along(tiles, k):
+        if k not in tiles[1]:
+            tile = tiles[0](k)
+            tiles[1][k] = (tile, pltpu.roll(tile, 128 - LEVELS, 1), pltpu.roll(tile, LEVELS, 1))
+        return tiles[1][k]
+
+    def along_row(tiles, k):
+        tile, left, right = along(tiles, k)
+        return (
+            tile,
+            jnp.where(lane < 128 - LEVELS, left, along(tiles, (k + 1) % TILES)[1]),
+            jnp.where(lane < LEVELS, along(tiles, (k - 1) % TILES)[2], right),
+        )
+
+    def put(ref, k, south, north, value):
+        ref[k, south:south + 4, :] = value[0:4]
+        ref[k, north:north + 8, :] = jnp.where(sub < 4, ref[k, north:north + 8, :], value)
+
+    low, high = PAD - 2, PAD + ROWS - 6
+    wets = (lambda k: sides(wet, k, low, high), {})
+    states = [(lambda k, f=f: sides(field.at[f], k, low, high), {}) for f in flows]
+    for k in inside:
+        w, we, ww = along_row(wets, k)
+        total = w * ((we + ww) + (sides(wet, k, low + 1, high + 1) + sides(wet, k, low - 1, high - 1)))
+        mixing = sides(wide_k, k, low, high) + sides(wide_b, k, low, high) * total
+        zonal_own, merid_own = 0.05 * along(states[0], k)[0], 0.05 * along(states[1], k)[0]
+        for i, f in enumerate(flows):
+            c, fe, fw = along_row(states[i], k)
+            fn, fs = sides(field.at[f], k, low + 1, high + 1), sides(field.at[f], k, low - 1, high - 1)
+            lap = w * ((fe + fw) + (fn + fs)) - total * c
+            put(once.at[f], k, low, high, lap)
+            put(part.at[f], k, low, high, (c - (zonal_own * (fe - fw) + merid_own * (fn - fs))) + mixing * lap)
+    low, high = PAD, PAD + ROWS - 8
+    laps = [(lambda k, f=f: sides(once.at[f], k, low, high), {}) for f in flows]
+    for k in inside:
+        at = slice(128 * k, 128 * k + 128)
+        fade = sides(wide_b, k, low, high) * sides(wet, k, low, high)
+        for i, (f, new) in enumerate(zip(flows, (un, vn))):
+            _, le, lw = along_row(laps[i], k)
+            ln, ls = sides(once.at[f], k, low + 1, high + 1), sides(once.at[f], k, low - 1, high - 1)
+            value = sides(part.at[f], k, low, high) - fade * ((le + lw) + (ln + ls))
+            new[0:8, at] = jnp.where(sub < 4, value, new[0:8, at])
+            new[ROWS - 8:ROWS, at] = jnp.where(sub < 4, new[ROWS - 8:ROWS, at], value)
 
     for half in range(2):
         width = span if half == 0 else LANES - span
@@ -569,17 +708,9 @@
             value = means[32 * i:32 * i + 16] + means[32 * i + 16:32 * i + 32]
             mean[i, half, 0:8, :] = value[0:8]
             mean[i, half, ROWS - 8:ROWS, :] = value[8:16]
-    from_lane = lax.broadcasted_iota(jnp.int32, (128, 256), 0)
-    to_lane = lax.broadcasted_iota(jnp.int32, (128, 256), 1)
     for i in range(2):
-        cell = turn(i + 2, from_lane) // LEVELS
-        hit = jnp.logical_or(
-            jnp.logical_and(cell - 12 == to_lane, to_lane < 2),
-            jnp.logical_and(cell - 2 == to_lane - (COLS - 2), to_lane >= COLS - 2))
-        hit = jnp.logical_and(hit, to_lane < COLS)
-        matrix = jnp.where(hit, 1.0 / LEVELS, 0.0).astype(bf16)
         means = jnp.dot(
-            jnp.concatenate(halves(end_new[i]), axis=0), matrix, preferred_element_type=f32)
+            jnp.concatenate(halves(end_new[i]), axis=0), end_pick[i], preferred_element_type=f32)
         value = means[0:ROWS] + means[128:128 + ROWS]
         mean[i, 0] = jnp.where(lane_c < 2, value[:, 0:128], mean[i, 0])
         mean[i, 1] = jnp.where(lane_c // 2 == (COLS - 2 - 128) // 2, value[:, 128:256], mean[i, 1])
@@ -602,10 +733,12 @@
     def spots2(ref):
         return ref.at[pl.ds(0, 16)], ref.at[pl.ds(16, 8)], ref.at[pl.ds(24, 8)]
 
-    north = plane.at[pl.ds(0, 2), :, pl.ds(PAD + ROWS - 8, 8), :]
-    south = plane.at[pl.ds(0, 2), :, pl.ds(PAD, 8), :]
+    for p in range(2):
+        for half in range(2):
+            npack2[p, half] = plane[p, half, PAD + ROWS - 8:PAD + ROWS, :]
+            spack2[p, half] = plane[p, half, PAD:PAD + 8, :]
     east, west, from_west, from_east = three2(epack2), three2(wpack2), spots2(rw2), spots2(re2)
-    wires2 = near.wire(north, south, east, west, rn2, rs2, from_west, from_east, send2, recv2)
+    wires2 = near.wire(npack2, spack2, east, west, rn2, rs2, from_west, from_east, send2, recv2)
     near.start(wires2, east, west, from_west, from_east)
 
     for e in range(2, end):
@@ -617,10 +750,31 @@
             new[rows, 0:128] = jnp.where(lane < 16, begin, new[rows, 0:128])
             new[rows, LANES - 128:LANES] = jnp.where(lane >= 112, last, new[rows, LANES - 128:LANES])
 
-    halo_rows(tracers)
-    west, east = rw[...], re[...]
-    wet_east = jnp.broadcast_to(east[:, 100:101], (ROWS + 16, 128))
-    wet_west = jnp.broadcast_to(west[:, 20:21], (ROWS + 16, 128))
+    near.arrived(wires_b)
+
+    @pl.when(near.x == 0)
+    def _():
+        rs_b[:, 8:16, :] = jnp.zeros((RING // 2 + 2, 8, 128), f32)
+        rw_b[0:8, :] = jnp.zeros((8, 128), f32)
+        re_b[0:8, :] = jnp.zeros((8, 128), f32)
+
+    @pl.when(near.top)
+    def _():
+        mirror_rows(rn_b, 1.0)
+        mirror = (2 * COLS - 241 - lane) % 128
+        start = turn_rows(pick_lanes(rn_b[RING // 2 + 1, 8:16, :], mirror))
+        last = turn_rows(pick_lanes(rn_b[RING // 2, 8:16, :], mirror))
+        rn_b[RING // 2, 8:16, :] = jnp.where(lane < 112, start, last)
+        rn_b[RING // 2 + 1, 8:16, :] = jnp.where(lane < 112, last, start)
+        index = jnp.where(
+            lane < 8, 71 - lane, jnp.where(jnp.logical_and(lane >= 48, lane < 80), swap - 48, 100))
+        rw_b[ROWS + 8:ROWS + 16, :] = turn_rows(pick_lanes(rw_b[ROWS + 8:ROWS + 16, :], index))
+        index = jnp.where(lane < 64, swap + 48, jnp.where(lane < 72, 71 - lane, 20))
+        re_b[ROWS + 8:ROWS + 16, :] = turn_rows(pick_lanes(re_b[ROWS + 8:ROWS + 16, :], index))
+
+    halo_rows(tracers, rs_b, rn_b)
+    west, east = rw_b[...], re_b[...]
+    wet_east, wet_west = wet_beyond[0, ends, :], wet_beyond[1, ends, :]
     wet[TILES, ends, :] = jnp.where(lane_h < 64, wet_east, wet_west)
     for f in tracers:
         right = pltpu.roll(east, 128 - 16 * f, 1) if f else east
@@ -630,15 +784,14 @@
     weigh(8 * 3, rim, [8 * e for e in early[1:]])
     weigh(8 * middle, rim, (8 * middle,))
     weigh(8 * (middle + 1), rim, [8 * e for e in late[:-1]])
-    by_three(2, end, lambda e: mask(e, tracers))
     for e in (1, end):
         first(8 * e, everywhere, tracers, RING, whole=False)
     by_three(2, end, lambda e: first(at_tile(e), everywhere, tracers, RING))
     by_three(2, end, lambda e: second(e, inside, tracers, RING))
 
-    for (got, flag), at in zip(((rs, halo_flags[0]), (rn, halo_flags[1])), (PAD - 8, PAD + ROWS)):
+    for (got, flag), at in zip(((rs_b, halo_flags[0]), (rn_b, halo_flags[1])), (PAD - 8, PAD + ROWS)):
         for half in range(2):
-            plane[2, half, at:at + 8, :] = got[RING + half, 8:16, :]
+            plane[2, half, at:at + 8, :] = got[RING // 2 + half, 8:16, :]
         plane[3, 0, at:at + 8, :] = jnp.where(
             lane < BLOCK, flag[0], jnp.where(lane < 2 * BLOCK, flag[1], flag[2]))
         plane[3, 1, at:at + 8, :] = jnp.where(lane < 3 * BLOCK - 128, flag[2], flag[3])
@@ -648,7 +801,20 @@
     ):
         plane[p, 1, ends, :] = jnp.where(lane_h < 112, plane[p, 1, ends, :], beyond)
 
-    near.finish(wires2)
+    def column_on(tiles):
+        turned = [pltpu.roll(tile, 127, 1) for tile in tiles]
+        return [jnp.where(lane < 127, turned[half], turned[1 - half]) for half in range(2)]
+
+    for e in range(1, end + 1):
+        here = slice(8 * e, 8 * e + 8)
+        for half in range(2):
+            plane[3, half, here, :] = 0.3 * plane[3, half, here, :]
+        for p, to in ((0, 0), (3, 1)):
+            if p or 1 < e < end:
+                for half, tile in enumerate(column_on([plane[p, half, here, :] for half in range(2)])):
+                    shifted[to, half, here, :] = tile
+
+    near.arrived(wires2)
 
     @pl.when(near.x == 0)
     def _():
@@ -666,48 +832,51 @@
         for got in (rw2, re2):
             got[24:32, :] = -turn_rows(pick_lanes(got[24:32, :], 112 + (lane // 8 % 2) * 8 + 7 - lane % 8))
 
-    for p in range(2):
-        for half in range(2):
-            plane[p, half, PAD - 8:PAD, :] = rs2[p, half]
-            plane[p, half, PAD + ROWS:PAD + ROWS + 8, :] = rn2[p, half]
+    for got, at in ((rs2, PAD - 8), (rn2, PAD + ROWS)):
+        for half, tile in enumerate(column_on([got[0, half] for half in range(2)])):
+            shifted[0, half, at:at + 8, :] = tile
+            plane[1, half, at:at + 8, :] = got[1, half]
     for e in range(1, end + 1):
         here = slice(8 * e, 8 * e + 8)
         g = 7 if e == 1 else 0 if e == end else (e - 2) // 2
         at = 16 if e == 1 else 24 if e == end else 8 * (e % 2)
-        for p in range(2):
+        for p, off in ((0, 1), (1, 0)):
             beyond = jnp.where(
-                lane < 120,
-                pltpu.roll(re2[at:at + 8, :], (112 - 16 * g - 8 * p) % 128, 1),
-                pltpu.roll(rw2[at:at + 8, :], (120 - 16 * g - 8 * p) % 128, 1))
-            plane[p, 1, here, :] = jnp.where(lane < 112, plane[p, 1, here, :], beyond)
-
-    def across(p, e):
-        tiles = [plane[p, half, 8 * e:8 * e + 8, :] for half in range(2)]
-        left = [pltpu.roll(tile, 127, 1) for tile in tiles]
-        right = [pltpu.roll(tile, 1, 1) for tile in tiles]
-        return [
-            jnp.where(lane < 127, left[half], left[1 - half]) - jnp.where(lane < 1, right[1 - half], right[half])
-            for half in range(2)
-        ]
+                lane < 120 - off,
+                pltpu.roll(re2[at:at + 8, :], (112 - 16 * g - 8 * p - off) % 128, 1),
+                pltpu.roll(rw2[at:at + 8, :], (120 - 16 * g - 8 * p - off) % 128, 1))
+            ref = plane.at[1, 1] if p else shifted.at[0, 1]
+            theirs = jnp.logical_and(lane >= 112 - off, lane < 128 - off)
+            ref[here, :] = jnp.where(theirs, beyond, ref[here, :])
+
+    def apart(tiles, ahead):
+        turned = [pltpu.roll(tile, 126 if ahead else 2, 1) for tile in tiles]
+        if ahead:
+            return [jnp.where(lane < 126, turned[half], turned[1 - half]) - tiles[half] for half in range(2)]
+        return [tiles[half] - jnp.where(lane < 2, turned[1 - half], turned[half]) for half in range(2)]
 
     def rows_apart(p, half, e):
         return plane[p, half, 8 * e + 1:8 * e + 9, :] - plane[p, half, 8 * e - 1:8 * e + 7, :]
 
     for n in range(NSUB):
         for e in range(1, end + 1):
-            zonal_slope = across(0, e)
+            here = slice(8 * e, 8 * e + 8)
+            slope = apart([shifted[0, half, here, :] for half in range(2)], False)
             for half in range(2):
-                here = (half, slice(8 * e, 8 * e + 8), slice(None))
-                flow = zonal_slope[half] + rows_apart(1, half, e)
-                plane[(2,) + here] = plane[(2,) + here] - 0.3 * plane[(3,) + here] * flow
+                flow = slope[half] + rows_apart(1, half, e)
+                plane[2, half, here, :] = plane[2, half, here, :] - plane[3, half, here, :] * flow
         inner = 1 if n == NSUB - 1 else 0
         for e in range(1 + inner, end + 1 - inner):
-            zonal_slope = across(2, e)
+            here = slice(8 * e, 8 * e + 8)
+            slope = apart([plane[2, half, here, :] for half in range(2)], True)
             for half in range(2):
-                here = (half, slice(8 * e, 8 * e + 8), slice(None))
-                w = plane[(3,) + here]
-                plane[(0,) + here] = w * (plane[(0,) + here] - 0.3 * zonal_slope[half])
-                plane[(1,) + here] = w * (plane[(1,) + here] - 0.3 * rows_apart(2, half, e))
+                shifted[0, half, here, :] = shifted[0, half, here, :] - shifted[1, half, here, :] * slope[half]
+                plane[1, half, here, :] = plane[1, half, here, :] - plane[3, half, here, :] * rows_apart(2, half, e)
+    for e in range(2, end):
+        here = slice(8 * e, 8 * e + 8)
+        turned = [pltpu.roll(shifted[0, half, here, :], 1, 1) for half in range(2)]
+        for half in range(2):
+            plane[0, half, here, :] = jnp.where(lane < 1, turned[1 - half], turned[half])
     for half, width in ((0, 128), (1, COLS - 128)):
         at = slice(128 * half, 128 * half + 128)
         du[:, at] = plane[0, half, own, :] - mean[0, half]
@@ -715,6 +884,7 @@
         at = slice(128 * half, 128 * half + width)
         for p, ref in ((0, zonal), (1, merid), (2, height)):
             ref[:, at] = plane[p, half, own, 0:width]
+    near.sent(wires, wires_b, wires2)
 
 
 def finish_kernel(
@@ -764,21 +934,24 @@
             pltpu.SMEM((8,), f32),
             pltpu.VMEM((ROWS, COLS), jnp.int32),
             scratch(ROWS, COLS), scratch(ROWS, COLS), scratch(ROWS, COLS),
-            scratch(4, ROWS, LANES),
-            scratch(RING + 2, 8, 128), scratch(RING + 2, 8, 128), scratch(ROWS, 128), scratch(ROWS, 128),
-            scratch(RING + 2, 24, 128), scratch(RING + 2, 24, 128),
+            scratch(2, 2, 8, LANES), scratch(2, 2, ROWS, 128), scratch(4, ROWS, LANES),
+            scratch(RING // 2, 8, 128), scratch(RING // 2, 8, 128), scratch(64, 128), scratch(64, 128),
+            scratch(RING // 2, 24, 128), scratch(RING // 2, 24, 128), scratch(80, 128), scratch(80, 128),
+            scratch(RING // 2 + 2, 8, 128), scratch(RING // 2 + 2, 8, 128), scratch(ROWS, 128), scratch(ROWS, 128),
+            scratch(RING // 2 + 2, 24, 128), scratch(RING // 2 + 2, 24, 128),
             scratch(ROWS + 16, 128), scratch(ROWS + 16, 128),
             scratch(4, RING, BAND, 128), scratch(4, RING, BAND, 128), scratch(4, TILES, BAND, 128),
             scratch(RING, BAND, 128), scratch(RING, BAND, 128),
             scratch(TILES, BAND, 128), scratch(TILES, BAND, 128),
-            pltpu.VMEM((128 * LEVELS, 128), jnp.bfloat16), pltpu.VMEM((256, 128 * LEVELS), jnp.bfloat16),
+            pltpu.VMEM((128 * LEVELS, 128), jnp.bfloat16), pltpu.VMEM((2, 128, 256), jnp.bfloat16),
+            pltpu.VMEM((256, 128 * LEVELS), jnp.bfloat16),
             scratch(2, 2, ROWS, 128), scratch(2, 2, ROWS, 128),
             scratch(2, BAND, 128), scratch(2, 2, BAND, 128), scratch(2, BAND, 128), scratch(2, BAND, 128),
             scratch(2, BAND, 128), scratch(2, BAND, 128), scratch(2, BAND, 128), scratch(2, BAND, 128),
-            scratch(2, 128, 128),
-            scratch(4, 2, BAND, 128), scratch(16, 128), scratch(16, 128),
+            scratch(2, 128, 128), scratch(2, BAND, 128), scratch(2, 2, BAND, 128),
+            scratch(4, 2, BAND, 128), scratch(2, 2, 8, 128), scratch(2, 2, 8, 128), scratch(16, 128), scratch(16, 128),
             scratch(2, 2, 8, 128), scratch(2, 2, 8, 128), scratch(32, 128), scratch(32, 128),
-            dma(7), dma(4), dma(8), dma(8), dma(8), dma(8),
+            dma(15), dma(4), dma(8), dma(8), dma(8), dma(8), dma(8), dma(8),
         ],
         compiler_params=pltpu.CompilerParams(
             collective_id=0, has_side_effects=True, vmem_limit_bytes=VMEM_BYTES),

time: 22.2 us -> 21.8 us (0.982)
  Pallas kernels: 21.5 us -> 21.1 us
    pallas_call x1, Pallas kernels: 19.3 us -> 18.9 us  [per_device(): pl.pallas_call(functools.partial(step_kernel, nb, nw), out_shape=(pltpu.V...]
where the time goes in v4:
time: 21.8 us; the launch traced here: 21.7 us
  Pallas kernels  21.1 us (97%)
  between operations  0.64 us (3%)
    pallas_call x1, Pallas kernels, per_device(): pl.pallas_call(functools.partial(step_kernel, nb, nw), out_shape=(pltpu.V...  18.9 us
    pallas_call x1, Pallas kernels, per_device(): pl.pallas_call(finish_kernel, out_shape=(big,) * 4 + (flat,) * 3, in_spec...  2.16 us

profile of v4, /device:TPU:7, one launch (start us, length us, event | category | flops | bytes accessed | tf_op | source)
XLA Modules:
  0.0 21.7 jit_solution(5863462661587361274)
XLA Ops:
  0.6 18.9 %step.1 = (f32[120,1920]{1,0:T(8,128)S(1)}, f32[120,1920]{1,0:T(8,128)S(1)}, f32[128,1920]{1,0:T(8,128)S(1)}, f32[128,1920]{1,0:T(8,128)S(1)}, f32[120,256]{1,0:...) custom-call(s32[2,4]{1,0:T(2,128)} %flags_in.1, ...), custom_call_target="tpu_custom_call" | custom-call | tf_op jit(solution)/shard_map/step/pallas_call | solution.py:923
  19.6 2.2 %finish.1 = (f32[120,1920]{1,0:T(8,128)}, f32[120,1920]{1,0:T(8,128)}, f32[120,1920]{1,0:T(8,128)}, f32[120,1920]{1,0:T(8,128)}, f32[120,240]{1,0:T(8,128)}, /*index=5*/f32[120,240]{1,0:T(8,128)}, f32[120,240]{1,0:T(8,128)}) custom-call(f32[120,1920]{1,0:T(8,128)S(1)} %get-tuple-element.16.tn, f32[120,1920]{1,0:T(8,128)S(1)} %get-tuple-element.17.sn, ...), custom_call_target="tpu_custom_call" | custom-call | tf_op jit(solution)/shard_map/finish/pallas_call | solution.py:964

commit v5 on v4

--- a/solution.py
+++ b/solution.py
@@ -33,15 +33,11 @@
     return jnp.take_along_axis(tile, index, axis=1, mode="promise_in_bounds")
 
 
-def row_xor(tile, bit):
-    keep = (rows_of(tile.shape) // bit) % 2 == 0
-    return jnp.where(keep, pltpu.roll(tile, 8 - bit, 0), pltpu.roll(tile, bit, 0))
-
-
-def turn_rows(tile):
-    for bit in (1, 2, 4):
-        tile = row_xor(tile, bit)
-    return tile
+def turn_rows(rows):
+    turned = jnp.broadcast_to(rows[7:8, :], (8, 128))
+    for i in range(1, 8):
+        turned = jnp.where(rows_of() == i, jnp.broadcast_to(rows[7 - i:8 - i, :], (8, 128)), turned)
+    return turned
 
 
 class Neighbours:
@@ -66,32 +62,39 @@
             pl.semaphore_signal(sem, inc=1, device_id=(b, x), device_id_type=MESH)
 
         b, x = self.b, self.x
+
+        @pl.when(self.far_east)
+        def _():
+            greet(self.fold_east, x)
+
+        @pl.when(self.far_west)
+        def _():
+            greet(self.fold_west, x)
+
+        @pl.when(self.inner)
+        def _():
+            greet(self.east, x + 1)
+            greet(self.west, x + 1)
+
+        @pl.when(self.above)
+        def _():
+            greet(self.east, x - 1)
+            greet(self.west, x - 1)
+
+        @pl.when(self.top)
+        def _():
+            greet(self.fold, x)
+
         greet(self.east, x)
         greet(self.west, x)
 
         @pl.when(self.inner)
         def _():
             greet(b, x + 1)
-            greet(self.east, x + 1)
-            greet(self.west, x + 1)
-
-        @pl.when(self.top)
-        def _():
-            greet(self.fold, x)
-
-        @pl.when(self.far_east)
-        def _():
-            greet(self.fold_east, x)
-
-        @pl.when(self.far_west)
-        def _():
-            greet(self.fold_west, x)
 
         @pl.when(self.above)
         def _():
             greet(b, x - 1)
-            greet(self.east, x - 1)
-            greet(self.west, x - 1)
 
     def meet(self):
         sem = pltpu.get_barrier_semaphore()
@@ -123,16 +126,16 @@
                 c(east[0], rw[0], 0, 0, self.east, x),
                 c(west[0], re[0], 1, 1, self.west, x),
             ],
-            inner=[
+            corner_inner=[
                 c(east[1], rw[1], 4, 4, self.east, x + 1),
                 c(west[1], re[1], 5, 5, self.west, x + 1),
-                c(north, rs, 2, 2, b, x + 1),
             ],
-            above=[
+            corner_above=[
                 c(east[2], rw[2], 6, 6, self.east, x - 1),
                 c(west[2], re[2], 7, 7, self.west, x - 1),
-                c(south, rn, 3, 3, b, x - 1),
             ],
+            inner=[c(north, rs, 2, 2, b, x + 1)],
+            above=[c(south, rn, 3, 3, b, x - 1)],
             top=[c(north, rn, 2, 3, self.fold, x)],
             far_east=[c(east[1], re[2], 4, 7, self.fold_east, x)],
             far_west=[c(west[1], rw[2], 5, 6, self.fold_west, x)],
@@ -145,11 +148,13 @@
                 for copy in wires[name]:
                     copy.start()
 
+        go("far_east", self.far_east)
+        go("far_west", self.far_west)
+        go("corner_inner", self.inner)
+        go("corner_above", self.above)
+        go("top", self.top)
         for copy in wires["always"]:
             copy.start()
-        go("far_east", self.far_east)
-        go("far_west", self.far_west)
-        go("top", self.top)
         go("inner", self.inner)
         go("above", self.above)
 
@@ -169,7 +174,7 @@
 
         @pl.when(self.above)
         def _():
-            for copy in w["inner"]:
+            for copy in w["inner"] + w["corner_inner"]:
                 copy.wait_recv()
 
         @pl.when(jnp.logical_not(self.own_east))
@@ -189,7 +194,7 @@
         @pl.when(self.above)
         def _():
             for w in every:
-                for copy in w["above"]:
+                for copy in w["above"] + w["corner_above"]:
                     copy.wait_send()
 
         @pl.when(jnp.logical_not(self.own_east))
@@ -232,7 +237,7 @@
     edge_rows, edge_cols, raw, npack, spack, wpack, epack, rn, rs, rw, re,
     npack_b, spack_b, wpack_b, epack_b, rn_b, rs_b, rw_b, re_b,
     field, once, part, wet, count, wide_k, wide_b, pick, end_pick, spread_out, mean, base_plane,
-    end_field, end_own, end_k, end_b, end_wet, end_side, end_once, end_part, end_new, wet_beyond, shifted,
+    end_field, end_own, end_k, end_b, end_wet, end_side, end_once, end_part, end_new, wet_beyond, end_halo, shifted,
     plane, npack2, spack2, wpack2, epack2, rn2, rs2, rw2, re2,
     small, load, send, recv, send_b, recv_b, send2, recv2,
 ):
@@ -389,67 +394,6 @@
             for k in range(8 * half, min(8 * half + 8, TILES)):
                 to[k, own, :] = wide[:, 128 * (k % 8):128 * (k % 8) + 128]
 
-    near.meet()
-    into = pl.ds(8, 8)
-
-    def three(ref):
-        return ref, ref.at[pl.ds(ROWS - 8 - 64, 8)], ref.at[pl.ds(0, 8)]
-
-    def spots(ref):
-        return ref.at[pl.ds(0, 64)], ref.at[pl.ds(64, 8)], ref.at[pl.ds(72, 8)]
-
-    east, west, from_west, from_east = three(epack), three(wpack), spots(rw), spots(re)
-    wires = near.wire(
-        npack, spack, east, west, rn.at[:, into, :], rs.at[:, into, :], from_west, from_east, send, recv)
-    near.start(wires, east, west, from_west, from_east)
-
-    for copy in tables[4:]:
-        copy.wait()
-    for half, width in ((0, 128), (1, COLS - 128)):
-        w = jnp.zeros((ROWS, 128), f32)
-        for i in range(2):
-            for j in range(4):
-                here = jnp.logical_and(row_c // BLOCK == i, (lane_c + 128 * half) // BLOCK == j)
-                w = jnp.where(here, flags[i, j].astype(f32), w)
-        plane[3, half, own, :] = w
-        if width < 128:
-            plane[2, half, own, :] = jnp.zeros((ROWS, 128), f32)
-            base_plane[:, half] = jnp.zeros((2, ROWS, 128), f32)
-        at = slice(128 * half, 128 * half + width)
-        plane[2, half, own, 0:width] = w[:, 0:width] * elev[:, at]
-        base_plane[0, half, :, 0:width] = w[:, 0:width] * zavg[:, at]
-        base_plane[1, half, :, 0:width] = w[:, 0:width] * mavg[:, at]
-
-    for copy in loads:
-        copy.wait()
-    pack_rows((spack_b, npack_b), lambda i, side, k: raw[i, (ROWS - 8) * side:(ROWS - 8) * side + 8, 128 * k:128 * k + 128],
-              [jnp.zeros((8, 128), f32)] * 2)
-    for pack, at in ((spack_b, PAD), (npack_b, PAD + ROWS - 8)):
-        for half in range(2):
-            pack[RING // 2 + half] = plane[2, half, at:at + 8, :]
-    for side, pack in ((0, wpack_b), (1, epack_b)):
-        w = wet[(TILES - 1) * side, own, :]
-        packed = jnp.zeros((ROWS, 128), f32)
-        for f in range(2):
-            shift = (16 * f + 64 * side) % 128
-            tile = raw[f, :, (LANES - 128) * side:(LANES - 128) * side + 128]
-            place = lane_c // 16 == f + 3 * side
-            packed = jnp.where(place, pltpu.roll(tile, shift, 1) if shift else tile, packed)
-        packed = packed * w
-        top = pltpu.roll(plane[2, side, own, :], 24 if side else 64, 1)
-        pack[...] = jnp.where(lane_c // 8 == (0 if side else 8), top, packed)
-
-    def three_b(ref):
-        return ref, ref.at[pl.ds(ROWS - 8, 8)], ref.at[pl.ds(0, 8)]
-
-    def spots_b(ref):
-        return ref.at[pl.ds(8, ROWS)], ref.at[pl.ds(0, 8)], ref.at[pl.ds(ROWS + 8, 8)]
-
-    east, west, from_west, from_east = three_b(epack_b), three_b(wpack_b), spots_b(rw_b), spots_b(re_b)
-    wires_b = near.wire(
-        npack_b, spack_b, east, west, rn_b.at[:, into, :], rs_b.at[:, into, :], from_west, from_east, send_b, recv_b)
-    near.start(wires_b, east, west, from_west, from_east)
-
     def around(ref, turned, key, k, base, ring_size):
         here, above, below = pl.ds(base, 8), pl.ds(base + 1, 8), pl.ds(base - 1, 8)
 
@@ -544,14 +488,88 @@
             to[0, here, :] = tile
             to[1, here, :] = pltpu.roll(tile, 16, 1)
 
-    for f in flows:
-        for k in inside:
-            for ref in (field, once):
-                ref[f, k, PAD - 8:PAD, :] = jnp.zeros((8, 128), f32)
-                ref[f, k, PAD + ROWS:PAD + ROWS + 8, :] = jnp.zeros((8, 128), f32)
-    by_three(2, end, lambda e: mask(e, (0, 1, 2, 3)))
-    by_three(2, end, lambda e: first(at_tile(e), inside, flows, TILES))
-    by_three(2, end, lambda e: second(e, inside, flows, TILES))
+    early_start = near.b < 2
+
+    def interior():
+        for f in flows:
+            for k in inside:
+                for ref in (field, once):
+                    ref[f, k, PAD - 8:PAD, :] = jnp.zeros((8, 128), f32)
+                    ref[f, k, PAD + ROWS:PAD + ROWS + 8, :] = jnp.zeros((8, 128), f32)
+        by_three(2, end, lambda e: mask(e, (0, 1, 2, 3)))
+        by_three(2, end, lambda e: first(at_tile(e), inside, flows, TILES))
+        by_three(2, end, lambda e: second(e, inside, flows, TILES))
+
+    def loaded():
+        for copy in loads:
+            copy.wait()
+
+    @pl.when(early_start)
+    def _():
+        loaded()
+        interior()
+
+    near.meet()
+    into = pl.ds(8, 8)
+
+    def three(ref):
+        return ref, ref.at[pl.ds(ROWS - 8 - 64, 8)], ref.at[pl.ds(0, 8)]
+
+    def spots(ref):
+        return ref.at[pl.ds(0, 64)], ref.at[pl.ds(64, 8)], ref.at[pl.ds(72, 8)]
+
+    east, west, from_west, from_east = three(epack), three(wpack), spots(rw), spots(re)
+    wires = near.wire(
+        npack, spack, east, west, rn.at[:, into, :], rs.at[:, into, :], from_west, from_east, send, recv)
+    near.start(wires, east, west, from_west, from_east)
+
+    for copy in tables[4:]:
+        copy.wait()
+    for half, width in ((0, 128), (1, COLS - 128)):
+        w = jnp.zeros((ROWS, 128), f32)
+        for i in range(2):
+            for j in range(4):
+                here = jnp.logical_and(row_c // BLOCK == i, (lane_c + 128 * half) // BLOCK == j)
+                w = jnp.where(here, flags[i, j].astype(f32), w)
+        plane[3, half, own, :] = w
+        if width < 128:
+            plane[2, half, own, :] = jnp.zeros((ROWS, 128), f32)
+            base_plane[:, half] = jnp.zeros((2, ROWS, 128), f32)
+        at = slice(128 * half, 128 * half + width)
+        plane[2, half, own, 0:width] = w[:, 0:width] * elev[:, at]
+        base_plane[0, half, :, 0:width] = w[:, 0:width] * zavg[:, at]
+        base_plane[1, half, :, 0:width] = w[:, 0:width] * mavg[:, at]
+
+    pl.when(jnp.logical_not(early_start))(loaded)
+    pack_rows((spack_b, npack_b), lambda i, side, k: raw[i, (ROWS - 8) * side:(ROWS - 8) * side + 8, 128 * k:128 * k + 128],
+              [jnp.zeros((8, 128), f32)] * 2)
+    for pack, at in ((spack_b, PAD), (npack_b, PAD + ROWS - 8)):
+        for half in range(2):
+            pack[RING // 2 + half] = plane[2, half, at:at + 8, :]
+    for side, pack in ((0, wpack_b), (1, epack_b)):
+        w = wet[(TILES - 1) * side, own, :]
+        packed = jnp.zeros((ROWS, 128), f32)
+        for f in range(2):
+            shift = (16 * f + 64 * side) % 128
+            tile = raw[f, :, (LANES - 128) * side:(LANES - 128) * side + 128]
+            place = lane_c // 16 == f + 3 * side
+            packed = jnp.where(place, pltpu.roll(tile, shift, 1) if shift else tile, packed)
+        packed = packed * w
+        top = pltpu.roll(plane[2, side, own, :], 24 if side else 64, 1)
+        pack[...] = jnp.where(lane_c // 8 == (0 if side else 8), top, packed)
+
+    def three_b(ref):
+        return ref, ref.at[pl.ds(ROWS - 8, 8)], ref.at[pl.ds(0, 8)]
+
+    def spots_b(ref):
+        return ref.at[pl.ds(8, ROWS)], ref.at[pl.ds(0, 8)], ref.at[pl.ds(ROWS + 8, 8)]
+
+    east, west, from_west, from_east = three_b(epack_b), three_b(wpack_b), spots_b(rw_b), spots_b(re_b)
+    wires_b = near.wire(
+        npack_b, spack_b, east, west, rn_b.at[:, into, :], rs_b.at[:, into, :], from_west, from_east, send_b, recv_b)
+    near.start(wires_b, east, west, from_west, from_east)
+
+    pl.when(jnp.logical_not(early_start))(interior)
     for e in range(2, end):
         bring_rest(e)
     for half in range(2):
@@ -572,7 +590,11 @@
     swap = lane + 8 - 16 * ((lane // 8) % 2)
 
     def mirror_rows(ref, sign):
-        turned = [sign * row_xor(pick_lanes(ref[m, 8:16, :], lane + 120 - 16 * (lane // 8)), 1) for m in range(RING // 2)]
+        turned = [
+            sign * pick_lanes(
+                jnp.where(sub % 2 == 0, ref[m, 9:17, :], ref[m, 7:15, :]), lane + 120 - 16 * (lane // 8))
+            for m in range(RING // 2)
+        ]
         tail = pick_lanes(ref[RING // 2 - 1, 8:16, :], lane + 96 - 64 * (lane // 32))
         for m in range(RING // 2):
             lower = turned[RING // 2 - 1 - m]
@@ -584,7 +606,7 @@
         mirror_rows(rn, -1.0)
         for got, low, off in ((rw, 80, 16), (re, 32, -16)):
             index = jnp.where(jnp.logical_and(lane >= low, lane < low + 32), swap + off, 8)
-            tile = turn_rows(pick_lanes(got[72:80, :], index))
+            tile = pick_lanes(turn_rows(got.at[72:80, :]), index)
             got[72:80, :] = jnp.where(lane < 16, tile, -tile)
 
     halo_flags = []
@@ -620,15 +642,22 @@
         wet_beyond[1, here, :] = wet_west
         if further:
             east, west = pltpu.roll(east, 64, 1), pltpu.roll(west, 64, 1)
-        last, begin = wet[TILES - 1, here, :], wet[0, here, :]
-        for f in flows:
-            at = turn(f)
-            end_wet[f - 2, here, :] = jnp.where(
-                at < 64, jnp.where(at < 32, last, wet_east), jnp.where(at < 96, wet_west, begin))
-            end_side[f - 2, here, :] = jnp.where(
-                at < 64, last + jnp.where(at < 24, last, wet_east), begin + jnp.where(at < 104, wet_west, begin))
-            end_field[f - 2, here, :] = jnp.where(
-                at // 16 == 2, east, jnp.where(at // 16 == 5, west, end_field[f - 2, here, :]))
+        end_halo[0, here, :] = east
+        end_halo[1, here, :] = west
+    for i, f in enumerate(flows):
+        at = turn(f)
+        last_side = at < 64
+        outer = jnp.logical_and(at >= 32, at < 96)
+        rim_side = jnp.logical_and(at >= 24, at < 104)
+        beyond = jnp.logical_or(at // 16 == 2, at // 16 == 5)
+        for e in range(1, end + 1):
+            here = slice(8 * e, 8 * e + 8)
+            mine = jnp.where(last_side, wet[TILES - 1, here, :], wet[0, here, :])
+            theirs = jnp.where(last_side, wet_beyond[0, here, :], wet_beyond[1, here, :])
+            end_wet[i, here, :] = jnp.where(outer, theirs, mine)
+            end_side[i, here, :] = mine + jnp.where(rim_side, theirs, mine)
+            halo = jnp.where(last_side, end_halo[0, here, :], end_halo[1, here, :])
+            end_field[i, here, :] = jnp.where(beyond, halo, end_field[i, here, :])
     for base in range(PAD - 1, PAD + ROWS + 1, 8):
         here, above, below = slice(base, base + 8), slice(base + 1, base + 9), slice(base - 1, base + 7)
         for i in range(2):
@@ -762,15 +791,15 @@
     def _():
         mirror_rows(rn_b, 1.0)
         mirror = (2 * COLS - 241 - lane) % 128
-        start = turn_rows(pick_lanes(rn_b[RING // 2 + 1, 8:16, :], mirror))
-        last = turn_rows(pick_lanes(rn_b[RING // 2, 8:16, :], mirror))
+        start = pick_lanes(turn_rows(rn_b.at[RING // 2 + 1, 8:16, :]), mirror)
+        last = pick_lanes(turn_rows(rn_b.at[RING // 2, 8:16, :]), mirror)
         rn_b[RING // 2, 8:16, :] = jnp.where(lane < 112, start, last)
         rn_b[RING // 2 + 1, 8:16, :] = jnp.where(lane < 112, last, start)
         index = jnp.where(
             lane < 8, 71 - lane, jnp.where(jnp.logical_and(lane >= 48, lane < 80), swap - 48, 100))
-        rw_b[ROWS + 8:ROWS + 16, :] = turn_rows(pick_lanes(rw_b[ROWS + 8:ROWS + 16, :], index))
+        rw_b[ROWS + 8:ROWS + 16, :] = pick_lanes(turn_rows(rw_b.at[ROWS + 8:ROWS + 16, :]), index)
         index = jnp.where(lane < 64, swap + 48, jnp.where(lane < 72, 71 - lane, 20))
-        re_b[ROWS + 8:ROWS + 16, :] = turn_rows(pick_lanes(re_b[ROWS + 8:ROWS + 16, :], index))
+        re_b[ROWS + 8:ROWS + 16, :] = pick_lanes(turn_rows(re_b.at[ROWS + 8:ROWS + 16, :]), index)
 
     halo_rows(tracers, rs_b, rn_b)
     west, east = rw_b[...], re_b[...]
@@ -825,12 +854,12 @@
     @pl.when(near.top)
     def _():
         for p in range(2):
-            start = -turn_rows(pick_lanes(rn2[p, 1], (239 - lane) % 128))
-            last = -turn_rows(pick_lanes(rn2[p, 0], (239 - lane) % 128))
+            start = -pick_lanes(turn_rows(rn2.at[p, 1]), (239 - lane) % 128)
+            last = -pick_lanes(turn_rows(rn2.at[p, 0]), (239 - lane) % 128)
             rn2[p, 0] = jnp.where(lane < 112, start, last)
             rn2[p, 1] = jnp.where(lane < 112, last, start)
         for got in (rw2, re2):
-            got[24:32, :] = -turn_rows(pick_lanes(got[24:32, :], 112 + (lane // 8 % 2) * 8 + 7 - lane % 8))
+            got[24:32, :] = -pick_lanes(turn_rows(got.at[24:32, :]), 112 + (lane // 8 % 2) * 8 + 7 - lane % 8)
 
     for got, at in ((rs2, PAD - 8), (rn2, PAD + ROWS)):
         for half, tile in enumerate(column_on([got[0, half] for half in range(2)])):
@@ -948,7 +977,7 @@
             scratch(2, 2, ROWS, 128), scratch(2, 2, ROWS, 128),
             scratch(2, BAND, 128), scratch(2, 2, BAND, 128), scratch(2, BAND, 128), scratch(2, BAND, 128),
             scratch(2, BAND, 128), scratch(2, BAND, 128), scratch(2, BAND, 128), scratch(2, BAND, 128),
-            scratch(2, 128, 128), scratch(2, BAND, 128), scratch(2, 2, BAND, 128),
+            scratch(2, 128, 128), scratch(2, BAND, 128), scratch(2, BAND, 128), scratch(2, 2, BAND, 128),
             scratch(4, 2, BAND, 128), scratch(2, 2, 8, 128), scratch(2, 2, 8, 128), scratch(16, 128), scratch(16, 128),
             scratch(2, 2, 8, 128), scratch(2, 2, 8, 128), scratch(32, 128), scratch(32, 128),
             dma(15), dma(4), dma(8), dma(8), dma(8), dma(8), dma(8), dma(8),

time: 21.8 us -> 21.8 us (level); the launches traced: 21.7 us -> 21.4 us
  Pallas kernels: 21.1 us -> 20.7 us
    pallas_call x1, Pallas kernels: 18.9 us -> 18.6 us  [per_device(): pl.pallas_call(functools.partial(step_kernel, nb, nw), out_shape=(pltpu.V...]
where the time goes in v5:
time: 21.8 us; the launch traced here: 21.4 us
  Pallas kernels  20.7 us (95%)
  between operations  0.64 us (3%)
    pallas_call x1, Pallas kernels, per_device(): pl.pallas_call(functools.partial(step_kernel, nb, nw), out_shape=(pltpu.V...  18.6 us
    pallas_call x1, Pallas kernels, per_device(): pl.pallas_call(finish_kernel, out_shape=(big,) * 4 + (flat,) * 3, in_spec...  2.16 us

profile of v5, /device:TPU:7, one launch (start us, length us, event | category | flops | bytes accessed | tf_op | source)
XLA Modules:
  0.0 21.4 jit_solution(17487454131730508758)
XLA Ops:
  0.6 18.6 %step.1 = (f32[120,1920]{1,0:T(8,128)S(1)}, f32[120,1920]{1,0:T(8,128)S(1)}, f32[128,1920]{1,0:T(8,128)S(1)}, f32[128,1920]{1,0:T(8,128)S(1)}, f32[120,256]{1,0:...) custom-call(s32[2,4]{1,0:T(2,128)} %flags_in.1, ...), custom_call_target="tpu_custom_call" | custom-call | tf_op jit(solution)/shard_map/step/pallas_call | solution.py:952
  19.2 2.2 %finish.1 = (f32[120,1920]{1,0:T(8,128)}, f32[120,1920]{1,0:T(8,128)}, f32[120,1920]{1,0:T(8,128)}, f32[120,1920]{1,0:T(8,128)}, f32[120,240]{1,0:T(8,128)}, /*index=5*/f32[120,240]{1,0:T(8,128)}, f32[120,240]{1,0:T(8,128)}) custom-call(f32[120,1920]{1,0:T(8,128)S(1)} %get-tuple-element.16.tn, f32[120,1920]{1,0:T(8,128)S(1)} %get-tuple-element.17.sn, ...), custom_call_target="tpu_custom_call" | custom-call | tf_op jit(solution)/shard_map/finish/pallas_call | solution.py:993

commit v6 on v5

--- a/solution.py
+++ b/solution.py
@@ -268,7 +268,7 @@
     for copy in tables[1:4]:
         copy.start()
     for f in (2, 3, 0, 1):
-        loads[f].start()
+        loads[f].start(priority=1)
     for copy in tables[4:]:
         copy.start()
 

time: 21.8 us -> 21.8 us (level)
  no operation moved by 1% of the time
where the time goes in v6:
time: 21.8 us; the launch traced here: 21.4 us
  Pallas kernels  20.7 us (95%)
  between operations  0.64 us (3%)
    pallas_call x1, Pallas kernels, per_device(): pl.pallas_call(functools.partial(step_kernel, nb, nw), out_shape=(pltpu.V...  18.6 us
    pallas_call x1, Pallas kernels, per_device(): pl.pallas_call(finish_kernel, out_shape=(big,) * 4 + (flat,) * 3, in_spec...  2.16 us

profile of v6, /device:TPU:7, one launch (start us, length us, event | category | flops | bytes accessed | tf_op | source)
XLA Modules:
  0.0 21.4 jit_solution(13326801220281733401)
XLA Ops:
  0.6 18.6 %step.1 = (f32[120,1920]{1,0:T(8,128)S(1)}, f32[120,1920]{1,0:T(8,128)S(1)}, f32[128,1920]{1,0:T(8,128)S(1)}, f32[128,1920]{1,0:T(8,128)S(1)}, f32[120,256]{1,0:...) custom-call(s32[2,4]{1,0:T(2,128)} %flags_in.1, ...), custom_call_target="tpu_custom_call" | custom-call | tf_op jit(solution)/shard_map/step/pallas_call | solution.py:952
  19.2 2.2 %finish.1 = (f32[120,1920]{1,0:T(8,128)}, f32[120,1920]{1,0:T(8,128)}, f32[120,1920]{1,0:T(8,128)}, f32[120,1920]{1,0:T(8,128)}, f32[120,240]{1,0:T(8,128)}, /*index=5*/f32[120,240]{1,0:T(8,128)}, f32[120,240]{1,0:T(8,128)}) custom-call(f32[120,1920]{1,0:T(8,128)S(1)} %get-tuple-element.16.tn, f32[120,1920]{1,0:T(8,128)S(1)} %get-tuple-element.17.sn, ...), custom_call_target="tpu_custom_call" | custom-call | tf_op jit(solution)/shard_map/finish/pallas_call | solution.py:993
